TPU v7x, 32 devices: a whole 2x2x4 slice. The times are simulated.
32 devices in a mesh: seq: 8 (over y, x, core), head: 4 (over z).
Axes of the slice: x: 2, y: 2, z: 4, core: 2. Of those that a mesh axis runs over, the one named last changes fastest.
Arguments:
- fixed_point: bfloat16 [1024, 2048], P('seq'), may hold values from -7 to 7
- upstream: bfloat16 [1024, 2048], P('seq'), may hold values from -70 to 70
- norm_gain: float32 [2048], replicated, may hold values from 0.7 to 1.3
- query_weight: bfloat16 [2048, 1024], P(None, 'head'), may hold values from -0.35355339 to 0.35355339
- keyval_weight: bfloat16 [2048, 512], P(None, 'head'), may hold values from -0.143631065 to 0.143631065
- output_weight: bfloat16 [1024, 2048], P('head'), may hold values from -0.09375 to 0.09375
- log_norm: float32 [16, 1024], P('head', 'seq'), as said below
- attention_out: bfloat16 [1024, 1024], P('seq', 'head'), as said below
Outputs:
- adjoint: float32 [1024, 2048], P('seq')
Inputs may be any that keep to these rules, and one draw needn't show every extreme that they name: attention_out[t, h] is the sum over the keys that query t sees of exp(scores[h, t, j] - log_norm[h, t]) v_c(j), rounded to bfloat16.
All inputs are finite; a program needn't handle non-finite values.
Results may differ from a plain program's by a relative error of at most 0.012.
The roundings to bfloat16 on the way count: a program that leaves them out, or rounds other values in their place, can miss the bound.
Values may be sent and summed in bfloat16 or wider, within the bound.
No kernel may reach another device: no remote copies, remote signals or barrier semaphores. Data moves between devices by JAX's collectives and lax.ppermute only.
A program may use at most 64 MiB of HBM per device.

v0:
```python
import functools

import jax
import jax.numpy as jnp
from jax import lax
from jax.experimental import pallas as pl
from jax.experimental.pallas import tpu as pltpu
from jax.sharding import PartitionSpec as P

WIN_DEVS = 4
norm_eps = 1e-05
mix_eps = 1e-06
F32 = jnp.float32
BF16 = jnp.bfloat16
COLLECT = 50000
EXTRA = 16
NT = (((1,), (1,)), ((), ()))


def shape_of(shape, dtype):
    return jax.ShapeDtypeStruct(shape, dtype)


def local_call(body, outs, flops, moved, room, **more):
    return pl.pallas_call(
        body,
        out_shape=outs,
        compiler_params=pltpu.CompilerParams(vmem_limit_bytes=room * 1024 * 1024),
        cost_estimate=pl.CostEstimate(flops=flops, bytes_accessed=moved, transcendentals=0),
        **more,
    )


def shifted(value, axis, steps):
    count = lax.axis_size(axis)
    initial, last = (max(0, -steps), min(count, count - steps))
    return lax.ppermute(value, axis, [(source, source + steps) for source in range(initial, last)])


def rotated(value, axis):
    count = lax.axis_size(axis)
    parts = [value]
    for step in range(1, count):
        parts.append(lax.ppermute(value, axis, [(i, (i - step) % count) for i in range(count)]))
    return parts


def doubled(value, axis, group, gates):
    count = lax.axis_size(axis)
    near, bit = list(value), group // 2
    for gate in gates:
        near = list(lax.optimization_barrier((tuple(near), gate))[0])
        pairs = [(i, i ^ bit) for i in range(count)]
        if len(near) > 1:
            near = [jnp.concatenate(near)]
        if bit == 1:
            return near + [lax.ppermute(near[0], axis, pairs)]
        near.append(lax.ppermute(near[0], axis, pairs))
        bit //= 2


def assemble(place, wide, out_ref, refs):
    group = sum(ref.shape[0] for ref in refs)
    cut = wide // group
    rest_cut = refs[0].shape[2] - cut
    entries = [(ref, j) for ref in refs for j in range(ref.shape[0])]
    for j, (ref, at) in enumerate(entries):
        distance, bit, rest = 0, group // 2, j
        while rest:
            distance += bit * (rest & 1)
            rest >>= 1
            bit //= 2
        index = lax.bitwise_xor(place, jnp.int32(distance))
        first = pl.multiple_of(index * cut, cut)
        second = pl.multiple_of(wide + index * rest_cut, rest_cut)
        for k in range(out_ref.shape[0]):
            out_ref[k, pl.ds(first, cut), :] = ref[at, k, :cut, :]
            out_ref[k, pl.ds(second, rest_cut), :] = ref[at, k, cut:, :]


def prep_body(block_ref, qw_ref, kvw_ref, z_ref, gain_ref, cols_ref, hidden_ref, kv_ref, kvf_ref,
              inv_ref, q_tile, kv_tile, z_tile, gain_tile, sems):
    tile = q_tile.shape[1]
    wide, narrow = qw_ref.shape[1], kvw_ref.shape[1]
    group = (wide + narrow) // cols_ref.shape[0]
    place = lax.rem(block_ref[0], group)
    q_take, kv_take = wide // group, narrow // group
    q_at = place * q_take
    q_first = pl.multiple_of(q_at // tile * tile, tile)
    copies = [
        pltpu.make_async_copy(qw_ref.at[:, pl.ds(q_first, tile)], q_tile, sems.at[0]),
        pltpu.make_async_copy(kvw_ref, kv_tile, sems.at[1]),
        pltpu.make_async_copy(z_ref, z_tile, sems.at[2]),
        pltpu.make_async_copy(gain_ref, gain_tile, sems.at[3]),
    ]
    for copy in copies:
        copy.start()
    first = 0
    for copy, ref, at, take in (
        (copies[0], q_tile, q_at - q_first, q_take),
        (copies[1], kv_tile, place * kv_take, kv_take),
    ):
        copy.wait()
        total = ref.shape[1]
        row = lax.broadcasted_iota(jnp.int32, (take, total), 0) + at
        pick = (row == lax.broadcasted_iota(jnp.int32, (take, total), 1)).astype(BF16)
        cols = lax.dot_general(pick, ref[...], NT, preferred_element_type=F32)
        cols_ref[first : first + take, :] = cols.astype(BF16)
        first += take
    copies[2].wait()
    copies[3].wait()
    z = z_tile[...].astype(F32)
    inverse = lax.rsqrt(jnp.mean(z * z, axis=1, keepdims=True) + norm_eps)
    hidden = (z * inverse * gain_tile[...]).astype(BF16)
    hidden_ref[...] = hidden
    kvf = jnp.dot(hidden, kv_tile[...], preferred_element_type=F32)
    kvf_ref[...] = kvf
    kv_ref[...] = kvf.astype(BF16)
    inv_ref[...] = jnp.broadcast_to(inverse, inv_ref.shape)


def chain_body(cols_ref, scaled_ref, out_ref):
    share = lax.dot_general(cols_ref[...], scaled_ref[...], NT, preferred_element_type=F32)
    out_ref[...] = share.astype(BF16)


def lanes_of(value, heads):
    size = value.shape[0] // heads
    return jnp.concatenate([value[i * size : (i + 1) * size] for i in range(heads)], axis=1)


def start_body(heads, hidden_ref, inv_ref, qw_ref, ow_ref, up_ref, z_ref, ao_ref, gain_ref, ln_ref,
               qf_ref, qt_ref, go_ref, nt_ref, aot_ref, scaled_ref, norms_ref,
               qw_tile, ow_tile, up_tile, z_tile, ao_tile, gain_tile, sems):
    copies = [
        pltpu.make_async_copy(source, target, sems.at[i])
        for i, (source, target) in enumerate(
            ((ow_ref, ow_tile), (up_ref, up_tile), (z_ref, z_tile), (qw_ref, qw_tile),
             (ao_ref, ao_tile), (gain_ref, gain_tile), (ln_ref, norms_ref))
        )
    ]
    for copy in copies:
        copy.start()
    for copy in copies[:3]:
        copy.wait()
    out = lax.dot_general(up_tile[...], ow_tile[...], NT, preferred_element_type=F32)
    go_ref[...] = lanes_of(out.T, heads)
    base = lax.dot_general(z_tile[...], ow_tile[...], NT, preferred_element_type=F32)
    nt_ref[...] = lanes_of((base * inv_ref[:, :1]).T, heads)
    copies[3].wait()
    qf = jnp.dot(hidden_ref[...], qw_tile[...], preferred_element_type=F32)
    qf_ref[...] = qf
    qt_ref[...] = lanes_of(qf.T, heads).astype(BF16)
    for copy in copies[4:]:
        copy.wait()
    scaled_ref[...] = (ow_tile[...].astype(F32) * gain_tile[...]).astype(BF16)
    aot_ref[...] = lanes_of(ao_tile[...].astype(F32).T, heads)


def pull(heads, scale, go, aot, qt, kvw_ref, probs, score_ref, own_ref, term_refs):
    e = go.shape[0]
    rows = go.shape[1] // heads
    row_terms = jnp.sum(go * aot, axis=0, keepdims=True)
    gob = go.astype(BF16)
    grad_prob = jnp.dot(kvw_ref[:, e:], gob, preferred_element_type=F32)
    grad_score = (probs.astype(F32) * (grad_prob - row_terms)).astype(BF16)
    score_ref[...] = grad_score
    grad_key = lax.dot_general(grad_score, qt, NT, preferred_element_type=F32) * scale
    grad_value = lax.dot_general(probs, gob, NT, preferred_element_type=F32)
    terms = jnp.concatenate([grad_key, grad_value], axis=1)
    for offset in range(1, len(term_refs) + 1):
        first = (len(term_refs) - offset) * rows
        term_refs[offset - 1][...] = terms[first : first + rows].astype(BF16)
    own_ref[...] = terms[len(term_refs) * rows :]


def query_body(heads, scale, kt_ref, score_ref, gq_ref):
    rows = gq_ref.shape[0]
    grad_query = jnp.dot(kt_ref[...], score_ref[...], preferred_element_type=F32) * scale
    parts = [grad_query[:, i * rows : (i + 1) * rows] for i in range(heads)]
    gq_ref[...] = jnp.concatenate(parts, axis=0).T.astype(BF16)


def first_body(heads, scale, block_ref, *refs):
    windows = refs[: WIN_DEVS + 1]
    qt_ref, go_ref, aot_ref, ln_ref = refs[WIN_DEVS + 1 : WIN_DEVS + 5]
    kvw_ref, kt_ref, probs_ref, score_ref, own_ref = refs[WIN_DEVS + 5 : WIN_DEVS + 10]
    term_refs = refs[WIN_DEVS + 10 :]
    rows = windows[0].shape[0]
    for place, ref in enumerate(windows):
        kvw_ref[place * rows : (place + 1) * rows, :] = ref[...]
    kvw = kvw_ref[...]
    e = kvw.shape[1] // 2
    kt_ref[...] = kvw.astype(F32).T[:e].astype(BF16)
    scores = jnp.dot(kvw[:, :e], qt_ref[...], preferred_element_type=F32) * scale
    norms = jnp.concatenate([ln_ref[i : i + 1, :] for i in range(heads)], axis=1)
    key_pos = lax.broadcasted_iota(jnp.int32, scores.shape, 0)
    query_pos = lax.broadcasted_iota(jnp.int32, scores.shape, 1) & (rows - 1)
    allowed = (key_pos > query_pos) & (key_pos <= query_pos + WIN_DEVS * rows)
    allowed = allowed & (key_pos >= (WIN_DEVS - block_ref[0]) * rows)
    probs = jnp.where(allowed, jnp.exp(scores - norms), 0.0).astype(BF16)
    probs_ref[...] = probs
    pull(heads, scale, go_ref[...], aot_ref[...], qt_ref[...], kvw_ref, probs,
         score_ref, own_ref, term_refs)


def next_body(heads, parts, scale, fresh, spot_ref, *refs):
    gq_refs, refs = ([], refs) if fresh else (refs[:parts], refs[parts:])
    msg_refs, refs = refs[:parts], refs[parts:]
    inv_ref, nt_ref, qt_ref, aot_ref, kvw_ref, probs_ref, *refs = refs
    if fresh:
        *parts_refs, score_ref, own_ref, lhs_ref, row_ref, chain_ref = refs[:7]
        term_refs = refs[7:]
        assemble(spot_ref[1], chain_ref.shape[2], chain_ref, parts_refs)
    else:
        chain_ref, score_ref, own_ref, lhs_ref, row_ref = refs[:5]
        term_refs = refs[5:]
    rows, wide = lhs_ref.shape[1], chain_ref.shape[2]
    out = jnp.zeros((rows, wide), F32)
    along = jnp.zeros((EXTRA, rows), F32)
    for k in range(parts):
        index = lax.rem(spot_ref[0] + k, parts)
        msg = msg_refs[k][...]
        chain = chain_ref[k]
        lhs = msg[:rows]
        if gq_refs:
            lhs = jnp.concatenate([gq_refs[k][...], lhs], axis=1)
        out += jnp.dot(lhs, chain, preferred_element_type=F32)
        lhs_ref[index] = lhs
        along += msg[rows:, :rows].astype(F32)
    row_ref[...] = along
    along = jnp.sum(along, axis=0, keepdims=True)
    along = jnp.concatenate([along] * heads, axis=1)
    go = lanes_of((out * inv_ref[:, :1]).T, heads)
    inv_row = jnp.concatenate([inv_ref[...].T[:1, :]] * heads, axis=1)
    go = go - inv_row * along * nt_ref[...]
    pull(heads, scale, go, aot_ref[...], qt_ref[...], kvw_ref, probs_ref[...],
         score_ref, own_ref, term_refs)


def collect_body(width, own_ref, gq_ref, qf_ref, kvf_ref, *refs):
    msg_ref = refs[-1]
    rows = own_ref.shape[0]
    total = own_ref[...]
    for ref in refs[:-1]:
        total += ref[...].astype(F32)
    total = total.astype(BF16)
    ahead = msg_ref.shape[1] - total.shape[1]
    if ahead:
        msg_ref[:rows, :ahead] = gq_ref[...]
        msg_ref[rows:, :] = jnp.zeros((EXTRA, msg_ref.shape[1]), BF16)
    msg_ref[:rows, ahead:] = total
    prods = gq_ref[...].astype(F32) * qf_ref[...]
    partial = total.astype(F32) * kvf_ref[...]
    lanes = partial.shape[1]
    for first in range(0, prods.shape[1], lanes):
        partial += prods[:, first : first + lanes]
    along = jnp.sum(partial.T, axis=0, keepdims=True) * (1.0 / width)
    high = along.astype(BF16).astype(F32)
    place = lax.broadcasted_iota(jnp.int32, (EXTRA, rows), 0)
    extra = jnp.where(place == 0, high, jnp.where(place == 1, along - high, 0.0))
    msg_ref[rows:, :rows] = extra.astype(BF16)


def field_body(parts, wide, spot_ref, *refs):
    gq_refs, msg_refs, refs = refs[:parts], refs[parts : 2 * parts], refs[2 * parts :]
    lhs1_ref, row1_ref, lhs2_ref, row2_ref, *refs = refs
    *w_refs, z_ref, up_ref, gain_ref, inv_ref, v_ref, tot_ref, lhs3_ref, w_ref = refs
    rows, part = v_ref.shape[1:]
    head = spot_ref[0]
    row3 = jnp.zeros((EXTRA, rows), F32)
    for k in range(parts):
        msg = msg_refs[k][...]
        lhs3_ref[lax.rem(head + k, parts)] = jnp.concatenate(
            [gq_refs[k][...], msg[:rows]], axis=1
        )
        row3 += msg[rows:].astype(F32)
    assemble(spot_ref[1], wide, w_ref, w_refs)
    y = jnp.zeros((3 * rows, part), F32)
    for k in range(parts):
        lhs = jnp.concatenate([lhs1_ref[k], lhs2_ref[k], lhs3_ref[k]], axis=0)
        weight = w_ref[lax.rem(k - head + parts, parts)]
        y += jnp.dot(lhs, weight, preferred_element_type=F32)
    at = pl.ds(pl.multiple_of(head * part, part), part)
    inverse = inv_ref[:, :1]
    normed = z_ref[:, at].astype(F32) * inverse
    gain = gain_ref[:, at]
    fields = []
    for step, row in enumerate((row1_ref[...], row2_ref[...], row3)):
        along = jnp.broadcast_to(jnp.sum(row, axis=0, keepdims=True), (rows, rows)).T[:, :1]
        y_step = y[step * rows : (step + 1) * rows]
        fields.append(inverse * (y_step * gain - normed * along))
        v_ref[step] = fields[step]
    first, second, third = fields
    change1 = first - up_ref[:, at].astype(F32)
    change2 = second - first
    change3 = third - second
    pairs = [
        (change1, first), (change1, change1), (change2, first), (change2, change2),
        (change2, second), (change2, change3), (change3, second), (change3, change3),
    ]
    lanes = tot_ref.shape[2]
    sums = []
    for a, b in pairs:
        total = jnp.sum(a * b, axis=0, keepdims=True)
        sums.append(sum(total[:, i : i + lanes] for i in range(0, part, lanes)))
    totals = jnp.concatenate(sums, axis=0)
    for k in range(tot_ref.shape[0]):
        tot_ref[k] = totals


def mix_body(entries, spot_ref, tot_ref, up_ref, v_ref, out_ref):
    totals = jnp.sum(jnp.sum(tot_ref[...], axis=0), axis=1, keepdims=True) / entries
    s_r1, s_s, d2_v1, d2_d2, d2_v2, d2_d3, d3_v2, d3_d3 = [totals[i : i + 1] for i in range(8)]
    mix1 = s_r1 / (s_s + mix_eps)
    keep1 = 1.0 - mix1
    mix2 = keep1 * (d2_v1 + keep1 * d2_d2) / (keep1 * keep1 * d2_d2 + mix_eps)
    keep2 = keep1 * (1.0 - mix2)
    cross = mix1 * (d2_v2 + keep2 * d2_d3) + keep2 * (d3_v2 + keep2 * d3_d3)
    square = mix1 * mix1 * d2_d2 + 2.0 * mix1 * keep2 * d2_d3 + keep2 * keep2 * d3_d3
    mix3 = cross / (square + mix_eps)
    part = out_ref.shape[1]
    at = pl.ds(pl.multiple_of(spot_ref[0] * part, part), part)
    mixed = (
        up_ref[:, at].astype(F32)
        + v_ref[0]
        + (1.0 - mix3 * mix1) * v_ref[1]
        + keep2 * (1.0 - mix3) * v_ref[2]
    )
    out_ref[...] = mixed.astype(BF16)


def join_body(spot_ref, *refs):
    *part_refs, out_ref, tile, sems = refs
    parts = len(part_refs)
    part = part_refs[0].shape[1]
    copies = []
    for k in range(parts):
        tile[k] = part_refs[k][...].astype(F32)
        first = pl.multiple_of(lax.rem(spot_ref[0] + k, parts) * part, part)
        copies.append(
            pltpu.make_async_copy(tile.at[k], out_ref.at[:, pl.ds(first, part)], sems.at[k])
        )
        copies[k].start()
    for copy in copies:
        copy.wait()


def shards(
    fixed_point,
    upstream,
    norm_gain,
    query_weight,
    keyval_weight,
    output_weight,
    log_norm,
    attention_out,
):
    rows, width = fixed_point.shape
    wide = query_weight.shape[1]
    narrow = keyval_weight.shape[1]
    size = wide + narrow
    e = narrow // 2
    heads = log_norm.shape[0]
    seq_count = lax.axis_size("seq")
    parts = lax.axis_size("head")
    block = lax.axis_index("seq")
    head = lax.axis_index("head")
    scale = e ** (-0.5)
    gain = norm_gain.reshape(1, width)
    span = (WIN_DEVS + 1) * rows
    group = min(8, seq_count)

    cols = size // group
    spot = jnp.stack([head, lax.rem(block, group)])
    smem = pl.BlockSpec(memory_space=pltpu.SMEM)
    vmem = pl.BlockSpec(memory_space=pltpu.VMEM)
    hbm = pl.BlockSpec(memory_space=pltpu.HBM)

    def pinned(value):
        return pltpu.with_memory_space_constraint(value, pltpu.HBM)

    tile = 128 if wide % 128 == 0 and 128 % (wide // group) == 0 else wide
    own_cols, hidden, kv, kvf, inv = local_call(
        prep_body,
        [
            shape_of((cols, width), BF16),
            shape_of((rows, width), BF16),
            shape_of((rows, narrow), BF16),
            shape_of((rows, narrow), F32),
            shape_of((rows, rows), F32),
        ],
        2 * width * size * cols,
        2 * width * (tile + narrow + rows),
        10,
        in_specs=[smem] + [hbm] * 4,
        scratch_shapes=[
            pltpu.VMEM((width, tile), BF16),
            pltpu.VMEM((width, narrow), BF16),
            pltpu.VMEM((rows, width), BF16),
            pltpu.VMEM((1, width), F32),
            pltpu.SemaphoreType.DMA((4,)),
        ],
    )(
        block.reshape(1),
        pinned(query_weight),
        pinned(keyval_weight),
        pinned(fixed_point),
        pinned(gain),
    )
    every_cols = jnp.stack(rotated(own_cols, "head"))
    earlier = [shifted(kv, "seq", offset) for offset in range(WIN_DEVS, 0, -1)]

    qf, qt, go, nt, aot, scaled, norms = local_call(
        functools.partial(start_body, heads),
        [
            shape_of((rows, wide), F32),
            shape_of((e, heads * rows), BF16),
            shape_of((e, heads * rows), F32),
            shape_of((e, heads * rows), F32),
            shape_of((e, heads * rows), F32),
            shape_of((wide, width), BF16),
            shape_of((heads, rows), F32),
        ],
        6 * rows * width * wide,
        4 * width * (2 * rows + wide),
        14,
        in_specs=[vmem] * 2 + [hbm] * 7,
        scratch_shapes=[
            pltpu.VMEM((width, wide), BF16),
            pltpu.VMEM((wide, width), BF16),
            pltpu.VMEM((rows, width), BF16),
            pltpu.VMEM((rows, width), BF16),
            pltpu.VMEM((rows, wide), BF16),
            pltpu.VMEM((1, width), F32),
            pltpu.SemaphoreType.DMA((7,)),
        ],
    )(
        hidden,
        inv,
        pinned(query_weight),
        pinned(output_weight),
        pinned(upstream),
        pinned(fixed_point),
        pinned(attention_out),
        pinned(gain),
        pinned(log_norm),
    )

    pull_outs = [shape_of((span, heads * rows), BF16), shape_of((rows, narrow), F32)]
    pull_outs += [shape_of((rows, narrow), BF16)] * WIN_DEVS
    pull_flops = 6 * span * e * heads * rows

    def exchange(score, own, terms, split):
        arrived = [shifted(term, "seq", -offset - 1) for offset, term in enumerate(terms)]
        gq = local_call(
            functools.partial(query_body, heads, scale),
            shape_of((rows, wide), BF16),
            2 * span * e * heads * rows,
            span * heads * rows * 2,
            4,
        )(kt, score)
        ahead = rotated(gq, "head") if split else []
        if not split:
            arrived = list(lax.optimization_barrier((tuple(arrived), near[1]))[0])
        msg = local_call(
            functools.partial(collect_body, width),
            shape_of((rows + EXTRA, narrow if split else size), BF16),
            COLLECT * rows * size,
            rows * size * 4,
            4,
        )(own, gq, qf, kvf, *arrived)
        return rotated(msg, "head"), msg, ahead

    kvw, kt, probs, score, own, *terms = local_call(
        functools.partial(first_body, heads, scale),
        [
            shape_of((span, narrow), BF16),
            shape_of((e, span), BF16),
            shape_of((span, heads * rows), BF16),
        ]
        + pull_outs,
        pull_flops * 5 // 4,
        span * heads * rows * 2,
        16,
        in_specs=[smem] + [vmem] * (WIN_DEVS + 5),
    )(block.reshape(1), *earlier, kv, qt, go, aot, norms)
    packed, marks = [], []
    chain_shape = shape_of((parts, size, wide), BF16)
    for step in range(3):
        if step:
            score, own, lhs, row, *terms = local_call(
                functools.partial(next_body, heads, parts, scale, step == 1),
                pull_outs[:2]
                + [shape_of((parts, rows, size), BF16), shape_of((EXTRA, rows), F32)]
                + [chain_shape] * (step == 1)
                + pull_outs[2:],
                pull_flops + 2 * rows * parts * size * wide,
                span * heads * rows * 2 + parts * size * wide * 2,
                16,
                in_specs=[smem] + [vmem] * (len(ahead) + parts + 6 + len(chain)),
            )(spot, *ahead, *every_msg, inv, nt, qt, aot, kvw, probs, *chain)
            packed += [lhs, row]
            if step == 1:
                chain, *terms = terms
                chain = [chain]
        if step == 0:
            every_cols, _ = lax.optimization_barrier((every_cols, score))
            share = local_call(
                chain_body,
                shape_of((parts * cols, wide), BF16),
                2 * parts * cols * width * wide,
                2 * width * (wide + parts * cols),
                8,
            )(every_cols.reshape(parts * cols, width), scaled)
            share = share.reshape(parts, cols, wide)
            *terms, share = lax.optimization_barrier((*terms, share))
            pairs = [(i, i ^ (group // 2)) for i in range(seq_count)]
            near = [share[None], lax.ppermute(share[None], "seq", pairs)]
        every_msg, msg, ahead = exchange(score, own, terms, step > 0)
        if step == 0:
            chain = doubled(near, "seq", group // 2, (msg, every_msg[1:2]))
        marks.append(dict(msg=msg, sent=(ahead[1:], every_msg[1:])))

    part = width // parts
    mine = lax.dynamic_slice_in_dim(every_cols, head * part, part, 2)
    weight = doubled([mine[None]], "seq", group, (marks[0]["msg"], marks[0]["sent"], marks[1]["sent"]))
    small = seq_count * parts <= 64
    fields, totals = local_call(
        functools.partial(field_body, parts, wide),
        [
            shape_of((3, rows, part), F32),
            shape_of((seq_count * parts if small else 1, 8, 128), F32),
        ],
        6 * rows * parts * size * part,
        2 * parts * size * part,
        20,
        in_specs=[smem] + [vmem] * (2 * parts + 8 + len(weight)),
        scratch_shapes=[
            pltpu.VMEM((parts, rows, size), BF16),
            pltpu.VMEM((parts, size, part), BF16),
        ],
    )(spot, *ahead, *every_msg, *packed, *weight, fixed_point, upstream, gain, inv)
    if small:
        totals = lax.all_to_all(totals, ("seq", "head"), 0, 0)
    else:
        totals = lax.psum(totals, ("seq", "head"))
    mixed = local_call(
        functools.partial(mix_body, rows * seq_count * width),
        shape_of((rows, part), BF16),
        8 * rows * part,
        18 * rows * part,
        6,
        in_specs=[smem] + [vmem] * 3,
    )(spot, totals, upstream, fields)
    every_mixed = rotated(mixed, "head")
    return local_call(
        join_body,
        shape_of((rows, width), F32),
        0,
        6 * rows * width,
        6,
        in_specs=[smem] + [vmem] * parts,
        out_specs=hbm,
        scratch_shapes=[
            pltpu.VMEM((parts, rows, part), F32),
            pltpu.SemaphoreType.DMA((parts,)),
        ],
    )(spot, *every_mixed)


def solution(mesh):
    in_specs = (
        P("seq", None),
        P("seq", None),
        P(),
        P(None, "head"),
        P(None, "head"),
        P("head", None),
        P("head", "seq"),
        P("seq", "head"),
    )
    out_specs = P("seq", None)
    return jax.shard_map(shards, mesh=mesh, in_specs=in_specs, out_specs=out_specs, check_vma=False)
```

profile of v0, /device:TPU:9, one launch (start us, length us, event | category | flops | bytes accessed | tf_op | source)
XLA Modules:
  0.0 132.4 jit_solution(8075327087250370464)
XLA Ops:
  0.0 2.1 %shard_map.82 = (bf16[48,2048]{1,0:T(8,128)(2,1)S(1)}, bf16[128,2048]{1,0:T(8,128)(2,1)S(1)}, bf16[128,128]{1,0:T(8,128)(2,1)S(1)}, f32[128,128]{1,0:T(8,128)S(1)}, f32[128,128]{1,0:T(8,128)S(1)}) custom-call(s32[1]{0:T(128)} %bitcast.2.block_ref, bf16[2048,256]{1,0:T(8,128)(2,1)} %qw_ref.3, bf16[2048,128]{1,0:T(8,128)(2,1)} %kvw_ref.1, ...), custom_call_target="tpu_custom_call" | custom-call | flops 75497472 | bytes 1572864 | tf_op jit(solution)/shard_map/pallas_call | solution.py:384
  2.1 1.3 %collective-permute-start.6 = (bf16[48,2048]{1,0:T(8,128)(2,1)S(1)}, bf16[48,2048]{1,0:T(8,128)(2,1)S(1)}, u32[]{:S(2)}, u32[]{:S(2)}) collective-permute-start(bf16[48,2048]{1,0:T(8,128)(2,1)S(1)} %get-tuple-element.80), channel_id=1, source_target_pairs={{0,1},{1,2},{2,3},{3,0},{4,5},{5,6},{6,7},{7,4},{8,9},{9,10},{10,1... | collective-permute-start | bytes 589832 | tf_op jit(solution)/shard_map/ppermute | solution.py:44
  3.4 1.1 collective-permute-start.5
  4.5 1.4 %collective-permute-start.4 = (bf16[48,2048]{1,0:T(8,128)(2,1)S(1)}, bf16[48,2048]{1,0:T(8,128)(2,1)S(1)}, u32[]{:S(2)}, u32[]{:S(2)}) collective-permute-start(bf16[48,2048]{1,0:T(8,128)(2,1)S(1)} %get-tuple-element.80), channel_id=1, source_target_pairs={{0,3},{1,0},{2,1},{3,2},{4,7},{5,4},{6,5},{7,6},{8,11},{9,8},{10,9... | collective-permute-start | bytes 589832 | tf_op jit(solution)/shard_map/ppermute | solution.py:44
  5.9 4.5 %collective-permute-start.3 = (bf16[128,128]{1,0:T(8,128)(2,1)S(1)}, bf16[128,128]{1,0:T(8,128)(2,1)S(1)}, u32[]{:S(2)}, u32[]{:S(2)}) collective-permute-start(bf16[128,128]{1,0:T(8,128)(2,1)S(1)} %get-tuple-element.64.refs_4_), channel_id=1, source_target_pairs={{0,4},{4,8},{8,12},{12,16},{16,20},{20,24},{24,28},{1,5},{5,9},{9,... | collective-permute-start | bytes 98312 | tf_op jit(solution)/shard_map/ppermute | solution.py:37
  10.4 3.1 %collective-permute-start.2 = (bf16[128,128]{1,0:T(8,128)(2,1)S(1)}, bf16[128,128]{1,0:T(8,128)(2,1)S(1)}, u32[]{:S(2)}, u32[]{:S(2)}) collective-permute-start(bf16[128,128]{1,0:T(8,128)(2,1)S(1)} %get-tuple-element.64.refs_4_), channel_id=1, source_target_pairs={{0,8},{4,12},{8,16},{12,20},{16,24},{20,28},{1,9},{5,13},{9,17},{1... | collective-permute-start | bytes 98312 | tf_op jit(solution)/shard_map/ppermute | solution.py:37
  13.6 3.0 %collective-permute-start.1 = (bf16[128,128]{1,0:T(8,128)(2,1)S(1)}, bf16[128,128]{1,0:T(8,128)(2,1)S(1)}, u32[]{:S(2)}, u32[]{:S(2)}) collective-permute-start(bf16[128,128]{1,0:T(8,128)(2,1)S(1)} %get-tuple-element.64.refs_4_), channel_id=1, source_target_pairs={{0,12},{4,16},{8,20},{12,24},{16,28},{1,13},{5,17},{9,21},{13,25},... | collective-permute-start | bytes 98312 | tf_op jit(solution)/shard_map/ppermute | solution.py:37
  16.6 2.5 %collective-permute-start = (bf16[128,128]{1,0:T(8,128)(2,1)S(1)}, bf16[128,128]{1,0:T(8,128)(2,1)S(1)}, u32[]{:S(2)}, u32[]{:S(2)}) collective-permute-start(bf16[128,128]{1,0:T(8,128)(2,1)S(1)} %get-tuple-element.64.refs_4_), channel_id=1, source_target_pairs={{0,16},{4,20},{8,24},{12,28},{1,17},{5,21},{9,25},{13,29},{2,18},{... | collective-permute-start | bytes 98312 | tf_op jit(solution)/shard_map/ppermute | solution.py:37
  19.1 3.6 %shard_map.83 = (f32[128,256]{1,0:T(8,128)S(1)}, bf16[64,512]{1,0:T(8,128)(2,1)S(1)}, f32[64,512]{1,0:T(8,128)S(1)}, f32[64,512]{1,0:T(8,128)S(1)}, f32[64,512]{...) custom-call(bf16[128,2048]{1,0:T(8,128)(2,1)S(1)} %get-tuple-element.65.hidden_ref, ...), custom_call_target="tpu_custom_call" | custom-call | flops 402653184 | bytes 4194304 | tf_op jit(solution)/shard_map/pallas_call | solution.py:414
  22.7 1.1 shard_map.84
  24.6 2.5 %collective-permute-start.7 = (bf16[128,128]{1,0:T(8,128)(2,1)S(1)}, bf16[128,128]{1,0:T(8,128)(2,1)S(1)}, u32[]{:S(2)}, u32[]{:S(2)}) collective-permute-start(bf16[128,128]{1,0:T(8,128)(2,1)S(1)} %get-tuple-element.83), channel_id=1, source_target_pairs={{4,0},{8,4},{12,8},{16,12},{20,16},{24,20},{28,24},{5,1},{9,5},{13... | collective-permute-start | bytes 98312 | tf_op jit(solution)/shard_map/ppermute | solution.py:37
  27.1 1.3 collective-permute-start.8
  28.4 1.3 collective-permute-start.9
  29.7 1.3 collective-permute-start.10
  32.4 2.8 %collective-permute-done.9.refs_2_ = bf16[128,128]{1,0:T(8,128)(2,1)S(1)} collective-permute-done((bf16[128,128]{1,0:T(8,128)(2,1)S(1)}, bf16[128,128]{1,0:T(8,128)(2,1)S(1)}, u32[]{:S(2)}, u32[]{:S(2)}) %collective-permute-start.9) | collective-permute-done | bytes 32800 | tf_op jit(solution)/shard_map/ppermute | solution.py:37
  36.1 1.8 %collective-permute-start.15 = (bf16[2,4,48,256]{3,2,1,0:T(8,128)(2,1)S(1)}, bf16[2,4,48,256]{3,2,1,0:T(8,128)(2,1)S(1)}, u32[]{:S(2)}, u32[]{:S(2)}) collective-permute-start(bf16[2,4,48,256]{3,2,1,0:T(8,128)(2,1)S(1)} %constant_dynamic-update-slice_fusion), channel_id=1, source_target_pairs={{0,8},{4,12},{8,0},{12,4},{16,24},{20,28},{24,16},{28,20},{1,9},{5... | collective-permute-start | bytes 589832 | tf_op jit(solution)/shard_map/ppermute | solution.py:58
  37.9 1.3 %collective-permute-start.12 = (bf16[144,384]{1,0:T(8,128)(2,1)S(1)}, bf16[144,384]{1,0:T(8,128)(2,1)S(1)}, u32[]{:S(2)}, u32[]{:S(2)}) collective-permute-start(bf16[144,384]{1,0:T(8,128)(2,1)S(1)} %shard_map.87.refs_0_), channel_id=1, source_target_pairs={{0,3},{1,0},{2,1},{3,2},{4,7},{5,4},{6,5},{7,6},{8,11},{9,8},{10,9... | collective-permute-start | bytes 331784 | tf_op jit(solution)/shard_map/ppermute | solution.py:44
  39.4 3.0 %collective-permute-start.13 = (bf16[144,384]{1,0:T(8,128)(2,1)S(1)}, bf16[144,384]{1,0:T(8,128)(2,1)S(1)}, u32[]{:S(2)}, u32[]{:S(2)}) collective-permute-start(bf16[144,384]{1,0:T(8,128)(2,1)S(1)} %shard_map.87.refs_0_), channel_id=1, source_target_pairs={{0,2},{1,3},{2,0},{3,1},{4,6},{5,7},{6,4},{7,5},{8,10},{9,11},{10,... | collective-permute-start | bytes 331784 | tf_op jit(solution)/shard_map/ppermute | solution.py:44
  42.5 1.4 %collective-permute-start.16 = (bf16[4,4,48,256]{3,2,1,0:T(8,128)(2,1)S(1)}, bf16[4,4,48,256]{3,2,1,0:T(8,128)(2,1)S(1)}, u32[]{:S(2)}, u32[]{:S(2)}) collective-permute-start(bf16[4,4,48,256]{3,2,1,0:T(8,128)(2,1)S(1)} %constant_dynamic-update-slice_fusion.2.refs_10_), channel_id=1, source_target_pairs={{0,4},{4,0},{8,12},{12,8},{16,20},{20,16},{24,28},{28,24},{1,5},{5... | collective-permute-start | bytes 1179656 | tf_op jit(solution)/shard_map/ppermute | solution.py:57
  43.8 1.6 %collective-permute-done.14.refs_3_ = bf16[144,384]{1,0:T(8,128)(2,1)S(1)} collective-permute-done((bf16[144,384]{1,0:T(8,128)(2,1)S(1)}, bf16[144,384]{1,0:T(8,128)(2,1)S(1)}, u32[]{:S(2)}, u32[]{:S(2)}) %collective-permute-start.14) | collective-permute-done | bytes 110624 | tf_op jit(solution)/shard_map/ppermute | solution.py:44
  45.4 3.3 %collective-permute-done.13.refs_2_ = bf16[144,384]{1,0:T(8,128)(2,1)S(1)} collective-permute-done((bf16[144,384]{1,0:T(8,128)(2,1)S(1)}, bf16[144,384]{1,0:T(8,128)(2,1)S(1)}, u32[]{:S(2)}, u32[]{:S(2)}) %collective-permute-start.13) | collective-permute-done | bytes 110624 | tf_op jit(solution)/shard_map/ppermute | solution.py:44
  48.9 1.9 %shard_map.88 = (bf16[640,512]{1,0:T(8,128)(2,1)S(1)}, f32[128,128]{1,0:T(8,128)S(1)}, bf16[4,128,384]{2,1,0:T(8,128)(2,1)S(1)}, f32[16,128]{1,0:T(8,128)S(1)}, ...) custom-call(s32[2]{0:T(128)S(1)} %pad_add_fusion.spot_ref, ...), custom_call_target="tpu_custom_call" | custom-call | flops 226492416 | bytes 1441792 | tf_op jit(solution)/shard_map/pallas_call | solution.py:492
  50.9 3.6 %collective-permute-start.20 = (bf16[128,128]{1,0:T(8,128)(2,1)S(1)}, bf16[128,128]{1,0:T(8,128)(2,1)S(1)}, u32[]{:S(2)}, u32[]{:S(2)}) collective-permute-start(bf16[128,128]{1,0:T(8,128)(2,1)S(1)} %get-tuple-element.101), channel_id=1, source_target_pairs={{4,0},{8,4},{12,8},{16,12},{20,16},{24,20},{28,24},{5,1},{9,5},{13... | collective-permute-start | bytes 98312 | tf_op jit(solution)/shard_map/ppermute | solution.py:37
  54.5 1.3 collective-permute-start.21
  55.8 1.3 collective-permute-start.22
  57.1 1.3 collective-permute-start.23
  58.7 1.6 %collective-permute-done.20.refs_0_ = bf16[128,128]{1,0:T(8,128)(2,1)S(1)} collective-permute-done((bf16[128,128]{1,0:T(8,128)(2,1)S(1)}, bf16[128,128]{1,0:T(8,128)(2,1)S(1)}, u32[]{:S(2)}, u32[]{:S(2)}) %collective-permute-start.20) | collective-permute-done | bytes 32800 | tf_op jit(solution)/shard_map/ppermute | solution.py:37
  60.6 4.0 %collective-permute-start.18 = (bf16[128,256]{1,0:T(8,128)(2,1)S(1)}, bf16[128,256]{1,0:T(8,128)(2,1)S(1)}, u32[]{:S(2)}, u32[]{:S(2)}) collective-permute-start(bf16[128,256]{1,0:T(8,128)(2,1)S(1)} %shard_map.89.gq_ref.refs_0_), channel_id=1, source_target_pairs={{0,2},{1,3},{2,0},{3,1},{4,6},{5,7},{6,4},{7,5},{8,10},{9,11},{10,... | collective-permute-start | bytes 196616 | tf_op jit(solution)/shard_map/ppermute | solution.py:44
  65.1 1.2 collective-permute-start.26
  66.3 2.7 %collective-permute-start.25 = (bf16[144,128]{1,0:T(8,128)(2,1)S(1)}, bf16[144,128]{1,0:T(8,128)(2,1)S(1)}, u32[]{:S(2)}, u32[]{:S(2)}) collective-permute-start(bf16[144,128]{1,0:T(8,128)(2,1)S(1)} %shard_map.90.refs_4_), channel_id=1, source_target_pairs={{0,2},{1,3},{2,0},{3,1},{4,6},{5,7},{6,4},{7,5},{8,10},{9,11},{10,... | collective-permute-start | bytes 110600 | tf_op jit(solution)/shard_map/ppermute | solution.py:44
  70.0 1.4 %collective-permute-done.25.refs_6_ = bf16[144,128]{1,0:T(8,128)(2,1)S(1)} collective-permute-done((bf16[144,128]{1,0:T(8,128)(2,1)S(1)}, bf16[144,128]{1,0:T(8,128)(2,1)S(1)}, u32[]{:S(2)}, u32[]{:S(2)}) %collective-permute-start.25) | collective-permute-done | bytes 36896 | tf_op jit(solution)/shard_map/ppermute | solution.py:44
  72.5 1.2 collective-permute-start.39
  73.7 1.9 %shard_map.91 = (bf16[640,512]{1,0:T(8,128)(2,1)S(1)}, f32[128,128]{1,0:T(8,128)S(1)}, bf16[4,128,384]{2,1,0:T(8,128)(2,1)S(1)}, f32[16,128]{1,0:T(8,128)S(1)}, ...) custom-call(s32[2]{0:T(128)S(1)} %pad_add_fusion.spot_ref, ...), custom_call_target="tpu_custom_call" | custom-call | flops 226492416 | bytes 1441792 | tf_op jit(solution)/shard_map/pallas_call | solution.py:492
  75.6 1.9 %collective-permute-start.30 = (bf16[128,128]{1,0:T(8,128)(2,1)S(1)}, bf16[128,128]{1,0:T(8,128)(2,1)S(1)}, u32[]{:S(2)}, u32[]{:S(2)}) collective-permute-start(bf16[128,128]{1,0:T(8,128)(2,1)S(1)} %get-tuple-element.108), channel_id=1, source_target_pairs={{4,0},{8,4},{12,8},{16,12},{20,16},{24,20},{28,24},{5,1},{9,5},{13... | collective-permute-start | bytes 98312 | tf_op jit(solution)/shard_map/ppermute | solution.py:37
  77.6 1.3 collective-permute-start.31
  78.9 1.3 collective-permute-start.32
  80.2 1.3 collective-permute-start.33
  82.4 2.4 %collective-permute-start.28 = (bf16[128,256]{1,0:T(8,128)(2,1)S(1)}, bf16[128,256]{1,0:T(8,128)(2,1)S(1)}, u32[]{:S(2)}, u32[]{:S(2)}) collective-permute-start(bf16[128,256]{1,0:T(8,128)(2,1)S(1)} %shard_map.92.gq_ref.refs_0_), channel_id=1, source_target_pairs={{0,2},{1,3},{2,0},{3,1},{4,6},{5,7},{6,4},{7,5},{8,10},{9,11},{10,... | collective-permute-start | bytes 196616 | tf_op jit(solution)/shard_map/ppermute | solution.py:44
  84.7 1.4 %collective-permute-done.32.refs_2_ = bf16[128,128]{1,0:T(8,128)(2,1)S(1)} collective-permute-done((bf16[128,128]{1,0:T(8,128)(2,1)S(1)}, bf16[128,128]{1,0:T(8,128)(2,1)S(1)}, u32[]{:S(2)}, u32[]{:S(2)}) %collective-permute-start.32) | collective-permute-done | bytes 32800 | tf_op jit(solution)/shard_map/ppermute | solution.py:37
  87.8 3.9 %collective-permute-start.35 = (bf16[144,128]{1,0:T(8,128)(2,1)S(1)}, bf16[144,128]{1,0:T(8,128)(2,1)S(1)}, u32[]{:S(2)}, u32[]{:S(2)}) collective-permute-start(bf16[144,128]{1,0:T(8,128)(2,1)S(1)} %shard_map.93.refs_4_), channel_id=1, source_target_pairs={{0,2},{1,3},{2,0},{3,1},{4,6},{5,7},{6,4},{7,5},{8,10},{9,11},{10,... | collective-permute-start | bytes 110600 | tf_op jit(solution)/shard_map/ppermute | solution.py:44
  92.0 2.5 %collective-permute-done.35.refs_6_ = bf16[144,128]{1,0:T(8,128)(2,1)S(1)} collective-permute-done((bf16[144,128]{1,0:T(8,128)(2,1)S(1)}, bf16[144,128]{1,0:T(8,128)(2,1)S(1)}, u32[]{:S(2)}, u32[]{:S(2)}) %collective-permute-start.35) | collective-permute-done | bytes 36896 | tf_op jit(solution)/shard_map/ppermute | solution.py:44
  95.4 1.9 %shard_map.94 = (f32[3,128,512]{2,1,0:T(8,128)S(1)}, f32[32,8,128]{2,1,0:T(8,128)S(1)}) custom-call(s32[2]{0:T(128)S(1)} %pad_add_fusion.spot_ref, bf16[128,256]{1,0:T(8,128)(2,1)S(1)} %shard_map.92.gq_ref.refs_0_, bf16[128,256]{1,0:T(8,128)(2,1)S(1)} %collective-permute-done.27.refs_1_, bf16[128,256]{1,0:T(8,128)(2,1)S(1)} %collective-permute-done.28.refs_2_, ...), custom_call_target="tpu_custom_call" | custom-call | flops 603979776 | bytes 1572864 | tf_op jit(solution)/shard_map/pallas_call | solution.py:529
  97.3 17.8 %all_to_all.5.tot_ref = f32[32,8,128]{2,1,0:T(8,128)S(1)} all-to-all(f32[32,8,128]{2,1,0:T(8,128)S(1)} %get-tuple-element.121), channel_id=1, replica_groups=mesh['seq'=8,'head'=4] {'seq','head'}, dimensions={0} | all-to-all | bytes 262144 | tf_op jit(solution)/shard_map/all_to_all | solution.py:545
  116.3 2.2 %collective-permute-start.41 = (bf16[128,512]{1,0:T(8,128)(2,1)S(1)}, bf16[128,512]{1,0:T(8,128)(2,1)S(1)}, u32[]{:S(2)}, u32[]{:S(2)}) collective-permute-start(bf16[128,512]{1,0:T(8,128)(2,1)S(1)} %shard_map.95.refs_0_), channel_id=1, source_target_pairs={{0,2},{1,3},{2,0},{3,1},{4,6},{5,7},{6,4},{7,5},{8,10},{9,11},{10,... | collective-permute-start | bytes 393224 | tf_op jit(solution)/shard_map/ppermute | solution.py:44
  118.6 2.2 %collective-permute-done.42.refs_3_ = bf16[128,512]{1,0:T(8,128)(2,1)S(1)} collective-permute-done((bf16[128,512]{1,0:T(8,128)(2,1)S(1)}, bf16[128,512]{1,0:T(8,128)(2,1)S(1)}, u32[]{:S(2)}, u32[]{:S(2)}) %collective-permute-start.42) | collective-permute-done | bytes 131104 | tf_op jit(solution)/shard_map/ppermute | solution.py:44
  120.8 6.4 %collective-permute-done.41.refs_2_ = bf16[128,512]{1,0:T(8,128)(2,1)S(1)} collective-permute-done((bf16[128,512]{1,0:T(8,128)(2,1)S(1)}, bf16[128,512]{1,0:T(8,128)(2,1)S(1)}, u32[]{:S(2)}, u32[]{:S(2)}) %collective-permute-start.41) | collective-permute-done | bytes 131104 | tf_op jit(solution)/shard_map/ppermute | solution.py:44
  127.2 3.7 %collective-permute-done.40.refs_1_ = bf16[128,512]{1,0:T(8,128)(2,1)S(1)} collective-permute-done((bf16[128,512]{1,0:T(8,128)(2,1)S(1)}, bf16[128,512]{1,0:T(8,128)(2,1)S(1)}, u32[]{:S(2)}, u32[]{:S(2)}) %collective-permute-start.40) | collective-permute-done | bytes 131104 | tf_op jit(solution)/shard_map/ppermute | solution.py:44
  130.9 1.6 %shard_map.96 = f32[128,2048]{1,0:T(8,128)} custom-call(s32[2]{0:T(128)S(1)} %pad_add_fusion.spot_ref, bf16[128,512]{1,0:T(8,128)(2,1)S(1)} %shard_map.95.refs_0_, bf16[128,512]{1,0:T(8,128)(2,1)S(1)} %collective-permute-done.40.refs_1_, bf16[128,512]{1,0:T(8,128)(2,1)S(1)} %collective-permute-done.41.refs_2_, ...), custom_call_target="tpu_custom_call" | custom-call | bytes 1572864 | tf_op jit(solution)/shard_map/pallas_call | solution.py:557
  (71 shorter events, 11.6 us)
Async XLA Ops:
  2.1 21.8 %collective-permute-start.6 = (bf16[48,2048]{1,0:T(8,128)(2,1)S(1)}, bf16[48,2048]{1,0:T(8,128)(2,1)S(1)}, u32[]{:S(2)}, u32[]{:S(2)}) collective-permute-start(bf16[48,2048]{1,0:T(8,128)(2,1)S(1)} %get-tuple-element.80), channel_id=1, source_target_pairs={{0,1},{1,2},{2,3},{3,0},{4,5},{5,6},{6,7},{7,4},{8,9},{9,10},{10,1... | collective-permute-start | bytes 589832 | tf_op jit(solution)/shard_map/ppermute | solution.py:44
  3.4 20.5 %collective-permute-start.5 = (bf16[48,2048]{1,0:T(8,128)(2,1)S(1)}, bf16[48,2048]{1,0:T(8,128)(2,1)S(1)}, u32[]{:S(2)}, u32[]{:S(2)}) collective-permute-start(bf16[48,2048]{1,0:T(8,128)(2,1)S(1)} %get-tuple-element.80), channel_id=1, source_target_pairs={{0,2},{1,3},{2,0},{3,1},{4,6},{5,7},{6,4},{7,5},{8,10},{9,11},{10,... | collective-permute-start | bytes 589832 | tf_op jit(solution)/shard_map/ppermute | solution.py:44
  4.5 19.4 %collective-permute-start.4 = (bf16[48,2048]{1,0:T(8,128)(2,1)S(1)}, bf16[48,2048]{1,0:T(8,128)(2,1)S(1)}, u32[]{:S(2)}, u32[]{:S(2)}) collective-permute-start(bf16[48,2048]{1,0:T(8,128)(2,1)S(1)} %get-tuple-element.80), channel_id=1, source_target_pairs={{0,3},{1,0},{2,1},{3,2},{4,7},{5,4},{6,5},{7,6},{8,11},{9,8},{10,9... | collective-permute-start | bytes 589832 | tf_op jit(solution)/shard_map/ppermute | solution.py:44
  5.9 7.6 %collective-permute-start.3 = (bf16[128,128]{1,0:T(8,128)(2,1)S(1)}, bf16[128,128]{1,0:T(8,128)(2,1)S(1)}, u32[]{:S(2)}, u32[]{:S(2)}) collective-permute-start(bf16[128,128]{1,0:T(8,128)(2,1)S(1)} %get-tuple-element.64.refs_4_), channel_id=1, source_target_pairs={{0,4},{4,8},{8,12},{12,16},{16,20},{20,24},{24,28},{1,5},{5,9},{9,... | collective-permute-start | bytes 98312 | tf_op jit(solution)/shard_map/ppermute | solution.py:37
  10.4 6.2 %collective-permute-start.2 = (bf16[128,128]{1,0:T(8,128)(2,1)S(1)}, bf16[128,128]{1,0:T(8,128)(2,1)S(1)}, u32[]{:S(2)}, u32[]{:S(2)}) collective-permute-start(bf16[128,128]{1,0:T(8,128)(2,1)S(1)} %get-tuple-element.64.refs_4_), channel_id=1, source_target_pairs={{0,8},{4,12},{8,16},{12,20},{16,24},{20,28},{1,9},{5,13},{9,17},{1... | collective-permute-start | bytes 98312 | tf_op jit(solution)/shard_map/ppermute | solution.py:37
  13.6 9.2 %collective-permute-start.1 = (bf16[128,128]{1,0:T(8,128)(2,1)S(1)}, bf16[128,128]{1,0:T(8,128)(2,1)S(1)}, u32[]{:S(2)}, u32[]{:S(2)}) collective-permute-start(bf16[128,128]{1,0:T(8,128)(2,1)S(1)} %get-tuple-element.64.refs_4_), channel_id=1, source_target_pairs={{0,12},{4,16},{8,20},{12,24},{16,28},{1,13},{5,17},{9,21},{13,25},... | collective-permute-start | bytes 98312 | tf_op jit(solution)/shard_map/ppermute | solution.py:37
  16.6 6.2 %collective-permute-start = (bf16[128,128]{1,0:T(8,128)(2,1)S(1)}, bf16[128,128]{1,0:T(8,128)(2,1)S(1)}, u32[]{:S(2)}, u32[]{:S(2)}) collective-permute-start(bf16[128,128]{1,0:T(8,128)(2,1)S(1)} %get-tuple-element.64.refs_4_), channel_id=1, source_target_pairs={{0,16},{4,20},{8,24},{12,28},{1,17},{5,21},{9,25},{13,29},{2,18},{... | collective-permute-start | bytes 98312 | tf_op jit(solution)/shard_map/ppermute | solution.py:37
  24.5 11.3 %collective-permute-start.11 = (bf16[1,4,48,256]{3,2,1,0:T(8,128)(2,1)S(1)}, bf16[1,4,48,256]{3,2,1,0:T(8,128)(2,1)S(1)}, u32[]{:S(2)}, u32[]{:S(2)}) collective-permute-start(bf16[1,4,48,256]{3,2,1,0:T(8,128)(2,1)S(1)} %bitcast.14), channel_id=1, source_target_pairs={{0,16},{4,20},{8,24},{12,28},{16,0},{20,4},{24,8},{28,12},{1,17},{... | collective-permute-start | bytes 294920 | tf_op jit(solution)/shard_map/ppermute | solution.py:519
  24.6 6.7 %collective-permute-start.7 = (bf16[128,128]{1,0:T(8,128)(2,1)S(1)}, bf16[128,128]{1,0:T(8,128)(2,1)S(1)}, u32[]{:S(2)}, u32[]{:S(2)}) collective-permute-start(bf16[128,128]{1,0:T(8,128)(2,1)S(1)} %get-tuple-element.83), channel_id=1, source_target_pairs={{4,0},{8,4},{12,8},{16,12},{20,16},{24,20},{28,24},{5,1},{9,5},{13... | collective-permute-start | bytes 98312 | tf_op jit(solution)/shard_map/ppermute | solution.py:37
  27.1 5.3 %collective-permute-start.8 = (bf16[128,128]{1,0:T(8,128)(2,1)S(1)}, bf16[128,128]{1,0:T(8,128)(2,1)S(1)}, u32[]{:S(2)}, u32[]{:S(2)}) collective-permute-start(bf16[128,128]{1,0:T(8,128)(2,1)S(1)} %get-tuple-element.84), channel_id=1, source_target_pairs={{8,0},{12,4},{16,8},{20,12},{24,16},{28,20},{9,1},{13,5},{17,9},{2... | collective-permute-start | bytes 98312 | tf_op jit(solution)/shard_map/ppermute | solution.py:37
  28.4 6.8 %collective-permute-start.9 = (bf16[128,128]{1,0:T(8,128)(2,1)S(1)}, bf16[128,128]{1,0:T(8,128)(2,1)S(1)}, u32[]{:S(2)}, u32[]{:S(2)}) collective-permute-start(bf16[128,128]{1,0:T(8,128)(2,1)S(1)} %get-tuple-element.85), channel_id=1, source_target_pairs={{12,0},{16,4},{20,8},{24,12},{28,16},{13,1},{17,5},{21,9},{25,13},... | collective-permute-start | bytes 98312 | tf_op jit(solution)/shard_map/ppermute | solution.py:37
  29.7 6.2 %collective-permute-start.10 = (bf16[128,128]{1,0:T(8,128)(2,1)S(1)}, bf16[128,128]{1,0:T(8,128)(2,1)S(1)}, u32[]{:S(2)}, u32[]{:S(2)}) collective-permute-start(bf16[128,128]{1,0:T(8,128)(2,1)S(1)} %get-tuple-element.86), channel_id=1, source_target_pairs={{16,0},{20,4},{24,8},{28,12},{17,1},{21,5},{25,9},{29,13},{18,2},{... | collective-permute-start | bytes 98312 | tf_op jit(solution)/shard_map/ppermute | solution.py:37
  36.1 6.4 %collective-permute-start.15 = (bf16[2,4,48,256]{3,2,1,0:T(8,128)(2,1)S(1)}, bf16[2,4,48,256]{3,2,1,0:T(8,128)(2,1)S(1)}, u32[]{:S(2)}, u32[]{:S(2)}) collective-permute-start(bf16[2,4,48,256]{3,2,1,0:T(8,128)(2,1)S(1)} %constant_dynamic-update-slice_fusion), channel_id=1, source_target_pairs={{0,8},{4,12},{8,0},{12,4},{16,24},{20,28},{24,16},{28,20},{1,9},{5... | collective-permute-start | bytes 589832 | tf_op jit(solution)/shard_map/ppermute | solution.py:58
  37.9 4.5 %collective-permute-start.12 = (bf16[144,384]{1,0:T(8,128)(2,1)S(1)}, bf16[144,384]{1,0:T(8,128)(2,1)S(1)}, u32[]{:S(2)}, u32[]{:S(2)}) collective-permute-start(bf16[144,384]{1,0:T(8,128)(2,1)S(1)} %shard_map.87.refs_0_), channel_id=1, source_target_pairs={{0,3},{1,0},{2,1},{3,2},{4,7},{5,4},{6,5},{7,6},{8,11},{9,8},{10,9... | collective-permute-start | bytes 331784 | tf_op jit(solution)/shard_map/ppermute | solution.py:44
  39.2 6.2 %collective-permute-start.14 = (bf16[144,384]{1,0:T(8,128)(2,1)S(1)}, bf16[144,384]{1,0:T(8,128)(2,1)S(1)}, u32[]{:S(2)}, u32[]{:S(2)}) collective-permute-start(bf16[144,384]{1,0:T(8,128)(2,1)S(1)} %shard_map.87.refs_0_), channel_id=1, source_target_pairs={{0,1},{1,2},{2,3},{3,0},{4,5},{5,6},{6,7},{7,4},{8,9},{9,10},{10,1... | collective-permute-start | bytes 331784 | tf_op jit(solution)/shard_map/ppermute | solution.py:44
  39.4 9.3 %collective-permute-start.13 = (bf16[144,384]{1,0:T(8,128)(2,1)S(1)}, bf16[144,384]{1,0:T(8,128)(2,1)S(1)}, u32[]{:S(2)}, u32[]{:S(2)}) collective-permute-start(bf16[144,384]{1,0:T(8,128)(2,1)S(1)} %shard_map.87.refs_0_), channel_id=1, source_target_pairs={{0,2},{1,3},{2,0},{3,1},{4,6},{5,7},{6,4},{7,5},{8,10},{9,11},{10,... | collective-permute-start | bytes 331784 | tf_op jit(solution)/shard_map/ppermute | solution.py:44
  42.4 6.3 %collective-permute-start.37 = (bf16[1,4,48,512]{3,2,1,0:T(8,128)(2,1)S(1)}, bf16[1,4,48,512]{3,2,1,0:T(8,128)(2,1)S(1)}, u32[]{:S(2)}, u32[]{:S(2)}) collective-permute-start(bf16[1,4,48,512]{3,2,1,0:T(8,128)(2,1)S(1)} %dynamic-slice_bitcast_fusion), channel_id=1, source_target_pairs={{0,16},{4,20},{8,24},{12,28},{16,0},{20,4},{24,8},{28,12},{1,17},{... | collective-permute-start | bytes 589832 | tf_op jit(solution)/shard_map/ppermute | solution.py:58
  42.5 6.5 %collective-permute-start.16 = (bf16[4,4,48,256]{3,2,1,0:T(8,128)(2,1)S(1)}, bf16[4,4,48,256]{3,2,1,0:T(8,128)(2,1)S(1)}, u32[]{:S(2)}, u32[]{:S(2)}) collective-permute-start(bf16[4,4,48,256]{3,2,1,0:T(8,128)(2,1)S(1)} %constant_dynamic-update-slice_fusion.2.refs_10_), channel_id=1, source_target_pairs={{0,4},{4,0},{8,12},{12,8},{16,20},{20,16},{24,28},{28,24},{1,5},{5... | collective-permute-start | bytes 1179656 | tf_op jit(solution)/shard_map/ppermute | solution.py:57
  48.8 17.5 %collective-permute-start.38 = (bf16[2,4,48,512]{3,2,1,0:T(8,128)(2,1)S(1)}, bf16[2,4,48,512]{3,2,1,0:T(8,128)(2,1)S(1)}, u32[]{:S(2)}, u32[]{:S(2)}) collective-permute-start(bf16[2,4,48,512]{3,2,1,0:T(8,128)(2,1)S(1)} %constant_dynamic-update-slice_fusion.4), channel_id=1, source_target_pairs={{0,8},{4,12},{8,0},{12,4},{16,24},{20,28},{24,16},{28,20},{1,9},{5... | collective-permute-start | bytes 1179656 | tf_op jit(solution)/shard_map/ppermute | solution.py:58
  50.9 9.5 %collective-permute-start.20 = (bf16[128,128]{1,0:T(8,128)(2,1)S(1)}, bf16[128,128]{1,0:T(8,128)(2,1)S(1)}, u32[]{:S(2)}, u32[]{:S(2)}) collective-permute-start(bf16[128,128]{1,0:T(8,128)(2,1)S(1)} %get-tuple-element.101), channel_id=1, source_target_pairs={{4,0},{8,4},{12,8},{16,12},{20,16},{24,20},{28,24},{5,1},{9,5},{13... | collective-permute-start | bytes 98312 | tf_op jit(solution)/shard_map/ppermute | solution.py:37
  54.5 6.1 %collective-permute-start.21 = (bf16[128,128]{1,0:T(8,128)(2,1)S(1)}, bf16[128,128]{1,0:T(8,128)(2,1)S(1)}, u32[]{:S(2)}, u32[]{:S(2)}) collective-permute-start(bf16[128,128]{1,0:T(8,128)(2,1)S(1)} %get-tuple-element.102), channel_id=1, source_target_pairs={{8,0},{12,4},{16,8},{20,12},{24,16},{28,20},{9,1},{13,5},{17,9},{2... | collective-permute-start | bytes 98312 | tf_op jit(solution)/shard_map/ppermute | solution.py:37
  55.8 8.8 %collective-permute-start.22 = (bf16[128,128]{1,0:T(8,128)(2,1)S(1)}, bf16[128,128]{1,0:T(8,128)(2,1)S(1)}, u32[]{:S(2)}, u32[]{:S(2)}) collective-permute-start(bf16[128,128]{1,0:T(8,128)(2,1)S(1)} %get-tuple-element.103), channel_id=1, source_target_pairs={{12,0},{16,4},{20,8},{24,12},{28,16},{13,1},{17,5},{21,9},{25,13},... | collective-permute-start | bytes 98312 | tf_op jit(solution)/shard_map/ppermute | solution.py:37
  57.1 7.8 %collective-permute-start.23 = (bf16[128,128]{1,0:T(8,128)(2,1)S(1)}, bf16[128,128]{1,0:T(8,128)(2,1)S(1)}, u32[]{:S(2)}, u32[]{:S(2)}) collective-permute-start(bf16[128,128]{1,0:T(8,128)(2,1)S(1)} %get-tuple-element.104), channel_id=1, source_target_pairs={{16,0},{20,4},{24,8},{28,12},{17,1},{21,5},{25,9},{29,13},{18,2},{... | collective-permute-start | bytes 98312 | tf_op jit(solution)/shard_map/ppermute | solution.py:37
  60.4 8.5 %collective-permute-start.19 = (bf16[128,256]{1,0:T(8,128)(2,1)S(1)}, bf16[128,256]{1,0:T(8,128)(2,1)S(1)}, u32[]{:S(2)}, u32[]{:S(2)}) collective-permute-start(bf16[128,256]{1,0:T(8,128)(2,1)S(1)} %shard_map.89.gq_ref.refs_0_), channel_id=1, source_target_pairs={{0,1},{1,2},{2,3},{3,0},{4,5},{5,6},{6,7},{7,4},{8,9},{9,10},{10,1... | collective-permute-start | bytes 196616 | tf_op jit(solution)/shard_map/ppermute | solution.py:44
  60.6 8.3 %collective-permute-start.18 = (bf16[128,256]{1,0:T(8,128)(2,1)S(1)}, bf16[128,256]{1,0:T(8,128)(2,1)S(1)}, u32[]{:S(2)}, u32[]{:S(2)}) collective-permute-start(bf16[128,256]{1,0:T(8,128)(2,1)S(1)} %shard_map.89.gq_ref.refs_0_), channel_id=1, source_target_pairs={{0,2},{1,3},{2,0},{3,1},{4,6},{5,7},{6,4},{7,5},{8,10},{9,11},{10,... | collective-permute-start | bytes 196616 | tf_op jit(solution)/shard_map/ppermute | solution.py:44
  64.6 4.8 %collective-permute-start.17 = (bf16[128,256]{1,0:T(8,128)(2,1)S(1)}, bf16[128,256]{1,0:T(8,128)(2,1)S(1)}, u32[]{:S(2)}, u32[]{:S(2)}) collective-permute-start(bf16[128,256]{1,0:T(8,128)(2,1)S(1)} %shard_map.89.gq_ref.refs_0_), channel_id=1, source_target_pairs={{0,3},{1,0},{2,1},{3,2},{4,7},{5,4},{6,5},{7,6},{8,11},{9,8},{10,9... | collective-permute-start | bytes 196616 | tf_op jit(solution)/shard_map/ppermute | solution.py:44
  65.1 4.9 %collective-permute-start.26 = (bf16[144,128]{1,0:T(8,128)(2,1)S(1)}, bf16[144,128]{1,0:T(8,128)(2,1)S(1)}, u32[]{:S(2)}, u32[]{:S(2)}) collective-permute-start(bf16[144,128]{1,0:T(8,128)(2,1)S(1)} %shard_map.90.refs_4_), channel_id=1, source_target_pairs={{0,1},{1,2},{2,3},{3,0},{4,5},{5,6},{6,7},{7,4},{8,9},{9,10},{10,1... | collective-permute-start | bytes 110600 | tf_op jit(solution)/shard_map/ppermute | solution.py:44
  66.3 5.2 %collective-permute-start.25 = (bf16[144,128]{1,0:T(8,128)(2,1)S(1)}, bf16[144,128]{1,0:T(8,128)(2,1)S(1)}, u32[]{:S(2)}, u32[]{:S(2)}) collective-permute-start(bf16[144,128]{1,0:T(8,128)(2,1)S(1)} %shard_map.90.refs_4_), channel_id=1, source_target_pairs={{0,2},{1,3},{2,0},{3,1},{4,6},{5,7},{6,4},{7,5},{8,10},{9,11},{10,... | collective-permute-start | bytes 110600 | tf_op jit(solution)/shard_map/ppermute | solution.py:44
  68.9 3.5 %collective-permute-start.24 = (bf16[144,128]{1,0:T(8,128)(2,1)S(1)}, bf16[144,128]{1,0:T(8,128)(2,1)S(1)}, u32[]{:S(2)}, u32[]{:S(2)}) collective-permute-start(bf16[144,128]{1,0:T(8,128)(2,1)S(1)} %shard_map.90.refs_4_), channel_id=1, source_target_pairs={{0,3},{1,0},{2,1},{3,2},{4,7},{5,4},{6,5},{7,6},{8,11},{9,8},{10,9... | collective-permute-start | bytes 110600 | tf_op jit(solution)/shard_map/ppermute | solution.py:44
  72.5 22.9 %collective-permute-start.39 = (bf16[4,4,48,512]{3,2,1,0:T(8,128)(2,1)S(1)}, bf16[4,4,48,512]{3,2,1,0:T(8,128)(2,1)S(1)}, u32[]{:S(2)}, u32[]{:S(2)}) collective-permute-start(bf16[4,4,48,512]{3,2,1,0:T(8,128)(2,1)S(1)} %constant_dynamic-update-slice_fusion.6.refs_12_), channel_id=1, source_target_pairs={{0,4},{4,0},{8,12},{12,8},{16,20},{20,16},{24,28},{28,24},{1,5},{5... | collective-permute-start | bytes 2359304 | tf_op jit(solution)/shard_map/ppermute | solution.py:57
  75.6 6.2 %collective-permute-start.30 = (bf16[128,128]{1,0:T(8,128)(2,1)S(1)}, bf16[128,128]{1,0:T(8,128)(2,1)S(1)}, u32[]{:S(2)}, u32[]{:S(2)}) collective-permute-start(bf16[128,128]{1,0:T(8,128)(2,1)S(1)} %get-tuple-element.108), channel_id=1, source_target_pairs={{4,0},{8,4},{12,8},{16,12},{20,16},{24,20},{28,24},{5,1},{9,5},{13... | collective-permute-start | bytes 98312 | tf_op jit(solution)/shard_map/ppermute | solution.py:37
  77.6 4.8 %collective-permute-start.31 = (bf16[128,128]{1,0:T(8,128)(2,1)S(1)}, bf16[128,128]{1,0:T(8,128)(2,1)S(1)}, u32[]{:S(2)}, u32[]{:S(2)}) collective-permute-start(bf16[128,128]{1,0:T(8,128)(2,1)S(1)} %get-tuple-element.109), channel_id=1, source_target_pairs={{8,0},{12,4},{16,8},{20,12},{24,16},{28,20},{9,1},{13,5},{17,9},{2... | collective-permute-start | bytes 98312 | tf_op jit(solution)/shard_map/ppermute | solution.py:37
  78.9 7.3 %collective-permute-start.32 = (bf16[128,128]{1,0:T(8,128)(2,1)S(1)}, bf16[128,128]{1,0:T(8,128)(2,1)S(1)}, u32[]{:S(2)}, u32[]{:S(2)}) collective-permute-start(bf16[128,128]{1,0:T(8,128)(2,1)S(1)} %get-tuple-element.110), channel_id=1, source_target_pairs={{12,0},{16,4},{20,8},{24,12},{28,16},{13,1},{17,5},{21,9},{25,13},... | collective-permute-start | bytes 98312 | tf_op jit(solution)/shard_map/ppermute | solution.py:37
  80.2 7.1 %collective-permute-start.33 = (bf16[128,128]{1,0:T(8,128)(2,1)S(1)}, bf16[128,128]{1,0:T(8,128)(2,1)S(1)}, u32[]{:S(2)}, u32[]{:S(2)}) collective-permute-start(bf16[128,128]{1,0:T(8,128)(2,1)S(1)} %get-tuple-element.111), channel_id=1, source_target_pairs={{16,0},{20,4},{24,8},{28,12},{17,1},{21,5},{25,9},{29,13},{18,2},{... | collective-permute-start | bytes 98312 | tf_op jit(solution)/shard_map/ppermute | solution.py:37
  81.8 6.0 %collective-permute-start.29 = (bf16[128,256]{1,0:T(8,128)(2,1)S(1)}, bf16[128,256]{1,0:T(8,128)(2,1)S(1)}, u32[]{:S(2)}, u32[]{:S(2)}) collective-permute-start(bf16[128,256]{1,0:T(8,128)(2,1)S(1)} %shard_map.92.gq_ref.refs_0_), channel_id=1, source_target_pairs={{0,1},{1,2},{2,3},{3,0},{4,5},{5,6},{6,7},{7,4},{8,9},{9,10},{10,1... | collective-permute-start | bytes 196616 | tf_op jit(solution)/shard_map/ppermute | solution.py:44
  82.4 9.3 %collective-permute-start.28 = (bf16[128,256]{1,0:T(8,128)(2,1)S(1)}, bf16[128,256]{1,0:T(8,128)(2,1)S(1)}, u32[]{:S(2)}, u32[]{:S(2)}) collective-permute-start(bf16[128,256]{1,0:T(8,128)(2,1)S(1)} %shard_map.92.gq_ref.refs_0_), channel_id=1, source_target_pairs={{0,2},{1,3},{2,0},{3,1},{4,6},{5,7},{6,4},{7,5},{8,10},{9,11},{10,... | collective-permute-start | bytes 196616 | tf_op jit(solution)/shard_map/ppermute | solution.py:44
  86.2 5.5 %collective-permute-start.27 = (bf16[128,256]{1,0:T(8,128)(2,1)S(1)}, bf16[128,256]{1,0:T(8,128)(2,1)S(1)}, u32[]{:S(2)}, u32[]{:S(2)}) collective-permute-start(bf16[128,256]{1,0:T(8,128)(2,1)S(1)} %shard_map.92.gq_ref.refs_0_), channel_id=1, source_target_pairs={{0,3},{1,0},{2,1},{3,2},{4,7},{5,4},{6,5},{7,6},{8,11},{9,8},{10,9... | collective-permute-start | bytes 196616 | tf_op jit(solution)/shard_map/ppermute | solution.py:44
  87.3 8.1 %copy-start = (bf16[128,2048]{1,0:T(8,128)(2,1)S(1)}, bf16[128,2048]{1,0:T(8,128)(2,1)}, u32[]{:S(2)}) copy-start(bf16[128,2048]{1,0:T(8,128)(2,1)} %refs_14_.1) | copy-start | bytes 1572868
  87.3 8.1 %copy-start.1 = (bf16[128,2048]{1,0:T(8,128)(2,1)S(1)}, bf16[128,2048]{1,0:T(8,128)(2,1)}, u32[]{:S(2)}) copy-start(bf16[128,2048]{1,0:T(8,128)(2,1)} %up_ref.3) | copy-start | bytes 1572868
  87.3 8.1 %copy-start.2 = (f32[2048]{0:T(1024)S(1)}, f32[2048]{0:T(1024)}, u32[]{:S(2)}) copy-start(f32[2048]{0:T(1024)} %param.10) | copy-start | bytes 24580
  87.4 4.6 %collective-permute-start.36 = (bf16[144,128]{1,0:T(8,128)(2,1)S(1)}, bf16[144,128]{1,0:T(8,128)(2,1)S(1)}, u32[]{:S(2)}, u32[]{:S(2)}) collective-permute-start(bf16[144,128]{1,0:T(8,128)(2,1)S(1)} %shard_map.93.refs_4_), channel_id=1, source_target_pairs={{0,1},{1,2},{2,3},{3,0},{4,5},{5,6},{6,7},{7,4},{8,9},{9,10},{10,1... | collective-permute-start | bytes 110600 | tf_op jit(solution)/shard_map/ppermute | solution.py:44
  87.8 6.6 %collective-permute-start.35 = (bf16[144,128]{1,0:T(8,128)(2,1)S(1)}, bf16[144,128]{1,0:T(8,128)(2,1)S(1)}, u32[]{:S(2)}, u32[]{:S(2)}) collective-permute-start(bf16[144,128]{1,0:T(8,128)(2,1)S(1)} %shard_map.93.refs_4_), channel_id=1, source_target_pairs={{0,2},{1,3},{2,0},{3,1},{4,6},{5,7},{6,4},{7,5},{8,10},{9,11},{10,... | collective-permute-start | bytes 110600 | tf_op jit(solution)/shard_map/ppermute | solution.py:44
  91.7 3.7 %collective-permute-start.34 = (bf16[144,128]{1,0:T(8,128)(2,1)S(1)}, bf16[144,128]{1,0:T(8,128)(2,1)S(1)}, u32[]{:S(2)}, u32[]{:S(2)}) collective-permute-start(bf16[144,128]{1,0:T(8,128)(2,1)S(1)} %shard_map.93.refs_4_), channel_id=1, source_target_pairs={{0,3},{1,0},{2,1},{3,2},{4,7},{5,4},{6,5},{7,6},{8,11},{9,8},{10,9... | collective-permute-start | bytes 110600 | tf_op jit(solution)/shard_map/ppermute | solution.py:44
  115.8 4.9 %collective-permute-start.42 = (bf16[128,512]{1,0:T(8,128)(2,1)S(1)}, bf16[128,512]{1,0:T(8,128)(2,1)S(1)}, u32[]{:S(2)}, u32[]{:S(2)}) collective-permute-start(bf16[128,512]{1,0:T(8,128)(2,1)S(1)} %shard_map.95.refs_0_), channel_id=1, source_target_pairs={{0,1},{1,2},{2,3},{3,0},{4,5},{5,6},{6,7},{7,4},{8,9},{9,10},{10,1... | collective-permute-start | bytes 393224 | tf_op jit(solution)/shard_map/ppermute | solution.py:44
  116.3 10.8 %collective-permute-start.41 = (bf16[128,512]{1,0:T(8,128)(2,1)S(1)}, bf16[128,512]{1,0:T(8,128)(2,1)S(1)}, u32[]{:S(2)}, u32[]{:S(2)}) collective-permute-start(bf16[128,512]{1,0:T(8,128)(2,1)S(1)} %shard_map.95.refs_0_), channel_id=1, source_target_pairs={{0,2},{1,3},{2,0},{3,1},{4,6},{5,7},{6,4},{7,5},{8,10},{9,11},{10,... | collective-permute-start | bytes 393224 | tf_op jit(solution)/shard_map/ppermute | solution.py:44
  118.6 12.3 %collective-permute-start.40 = (bf16[128,512]{1,0:T(8,128)(2,1)S(1)}, bf16[128,512]{1,0:T(8,128)(2,1)S(1)}, u32[]{:S(2)}, u32[]{:S(2)}) collective-permute-start(bf16[128,512]{1,0:T(8,128)(2,1)S(1)} %shard_map.95.refs_0_), channel_id=1, source_target_pairs={{0,3},{1,0},{2,1},{3,2},{4,7},{5,4},{6,5},{7,6},{8,11},{9,8},{10,9... | collective-permute-start | bytes 393224 | tf_op jit(solution)/shard_map/ppermute | solution.py:44
where the time goes:
time: 133 us; the launch traced here: 132 us
  starting transfers between devices  64.7 us (49%)
  waiting for transfers between devices  32.5 us (24%)
  blocking collectives  17.8 us (13%)
  Pallas kernels  16.7 us (13%)
    ppermute x16, starting transfers between devices, shifted(): lax.ppermute(value, axis, [(source, source + steps) for source in range(i...  32.8 us
    ppermute x21, starting transfers between devices, rotated(): lax.ppermute(value, axis, [(i, (i - step) % count) for i in range(count)])  27.3 us
    ppermute x21, waiting for transfers between devices, rotated(): lax.ppermute(value, axis, [(i, (i - step) % count) for i in range(count)])  24.4 us
    all_to_all x1, blocking collectives, shards(): totals = lax.all_to_all(totals, ('seq', 'head'), 0, 0)  17.8 us
    ppermute x16, waiting for transfers between devices, shifted(): lax.ppermute(value, axis, [(source, source + steps) for source in range(i...  8.13 us
    pallas_call x2, Pallas kernels, shards(): local_call(functools.partial(next_body, heads, parts, scale, step == 1),...  3.82 us
    pallas_call x1, Pallas kernels, shards(): local_call(functools.partial(start_body, heads), [shape_of((rows, wide),...  3.59 us
  transfers between devices with their start and end apart: 43, of which 18 were waited for; matrix products, arithmetic and copies ran while one was open for 0% of the time, Pallas kernels for 7%

commit v1 on v0

--- a/solution.py
+++ b/solution.py
@@ -451,8 +451,11 @@
     pull_outs += [shape_of((rows, narrow), BF16)] * WIN_DEVS
     pull_flops = 6 * span * e * heads * rows
 
-    def exchange(score, own, terms, split):
-        arrived = [shifted(term, "seq", -offset - 1) for offset, term in enumerate(terms)]
+    def exchange(score, own, terms, split, step):
+        if step == 2:
+            score, weight[:] = (lambda a, *b: (a, list(b)))(
+                *lax.optimization_barrier((score, *weight))
+            )
         gq = local_call(
             functools.partial(query_body, heads, scale),
             shape_of((rows, wide), BF16),
@@ -460,7 +463,10 @@
             span * heads * rows * 2,
             4,
         )(kt, score)
+        arrived = [shifted(term, "seq", -offset - 1) for offset, term in enumerate(terms)]
         ahead = rotated(gq, "head") if split else []
+        if step in (2,):
+            arrived = list(lax.optimization_barrier((tuple(arrived), tuple(ahead[1:1+3])))[0])
         if not split:
             arrived = list(lax.optimization_barrier((tuple(arrived), near[1]))[0])
         msg = local_call(
@@ -517,14 +523,16 @@
             *terms, share = lax.optimization_barrier((*terms, share))
             pairs = [(i, i ^ (group // 2)) for i in range(seq_count)]
             near = [share[None], lax.ppermute(share[None], "seq", pairs)]
-        every_msg, msg, ahead = exchange(score, own, terms, step > 0)
+        every_msg, msg, ahead = exchange(score, own, terms, step > 0, step)
         if step == 0:
             chain = doubled(near, "seq", group // 2, (msg, every_msg[1:2]))
         marks.append(dict(msg=msg, sent=(ahead[1:], every_msg[1:])))
-
-    part = width // parts
-    mine = lax.dynamic_slice_in_dim(every_cols, head * part, part, 2)
-    weight = doubled([mine[None]], "seq", group, (marks[0]["msg"], marks[0]["sent"], marks[1]["sent"]))
+        if step == 1:
+            gates = (marks[0]["msg"], marks[0]["sent"], marks[1]["sent"])
+            part = width // parts
+            mine = lax.dynamic_slice_in_dim(every_cols, head * part, part, 2)
+            weight = doubled([mine[None]], "seq", group, gates)
+
     small = seq_count * parts <= 64
     fields, totals = local_call(
         functools.partial(field_body, parts, wide),

time: 133 us -> 131 us (0.985)
  waiting for transfers between devices: 32.5 us -> 36.1 us
  blocking collectives: 17.8 us -> 14.4 us
  starting transfers between devices: 64.7 us -> 62.8 us
    ppermute x16, waiting for transfers between devices: 8.13 us -> 12.5 us  [shifted(): lax.ppermute(value, axis, [(source, source + steps) for source in range(i...]
    all_to_all x1, blocking collectives: 17.8 us -> 14.4 us  [shards(): totals = lax.all_to_all(totals, ('seq', 'head'), 0, 0)]
    ppermute x21, starting transfers between devices: 27.3 us -> 25.4 us  [rotated(): lax.ppermute(value, axis, [(i, (i - step) % count) for i in range(count)])]
where the time goes in v1:
time: 131 us
  starting transfers between devices  62.8 us (48%)
  waiting for transfers between devices  36.1 us (28%)
  Pallas kernels  16.7 us (13%)
  blocking collectives  14.4 us (11%)
    ppermute x16, starting transfers between devices, shifted(): lax.ppermute(value, axis, [(source, source + steps) for source in range(i...  32.8 us
    ppermute x21, starting transfers between devices, rotated(): lax.ppermute(value, axis, [(i, (i - step) % count) for i in range(count)])  25.4 us
    ppermute x21, waiting for transfers between devices, rotated(): lax.ppermute(value, axis, [(i, (i - step) % count) for i in range(count)])  23.7 us
    all_to_all x1, blocking collectives, shards(): totals = lax.all_to_all(totals, ('seq', 'head'), 0, 0)  14.4 us
    ppermute x16, waiting for transfers between devices, shifted(): lax.ppermute(value, axis, [(source, source + steps) for source in range(i...  12.5 us
    pallas_call x2, Pallas kernels, shards(): local_call(functools.partial(next_body, heads, parts, scale, step == 1),...  3.82 us
    pallas_call x1, Pallas kernels, shards(): local_call(functools.partial(start_body, heads), [shape_of((rows, wide),...  3.59 us
  transfers between devices with their start and end apart: 43, of which 18 were waited for; matrix products, arithmetic and copies ran while one was open for 0% of the time, Pallas kernels for 7%

profile of v1, /device:TPU:9, one launch (start us, length us, event | category | flops | bytes accessed | tf_op | source)
XLA Modules:
  0.0 130.8 jit_solution(14265020047784640730)
XLA Ops:
  0.0 2.1 %shard_map.82 = (bf16[48,2048]{1,0:T(8,128)(2,1)S(1)}, bf16[128,2048]{1,0:T(8,128)(2,1)S(1)}, bf16[128,128]{1,0:T(8,128)(2,1)S(1)}, f32[128,128]{1,0:T(8,128)S(1)}, f32[128,128]{1,0:T(8,128)S(1)}) custom-call(s32[1]{0:T(128)} %bitcast.2.block_ref, bf16[2048,256]{1,0:T(8,128)(2,1)} %qw_ref.3, bf16[2048,128]{1,0:T(8,128)(2,1)} %kvw_ref.1, ...), custom_call_target="tpu_custom_call" | custom-call | flops 75497472 | bytes 1572864 | tf_op jit(solution)/shard_map/pallas_call | solution.py:384
  2.1 1.3 %collective-permute-start.6 = (bf16[48,2048]{1,0:T(8,128)(2,1)S(1)}, bf16[48,2048]{1,0:T(8,128)(2,1)S(1)}, u32[]{:S(2)}, u32[]{:S(2)}) collective-permute-start(bf16[48,2048]{1,0:T(8,128)(2,1)S(1)} %get-tuple-element.87), channel_id=1, source_target_pairs={{0,1},{1,2},{2,3},{3,0},{4,5},{5,6},{6,7},{7,4},{8,9},{9,10},{10,1... | collective-permute-start | bytes 589832 | tf_op jit(solution)/shard_map/ppermute | solution.py:44
  3.4 1.1 collective-permute-start.5
  4.5 1.4 %collective-permute-start.4 = (bf16[48,2048]{1,0:T(8,128)(2,1)S(1)}, bf16[48,2048]{1,0:T(8,128)(2,1)S(1)}, u32[]{:S(2)}, u32[]{:S(2)}) collective-permute-start(bf16[48,2048]{1,0:T(8,128)(2,1)S(1)} %get-tuple-element.87), channel_id=1, source_target_pairs={{0,3},{1,0},{2,1},{3,2},{4,7},{5,4},{6,5},{7,6},{8,11},{9,8},{10,9... | collective-permute-start | bytes 589832 | tf_op jit(solution)/shard_map/ppermute | solution.py:44
  5.9 4.5 %collective-permute-start.3 = (bf16[128,128]{1,0:T(8,128)(2,1)S(1)}, bf16[128,128]{1,0:T(8,128)(2,1)S(1)}, u32[]{:S(2)}, u32[]{:S(2)}) collective-permute-start(bf16[128,128]{1,0:T(8,128)(2,1)S(1)} %get-tuple-element.71.refs_4_), channel_id=1, source_target_pairs={{0,4},{4,8},{8,12},{12,16},{16,20},{20,24},{24,28},{1,5},{5,9},{9,... | collective-permute-start | bytes 98312 | tf_op jit(solution)/shard_map/ppermute | solution.py:37
  10.4 3.1 %collective-permute-start.2 = (bf16[128,128]{1,0:T(8,128)(2,1)S(1)}, bf16[128,128]{1,0:T(8,128)(2,1)S(1)}, u32[]{:S(2)}, u32[]{:S(2)}) collective-permute-start(bf16[128,128]{1,0:T(8,128)(2,1)S(1)} %get-tuple-element.71.refs_4_), channel_id=1, source_target_pairs={{0,8},{4,12},{8,16},{12,20},{16,24},{20,28},{1,9},{5,13},{9,17},{1... | collective-permute-start | bytes 98312 | tf_op jit(solution)/shard_map/ppermute | solution.py:37
  13.6 3.0 %collective-permute-start.1 = (bf16[128,128]{1,0:T(8,128)(2,1)S(1)}, bf16[128,128]{1,0:T(8,128)(2,1)S(1)}, u32[]{:S(2)}, u32[]{:S(2)}) collective-permute-start(bf16[128,128]{1,0:T(8,128)(2,1)S(1)} %get-tuple-element.71.refs_4_), channel_id=1, source_target_pairs={{0,12},{4,16},{8,20},{12,24},{16,28},{1,13},{5,17},{9,21},{13,25},... | collective-permute-start | bytes 98312 | tf_op jit(solution)/shard_map/ppermute | solution.py:37
  16.6 2.5 %collective-permute-start = (bf16[128,128]{1,0:T(8,128)(2,1)S(1)}, bf16[128,128]{1,0:T(8,128)(2,1)S(1)}, u32[]{:S(2)}, u32[]{:S(2)}) collective-permute-start(bf16[128,128]{1,0:T(8,128)(2,1)S(1)} %get-tuple-element.71.refs_4_), channel_id=1, source_target_pairs={{0,16},{4,20},{8,24},{12,28},{1,17},{5,21},{9,25},{13,29},{2,18},{... | collective-permute-start | bytes 98312 | tf_op jit(solution)/shard_map/ppermute | solution.py:37
  19.1 3.6 %shard_map.83 = (f32[128,256]{1,0:T(8,128)S(1)}, bf16[64,512]{1,0:T(8,128)(2,1)S(1)}, f32[64,512]{1,0:T(8,128)S(1)}, f32[64,512]{1,0:T(8,128)S(1)}, f32[64,512]{...) custom-call(bf16[128,2048]{1,0:T(8,128)(2,1)S(1)} %get-tuple-element.72.hidden_ref, ...), custom_call_target="tpu_custom_call" | custom-call | flops 402653184 | bytes 4194304 | tf_op jit(solution)/shard_map/pallas_call | solution.py:414
  22.7 1.1 shard_map.84
  24.6 2.5 %collective-permute-start.7 = (bf16[128,128]{1,0:T(8,128)(2,1)S(1)}, bf16[128,128]{1,0:T(8,128)(2,1)S(1)}, u32[]{:S(2)}, u32[]{:S(2)}) collective-permute-start(bf16[128,128]{1,0:T(8,128)(2,1)S(1)} %get-tuple-element.90), channel_id=1, source_target_pairs={{4,0},{8,4},{12,8},{16,12},{20,16},{24,20},{28,24},{5,1},{9,5},{13... | collective-permute-start | bytes 98312 | tf_op jit(solution)/shard_map/ppermute | solution.py:37
  27.1 1.3 collective-permute-start.8
  28.4 1.3 collective-permute-start.9
  29.7 1.3 collective-permute-start.10
  32.4 2.8 %collective-permute-done.9.refs_2_ = bf16[128,128]{1,0:T(8,128)(2,1)S(1)} collective-permute-done((bf16[128,128]{1,0:T(8,128)(2,1)S(1)}, bf16[128,128]{1,0:T(8,128)(2,1)S(1)}, u32[]{:S(2)}, u32[]{:S(2)}) %collective-permute-start.9) | collective-permute-done | bytes 32800 | tf_op jit(solution)/shard_map/ppermute | solution.py:37
  36.1 1.8 %collective-permute-start.15 = (bf16[2,4,48,256]{3,2,1,0:T(8,128)(2,1)S(1)}, bf16[2,4,48,256]{3,2,1,0:T(8,128)(2,1)S(1)}, u32[]{:S(2)}, u32[]{:S(2)}) collective-permute-start(bf16[2,4,48,256]{3,2,1,0:T(8,128)(2,1)S(1)} %constant_dynamic-update-slice_fusion), channel_id=1, source_target_pairs={{0,8},{4,12},{8,0},{12,4},{16,24},{20,28},{24,16},{28,20},{1,9},{5... | collective-permute-start | bytes 589832 | tf_op jit(solution)/shard_map/ppermute | solution.py:58
  37.9 1.3 %collective-permute-start.12 = (bf16[144,384]{1,0:T(8,128)(2,1)S(1)}, bf16[144,384]{1,0:T(8,128)(2,1)S(1)}, u32[]{:S(2)}, u32[]{:S(2)}) collective-permute-start(bf16[144,384]{1,0:T(8,128)(2,1)S(1)} %shard_map.87.refs_0_), channel_id=1, source_target_pairs={{0,3},{1,0},{2,1},{3,2},{4,7},{5,4},{6,5},{7,6},{8,11},{9,8},{10,9... | collective-permute-start | bytes 331784 | tf_op jit(solution)/shard_map/ppermute | solution.py:44
  39.4 3.0 %collective-permute-start.13 = (bf16[144,384]{1,0:T(8,128)(2,1)S(1)}, bf16[144,384]{1,0:T(8,128)(2,1)S(1)}, u32[]{:S(2)}, u32[]{:S(2)}) collective-permute-start(bf16[144,384]{1,0:T(8,128)(2,1)S(1)} %shard_map.87.refs_0_), channel_id=1, source_target_pairs={{0,2},{1,3},{2,0},{3,1},{4,6},{5,7},{6,4},{7,5},{8,10},{9,11},{10,... | collective-permute-start | bytes 331784 | tf_op jit(solution)/shard_map/ppermute | solution.py:44
  42.5 1.4 %collective-permute-start.16 = (bf16[4,4,48,256]{3,2,1,0:T(8,128)(2,1)S(1)}, bf16[4,4,48,256]{3,2,1,0:T(8,128)(2,1)S(1)}, u32[]{:S(2)}, u32[]{:S(2)}) collective-permute-start(bf16[4,4,48,256]{3,2,1,0:T(8,128)(2,1)S(1)} %constant_dynamic-update-slice_fusion.2.refs_10_), channel_id=1, source_target_pairs={{0,4},{4,0},{8,12},{12,8},{16,20},{20,16},{24,28},{28,24},{1,5},{5... | collective-permute-start | bytes 1179656 | tf_op jit(solution)/shard_map/ppermute | solution.py:57
  43.8 1.6 %collective-permute-done.14.refs_3_ = bf16[144,384]{1,0:T(8,128)(2,1)S(1)} collective-permute-done((bf16[144,384]{1,0:T(8,128)(2,1)S(1)}, bf16[144,384]{1,0:T(8,128)(2,1)S(1)}, u32[]{:S(2)}, u32[]{:S(2)}) %collective-permute-start.14) | collective-permute-done | bytes 110624 | tf_op jit(solution)/shard_map/ppermute | solution.py:44
  45.4 3.3 %collective-permute-done.13.refs_2_ = bf16[144,384]{1,0:T(8,128)(2,1)S(1)} collective-permute-done((bf16[144,384]{1,0:T(8,128)(2,1)S(1)}, bf16[144,384]{1,0:T(8,128)(2,1)S(1)}, u32[]{:S(2)}, u32[]{:S(2)}) %collective-permute-start.13) | collective-permute-done | bytes 110624 | tf_op jit(solution)/shard_map/ppermute | solution.py:44
  48.9 1.9 %shard_map.88 = (bf16[640,512]{1,0:T(8,128)(2,1)S(1)}, f32[128,128]{1,0:T(8,128)S(1)}, bf16[4,128,384]{2,1,0:T(8,128)(2,1)S(1)}, f32[16,128]{1,0:T(8,128)S(1)}, ...) custom-call(s32[2]{0:T(128)S(1)} %pad_add_fusion.spot_ref, ...), custom_call_target="tpu_custom_call" | custom-call | flops 226492416 | bytes 1441792 | tf_op jit(solution)/shard_map/pallas_call | solution.py:498
  50.9 3.6 %collective-permute-start.20 = (bf16[128,128]{1,0:T(8,128)(2,1)S(1)}, bf16[128,128]{1,0:T(8,128)(2,1)S(1)}, u32[]{:S(2)}, u32[]{:S(2)}) collective-permute-start(bf16[128,128]{1,0:T(8,128)(2,1)S(1)} %get-tuple-element.108), channel_id=1, source_target_pairs={{4,0},{8,4},{12,8},{16,12},{20,16},{24,20},{28,24},{5,1},{9,5},{13... | collective-permute-start | bytes 98312 | tf_op jit(solution)/shard_map/ppermute | solution.py:37
  54.5 1.3 collective-permute-start.21
  55.8 1.3 collective-permute-start.22
  57.1 1.3 collective-permute-start.23
  58.7 1.6 %collective-permute-done.20.refs_0_ = bf16[128,128]{1,0:T(8,128)(2,1)S(1)} collective-permute-done((bf16[128,128]{1,0:T(8,128)(2,1)S(1)}, bf16[128,128]{1,0:T(8,128)(2,1)S(1)}, u32[]{:S(2)}, u32[]{:S(2)}) %collective-permute-start.20) | collective-permute-done | bytes 32800 | tf_op jit(solution)/shard_map/ppermute | solution.py:37
  60.6 4.0 %collective-permute-start.18 = (bf16[128,256]{1,0:T(8,128)(2,1)S(1)}, bf16[128,256]{1,0:T(8,128)(2,1)S(1)}, u32[]{:S(2)}, u32[]{:S(2)}) collective-permute-start(bf16[128,256]{1,0:T(8,128)(2,1)S(1)} %shard_map.89.gq_ref.refs_0_), channel_id=1, source_target_pairs={{0,2},{1,3},{2,0},{3,1},{4,6},{5,7},{6,4},{7,5},{8,10},{9,11},{10,... | collective-permute-start | bytes 196616 | tf_op jit(solution)/shard_map/ppermute | solution.py:44
  65.1 1.2 collective-permute-start.26
  66.3 2.7 %collective-permute-start.25 = (bf16[144,128]{1,0:T(8,128)(2,1)S(1)}, bf16[144,128]{1,0:T(8,128)(2,1)S(1)}, u32[]{:S(2)}, u32[]{:S(2)}) collective-permute-start(bf16[144,128]{1,0:T(8,128)(2,1)S(1)} %shard_map.90.refs_4_), channel_id=1, source_target_pairs={{0,2},{1,3},{2,0},{3,1},{4,6},{5,7},{6,4},{7,5},{8,10},{9,11},{10,... | collective-permute-start | bytes 110600 | tf_op jit(solution)/shard_map/ppermute | solution.py:44
  70.0 1.4 %collective-permute-done.25.refs_6_ = bf16[144,128]{1,0:T(8,128)(2,1)S(1)} collective-permute-done((bf16[144,128]{1,0:T(8,128)(2,1)S(1)}, bf16[144,128]{1,0:T(8,128)(2,1)S(1)}, u32[]{:S(2)}, u32[]{:S(2)}) %collective-permute-start.25) | collective-permute-done | bytes 36896 | tf_op jit(solution)/shard_map/ppermute | solution.py:44
  72.5 1.2 collective-permute-start.29
  73.7 1.9 %shard_map.91 = (bf16[640,512]{1,0:T(8,128)(2,1)S(1)}, f32[128,128]{1,0:T(8,128)S(1)}, bf16[4,128,384]{2,1,0:T(8,128)(2,1)S(1)}, f32[16,128]{1,0:T(8,128)S(1)}, ...) custom-call(s32[2]{0:T(128)S(1)} %pad_add_fusion.spot_ref, ...), custom_call_target="tpu_custom_call" | custom-call | flops 226492416 | bytes 1441792 | tf_op jit(solution)/shard_map/pallas_call | solution.py:498
  75.6 1.9 %collective-permute-start.33 = (bf16[128,128]{1,0:T(8,128)(2,1)S(1)}, bf16[128,128]{1,0:T(8,128)(2,1)S(1)}, u32[]{:S(2)}, u32[]{:S(2)}) collective-permute-start(bf16[128,128]{1,0:T(8,128)(2,1)S(1)} %get-tuple-element.121), channel_id=1, source_target_pairs={{4,0},{8,4},{12,8},{16,12},{20,16},{24,20},{28,24},{5,1},{9,5},{13... | collective-permute-start | bytes 98312 | tf_op jit(solution)/shard_map/ppermute | solution.py:37
  77.6 1.3 collective-permute-start.34
  79.3 2.9 %collective-permute-start.31 = (bf16[128,256]{1,0:T(8,128)(2,1)S(1)}, bf16[128,256]{1,0:T(8,128)(2,1)S(1)}, u32[]{:S(2)}, u32[]{:S(2)}) collective-permute-start(bf16[128,256]{1,0:T(8,128)(2,1)S(1)} %shard_map.92.gq_ref.refs_0_), channel_id=1, source_target_pairs={{0,2},{1,3},{2,0},{3,1},{4,6},{5,7},{6,4},{7,5},{8,10},{9,11},{10,... | collective-permute-start | bytes 196616 | tf_op jit(solution)/shard_map/ppermute | solution.py:44
  82.8 1.3 collective-permute-start.35
  84.1 1.3 collective-permute-start.36
  85.4 5.5 %collective-permute-done.35.refs_2_ = bf16[128,128]{1,0:T(8,128)(2,1)S(1)} collective-permute-done((bf16[128,128]{1,0:T(8,128)(2,1)S(1)}, bf16[128,128]{1,0:T(8,128)(2,1)S(1)}, u32[]{:S(2)}, u32[]{:S(2)}) %collective-permute-start.35) | collective-permute-done | bytes 32800 | tf_op jit(solution)/shard_map/ppermute | solution.py:37
  92.7 1.5 %collective-permute-start.38 = (bf16[144,128]{1,0:T(8,128)(2,1)S(1)}, bf16[144,128]{1,0:T(8,128)(2,1)S(1)}, u32[]{:S(2)}, u32[]{:S(2)}) collective-permute-start(bf16[144,128]{1,0:T(8,128)(2,1)S(1)} %shard_map.93.refs_4_), channel_id=1, source_target_pairs={{0,2},{1,3},{2,0},{3,1},{4,6},{5,7},{6,4},{7,5},{8,10},{9,11},{10,... | collective-permute-start | bytes 110600 | tf_op jit(solution)/shard_map/ppermute | solution.py:44
  94.7 1.7 %collective-permute-done.38.refs_6_ = bf16[144,128]{1,0:T(8,128)(2,1)S(1)} collective-permute-done((bf16[144,128]{1,0:T(8,128)(2,1)S(1)}, bf16[144,128]{1,0:T(8,128)(2,1)S(1)}, u32[]{:S(2)}, u32[]{:S(2)}) %collective-permute-start.38) | collective-permute-done | bytes 36896 | tf_op jit(solution)/shard_map/ppermute | solution.py:44
  97.2 1.9 %shard_map.94 = (f32[3,128,512]{2,1,0:T(8,128)S(1)}, f32[32,8,128]{2,1,0:T(8,128)S(1)}) custom-call(s32[2]{0:T(128)S(1)} %pad_add_fusion.spot_ref, bf16[128,256]{1,0:T(8,128)(2,1)S(1)} %shard_map.92.gq_ref.refs_0_, bf16[128,256]{1,0:T(8,128)(2,1)S(1)} %collective-permute-done.30.refs_1_, bf16[128,256]{1,0:T(8,128)(2,1)S(1)} %collective-permute-done.31.refs_2_, ...), custom_call_target="tpu_custom_call" | custom-call | flops 603979776 | bytes 1572864 | tf_op jit(solution)/shard_map/pallas_call | solution.py:537
  99.0 14.4 %all_to_all.5.tot_ref = f32[32,8,128]{2,1,0:T(8,128)S(1)} all-to-all(f32[32,8,128]{2,1,0:T(8,128)S(1)} %get-tuple-element.135), channel_id=1, replica_groups=mesh['seq'=8,'head'=4] {'seq','head'}, dimensions={0} | all-to-all | bytes 262144 | tf_op jit(solution)/shard_map/all_to_all | solution.py:553
  114.7 2.2 %collective-permute-start.41 = (bf16[128,512]{1,0:T(8,128)(2,1)S(1)}, bf16[128,512]{1,0:T(8,128)(2,1)S(1)}, u32[]{:S(2)}, u32[]{:S(2)}) collective-permute-start(bf16[128,512]{1,0:T(8,128)(2,1)S(1)} %shard_map.95.refs_0_), channel_id=1, source_target_pairs={{0,2},{1,3},{2,0},{3,1},{4,6},{5,7},{6,4},{7,5},{8,10},{9,11},{10,... | collective-permute-start | bytes 393224 | tf_op jit(solution)/shard_map/ppermute | solution.py:44
  117.0 2.2 %collective-permute-done.42.refs_3_ = bf16[128,512]{1,0:T(8,128)(2,1)S(1)} collective-permute-done((bf16[128,512]{1,0:T(8,128)(2,1)S(1)}, bf16[128,512]{1,0:T(8,128)(2,1)S(1)}, u32[]{:S(2)}, u32[]{:S(2)}) %collective-permute-start.42) | collective-permute-done | bytes 131104 | tf_op jit(solution)/shard_map/ppermute | solution.py:44
  119.2 6.4 %collective-permute-done.41.refs_2_ = bf16[128,512]{1,0:T(8,128)(2,1)S(1)} collective-permute-done((bf16[128,512]{1,0:T(8,128)(2,1)S(1)}, bf16[128,512]{1,0:T(8,128)(2,1)S(1)}, u32[]{:S(2)}, u32[]{:S(2)}) %collective-permute-start.41) | collective-permute-done | bytes 131104 | tf_op jit(solution)/shard_map/ppermute | solution.py:44
  125.6 3.7 %collective-permute-done.40.refs_1_ = bf16[128,512]{1,0:T(8,128)(2,1)S(1)} collective-permute-done((bf16[128,512]{1,0:T(8,128)(2,1)S(1)}, bf16[128,512]{1,0:T(8,128)(2,1)S(1)}, u32[]{:S(2)}, u32[]{:S(2)}) %collective-permute-start.40) | collective-permute-done | bytes 131104 | tf_op jit(solution)/shard_map/ppermute | solution.py:44
  129.3 1.6 %shard_map.96 = f32[128,2048]{1,0:T(8,128)} custom-call(s32[2]{0:T(128)S(1)} %pad_add_fusion.spot_ref, bf16[128,512]{1,0:T(8,128)(2,1)S(1)} %shard_map.95.refs_0_, bf16[128,512]{1,0:T(8,128)(2,1)S(1)} %collective-permute-done.40.refs_1_, bf16[128,512]{1,0:T(8,128)(2,1)S(1)} %collective-permute-done.41.refs_2_, ...), custom_call_target="tpu_custom_call" | custom-call | bytes 1572864 | tf_op jit(solution)/shard_map/pallas_call | solution.py:565
  (71 shorter events, 11.9 us)
Async XLA Ops:
  2.1 21.8 %collective-permute-start.6 = (bf16[48,2048]{1,0:T(8,128)(2,1)S(1)}, bf16[48,2048]{1,0:T(8,128)(2,1)S(1)}, u32[]{:S(2)}, u32[]{:S(2)}) collective-permute-start(bf16[48,2048]{1,0:T(8,128)(2,1)S(1)} %get-tuple-element.87), channel_id=1, source_target_pairs={{0,1},{1,2},{2,3},{3,0},{4,5},{5,6},{6,7},{7,4},{8,9},{9,10},{10,1... | collective-permute-start | bytes 589832 | tf_op jit(solution)/shard_map/ppermute | solution.py:44
  3.4 20.5 %collective-permute-start.5 = (bf16[48,2048]{1,0:T(8,128)(2,1)S(1)}, bf16[48,2048]{1,0:T(8,128)(2,1)S(1)}, u32[]{:S(2)}, u32[]{:S(2)}) collective-permute-start(bf16[48,2048]{1,0:T(8,128)(2,1)S(1)} %get-tuple-element.87), channel_id=1, source_target_pairs={{0,2},{1,3},{2,0},{3,1},{4,6},{5,7},{6,4},{7,5},{8,10},{9,11},{10,... | collective-permute-start | bytes 589832 | tf_op jit(solution)/shard_map/ppermute | solution.py:44
  4.5 19.4 %collective-permute-start.4 = (bf16[48,2048]{1,0:T(8,128)(2,1)S(1)}, bf16[48,2048]{1,0:T(8,128)(2,1)S(1)}, u32[]{:S(2)}, u32[]{:S(2)}) collective-permute-start(bf16[48,2048]{1,0:T(8,128)(2,1)S(1)} %get-tuple-element.87), channel_id=1, source_target_pairs={{0,3},{1,0},{2,1},{3,2},{4,7},{5,4},{6,5},{7,6},{8,11},{9,8},{10,9... | collective-permute-start | bytes 589832 | tf_op jit(solution)/shard_map/ppermute | solution.py:44
  5.9 7.6 %collective-permute-start.3 = (bf16[128,128]{1,0:T(8,128)(2,1)S(1)}, bf16[128,128]{1,0:T(8,128)(2,1)S(1)}, u32[]{:S(2)}, u32[]{:S(2)}) collective-permute-start(bf16[128,128]{1,0:T(8,128)(2,1)S(1)} %get-tuple-element.71.refs_4_), channel_id=1, source_target_pairs={{0,4},{4,8},{8,12},{12,16},{16,20},{20,24},{24,28},{1,5},{5,9},{9,... | collective-permute-start | bytes 98312 | tf_op jit(solution)/shard_map/ppermute | solution.py:37
  10.4 6.2 %collective-permute-start.2 = (bf16[128,128]{1,0:T(8,128)(2,1)S(1)}, bf16[128,128]{1,0:T(8,128)(2,1)S(1)}, u32[]{:S(2)}, u32[]{:S(2)}) collective-permute-start(bf16[128,128]{1,0:T(8,128)(2,1)S(1)} %get-tuple-element.71.refs_4_), channel_id=1, source_target_pairs={{0,8},{4,12},{8,16},{12,20},{16,24},{20,28},{1,9},{5,13},{9,17},{1... | collective-permute-start | bytes 98312 | tf_op jit(solution)/shard_map/ppermute | solution.py:37
  13.6 9.2 %collective-permute-start.1 = (bf16[128,128]{1,0:T(8,128)(2,1)S(1)}, bf16[128,128]{1,0:T(8,128)(2,1)S(1)}, u32[]{:S(2)}, u32[]{:S(2)}) collective-permute-start(bf16[128,128]{1,0:T(8,128)(2,1)S(1)} %get-tuple-element.71.refs_4_), channel_id=1, source_target_pairs={{0,12},{4,16},{8,20},{12,24},{16,28},{1,13},{5,17},{9,21},{13,25},... | collective-permute-start | bytes 98312 | tf_op jit(solution)/shard_map/ppermute | solution.py:37
  16.6 6.2 %collective-permute-start = (bf16[128,128]{1,0:T(8,128)(2,1)S(1)}, bf16[128,128]{1,0:T(8,128)(2,1)S(1)}, u32[]{:S(2)}, u32[]{:S(2)}) collective-permute-start(bf16[128,128]{1,0:T(8,128)(2,1)S(1)} %get-tuple-element.71.refs_4_), channel_id=1, source_target_pairs={{0,16},{4,20},{8,24},{12,28},{1,17},{5,21},{9,25},{13,29},{2,18},{... | collective-permute-start | bytes 98312 | tf_op jit(solution)/shard_map/ppermute | solution.py:37
  24.5 11.3 %collective-permute-start.11 = (bf16[1,4,48,256]{3,2,1,0:T(8,128)(2,1)S(1)}, bf16[1,4,48,256]{3,2,1,0:T(8,128)(2,1)S(1)}, u32[]{:S(2)}, u32[]{:S(2)}) collective-permute-start(bf16[1,4,48,256]{3,2,1,0:T(8,128)(2,1)S(1)} %bitcast.14), channel_id=1, source_target_pairs={{0,16},{4,20},{8,24},{12,28},{16,0},{20,4},{24,8},{28,12},{1,17},{... | collective-permute-start | bytes 294920 | tf_op jit(solution)/shard_map/ppermute | solution.py:525
  24.6 6.7 %collective-permute-start.7 = (bf16[128,128]{1,0:T(8,128)(2,1)S(1)}, bf16[128,128]{1,0:T(8,128)(2,1)S(1)}, u32[]{:S(2)}, u32[]{:S(2)}) collective-permute-start(bf16[128,128]{1,0:T(8,128)(2,1)S(1)} %get-tuple-element.90), channel_id=1, source_target_pairs={{4,0},{8,4},{12,8},{16,12},{20,16},{24,20},{28,24},{5,1},{9,5},{13... | collective-permute-start | bytes 98312 | tf_op jit(solution)/shard_map/ppermute | solution.py:37
  27.1 5.3 %collective-permute-start.8 = (bf16[128,128]{1,0:T(8,128)(2,1)S(1)}, bf16[128,128]{1,0:T(8,128)(2,1)S(1)}, u32[]{:S(2)}, u32[]{:S(2)}) collective-permute-start(bf16[128,128]{1,0:T(8,128)(2,1)S(1)} %get-tuple-element.91), channel_id=1, source_target_pairs={{8,0},{12,4},{16,8},{20,12},{24,16},{28,20},{9,1},{13,5},{17,9},{2... | collective-permute-start | bytes 98312 | tf_op jit(solution)/shard_map/ppermute | solution.py:37
  28.4 6.8 %collective-permute-start.9 = (bf16[128,128]{1,0:T(8,128)(2,1)S(1)}, bf16[128,128]{1,0:T(8,128)(2,1)S(1)}, u32[]{:S(2)}, u32[]{:S(2)}) collective-permute-start(bf16[128,128]{1,0:T(8,128)(2,1)S(1)} %get-tuple-element.92), channel_id=1, source_target_pairs={{12,0},{16,4},{20,8},{24,12},{28,16},{13,1},{17,5},{21,9},{25,13},... | collective-permute-start | bytes 98312 | tf_op jit(solution)/shard_map/ppermute | solution.py:37
  29.7 6.2 %collective-permute-start.10 = (bf16[128,128]{1,0:T(8,128)(2,1)S(1)}, bf16[128,128]{1,0:T(8,128)(2,1)S(1)}, u32[]{:S(2)}, u32[]{:S(2)}) collective-permute-start(bf16[128,128]{1,0:T(8,128)(2,1)S(1)} %get-tuple-element.93), channel_id=1, source_target_pairs={{16,0},{20,4},{24,8},{28,12},{17,1},{21,5},{25,9},{29,13},{18,2},{... | collective-permute-start | bytes 98312 | tf_op jit(solution)/shard_map/ppermute | solution.py:37
  36.1 6.4 %collective-permute-start.15 = (bf16[2,4,48,256]{3,2,1,0:T(8,128)(2,1)S(1)}, bf16[2,4,48,256]{3,2,1,0:T(8,128)(2,1)S(1)}, u32[]{:S(2)}, u32[]{:S(2)}) collective-permute-start(bf16[2,4,48,256]{3,2,1,0:T(8,128)(2,1)S(1)} %constant_dynamic-update-slice_fusion), channel_id=1, source_target_pairs={{0,8},{4,12},{8,0},{12,4},{16,24},{20,28},{24,16},{28,20},{1,9},{5... | collective-permute-start | bytes 589832 | tf_op jit(solution)/shard_map/ppermute | solution.py:58
  37.9 4.5 %collective-permute-start.12 = (bf16[144,384]{1,0:T(8,128)(2,1)S(1)}, bf16[144,384]{1,0:T(8,128)(2,1)S(1)}, u32[]{:S(2)}, u32[]{:S(2)}) collective-permute-start(bf16[144,384]{1,0:T(8,128)(2,1)S(1)} %shard_map.87.refs_0_), channel_id=1, source_target_pairs={{0,3},{1,0},{2,1},{3,2},{4,7},{5,4},{6,5},{7,6},{8,11},{9,8},{10,9... | collective-permute-start | bytes 331784 | tf_op jit(solution)/shard_map/ppermute | solution.py:44
  39.2 6.2 %collective-permute-start.14 = (bf16[144,384]{1,0:T(8,128)(2,1)S(1)}, bf16[144,384]{1,0:T(8,128)(2,1)S(1)}, u32[]{:S(2)}, u32[]{:S(2)}) collective-permute-start(bf16[144,384]{1,0:T(8,128)(2,1)S(1)} %shard_map.87.refs_0_), channel_id=1, source_target_pairs={{0,1},{1,2},{2,3},{3,0},{4,5},{5,6},{6,7},{7,4},{8,9},{9,10},{10,1... | collective-permute-start | bytes 331784 | tf_op jit(solution)/shard_map/ppermute | solution.py:44
  39.4 9.3 %collective-permute-start.13 = (bf16[144,384]{1,0:T(8,128)(2,1)S(1)}, bf16[144,384]{1,0:T(8,128)(2,1)S(1)}, u32[]{:S(2)}, u32[]{:S(2)}) collective-permute-start(bf16[144,384]{1,0:T(8,128)(2,1)S(1)} %shard_map.87.refs_0_), channel_id=1, source_target_pairs={{0,2},{1,3},{2,0},{3,1},{4,6},{5,7},{6,4},{7,5},{8,10},{9,11},{10,... | collective-permute-start | bytes 331784 | tf_op jit(solution)/shard_map/ppermute | solution.py:44
  42.4 6.3 %collective-permute-start.27 = (bf16[1,4,48,512]{3,2,1,0:T(8,128)(2,1)S(1)}, bf16[1,4,48,512]{3,2,1,0:T(8,128)(2,1)S(1)}, u32[]{:S(2)}, u32[]{:S(2)}) collective-permute-start(bf16[1,4,48,512]{3,2,1,0:T(8,128)(2,1)S(1)} %dynamic-slice_bitcast_fusion), channel_id=1, source_target_pairs={{0,16},{4,20},{8,24},{12,28},{16,0},{20,4},{24,8},{28,12},{1,17},{... | collective-permute-start | bytes 589832 | tf_op jit(solution)/shard_map/ppermute | solution.py:58
  42.5 6.5 %collective-permute-start.16 = (bf16[4,4,48,256]{3,2,1,0:T(8,128)(2,1)S(1)}, bf16[4,4,48,256]{3,2,1,0:T(8,128)(2,1)S(1)}, u32[]{:S(2)}, u32[]{:S(2)}) collective-permute-start(bf16[4,4,48,256]{3,2,1,0:T(8,128)(2,1)S(1)} %constant_dynamic-update-slice_fusion.2.refs_10_), channel_id=1, source_target_pairs={{0,4},{4,0},{8,12},{12,8},{16,20},{20,16},{24,28},{28,24},{1,5},{5... | collective-permute-start | bytes 1179656 | tf_op jit(solution)/shard_map/ppermute | solution.py:57
  48.8 17.5 %collective-permute-start.28 = (bf16[2,4,48,512]{3,2,1,0:T(8,128)(2,1)S(1)}, bf16[2,4,48,512]{3,2,1,0:T(8,128)(2,1)S(1)}, u32[]{:S(2)}, u32[]{:S(2)}) collective-permute-start(bf16[2,4,48,512]{3,2,1,0:T(8,128)(2,1)S(1)} %constant_dynamic-update-slice_fusion.4), channel_id=1, source_target_pairs={{0,8},{4,12},{8,0},{12,4},{16,24},{20,28},{24,16},{28,20},{1,9},{5... | collective-permute-start | bytes 1179656 | tf_op jit(solution)/shard_map/ppermute | solution.py:58
  50.9 9.5 %collective-permute-start.20 = (bf16[128,128]{1,0:T(8,128)(2,1)S(1)}, bf16[128,128]{1,0:T(8,128)(2,1)S(1)}, u32[]{:S(2)}, u32[]{:S(2)}) collective-permute-start(bf16[128,128]{1,0:T(8,128)(2,1)S(1)} %get-tuple-element.108), channel_id=1, source_target_pairs={{4,0},{8,4},{12,8},{16,12},{20,16},{24,20},{28,24},{5,1},{9,5},{13... | collective-permute-start | bytes 98312 | tf_op jit(solution)/shard_map/ppermute | solution.py:37
  54.5 6.1 %collective-permute-start.21 = (bf16[128,128]{1,0:T(8,128)(2,1)S(1)}, bf16[128,128]{1,0:T(8,128)(2,1)S(1)}, u32[]{:S(2)}, u32[]{:S(2)}) collective-permute-start(bf16[128,128]{1,0:T(8,128)(2,1)S(1)} %get-tuple-element.109), channel_id=1, source_target_pairs={{8,0},{12,4},{16,8},{20,12},{24,16},{28,20},{9,1},{13,5},{17,9},{2... | collective-permute-start | bytes 98312 | tf_op jit(solution)/shard_map/ppermute | solution.py:37
  55.8 8.8 %collective-permute-start.22 = (bf16[128,128]{1,0:T(8,128)(2,1)S(1)}, bf16[128,128]{1,0:T(8,128)(2,1)S(1)}, u32[]{:S(2)}, u32[]{:S(2)}) collective-permute-start(bf16[128,128]{1,0:T(8,128)(2,1)S(1)} %get-tuple-element.110), channel_id=1, source_target_pairs={{12,0},{16,4},{20,8},{24,12},{28,16},{13,1},{17,5},{21,9},{25,13},... | collective-permute-start | bytes 98312 | tf_op jit(solution)/shard_map/ppermute | solution.py:37
  57.1 7.8 %collective-permute-start.23 = (bf16[128,128]{1,0:T(8,128)(2,1)S(1)}, bf16[128,128]{1,0:T(8,128)(2,1)S(1)}, u32[]{:S(2)}, u32[]{:S(2)}) collective-permute-start(bf16[128,128]{1,0:T(8,128)(2,1)S(1)} %get-tuple-element.111), channel_id=1, source_target_pairs={{16,0},{20,4},{24,8},{28,12},{17,1},{21,5},{25,9},{29,13},{18,2},{... | collective-permute-start | bytes 98312 | tf_op jit(solution)/shard_map/ppermute | solution.py:37
  60.4 8.5 %collective-permute-start.19 = (bf16[128,256]{1,0:T(8,128)(2,1)S(1)}, bf16[128,256]{1,0:T(8,128)(2,1)S(1)}, u32[]{:S(2)}, u32[]{:S(2)}) collective-permute-start(bf16[128,256]{1,0:T(8,128)(2,1)S(1)} %shard_map.89.gq_ref.refs_0_), channel_id=1, source_target_pairs={{0,1},{1,2},{2,3},{3,0},{4,5},{5,6},{6,7},{7,4},{8,9},{9,10},{10,1... | collective-permute-start | bytes 196616 | tf_op jit(solution)/shard_map/ppermute | solution.py:44
  60.6 8.3 %collective-permute-start.18 = (bf16[128,256]{1,0:T(8,128)(2,1)S(1)}, bf16[128,256]{1,0:T(8,128)(2,1)S(1)}, u32[]{:S(2)}, u32[]{:S(2)}) collective-permute-start(bf16[128,256]{1,0:T(8,128)(2,1)S(1)} %shard_map.89.gq_ref.refs_0_), channel_id=1, source_target_pairs={{0,2},{1,3},{2,0},{3,1},{4,6},{5,7},{6,4},{7,5},{8,10},{9,11},{10,... | collective-permute-start | bytes 196616 | tf_op jit(solution)/shard_map/ppermute | solution.py:44
  64.6 4.8 %collective-permute-start.17 = (bf16[128,256]{1,0:T(8,128)(2,1)S(1)}, bf16[128,256]{1,0:T(8,128)(2,1)S(1)}, u32[]{:S(2)}, u32[]{:S(2)}) collective-permute-start(bf16[128,256]{1,0:T(8,128)(2,1)S(1)} %shard_map.89.gq_ref.refs_0_), channel_id=1, source_target_pairs={{0,3},{1,0},{2,1},{3,2},{4,7},{5,4},{6,5},{7,6},{8,11},{9,8},{10,9... | collective-permute-start | bytes 196616 | tf_op jit(solution)/shard_map/ppermute | solution.py:44
  65.1 4.9 %collective-permute-start.26 = (bf16[144,128]{1,0:T(8,128)(2,1)S(1)}, bf16[144,128]{1,0:T(8,128)(2,1)S(1)}, u32[]{:S(2)}, u32[]{:S(2)}) collective-permute-start(bf16[144,128]{1,0:T(8,128)(2,1)S(1)} %shard_map.90.refs_4_), channel_id=1, source_target_pairs={{0,1},{1,2},{2,3},{3,0},{4,5},{5,6},{6,7},{7,4},{8,9},{9,10},{10,1... | collective-permute-start | bytes 110600 | tf_op jit(solution)/shard_map/ppermute | solution.py:44
  66.3 5.2 %collective-permute-start.25 = (bf16[144,128]{1,0:T(8,128)(2,1)S(1)}, bf16[144,128]{1,0:T(8,128)(2,1)S(1)}, u32[]{:S(2)}, u32[]{:S(2)}) collective-permute-start(bf16[144,128]{1,0:T(8,128)(2,1)S(1)} %shard_map.90.refs_4_), channel_id=1, source_target_pairs={{0,2},{1,3},{2,0},{3,1},{4,6},{5,7},{6,4},{7,5},{8,10},{9,11},{10,... | collective-permute-start | bytes 110600 | tf_op jit(solution)/shard_map/ppermute | solution.py:44
  68.9 3.5 %collective-permute-start.24 = (bf16[144,128]{1,0:T(8,128)(2,1)S(1)}, bf16[144,128]{1,0:T(8,128)(2,1)S(1)}, u32[]{:S(2)}, u32[]{:S(2)}) collective-permute-start(bf16[144,128]{1,0:T(8,128)(2,1)S(1)} %shard_map.90.refs_4_), channel_id=1, source_target_pairs={{0,3},{1,0},{2,1},{3,2},{4,7},{5,4},{6,5},{7,6},{8,11},{9,8},{10,9... | collective-permute-start | bytes 110600 | tf_op jit(solution)/shard_map/ppermute | solution.py:44
  72.5 6.4 %collective-permute-start.29 = (bf16[4,4,48,512]{3,2,1,0:T(8,128)(2,1)S(1)}, bf16[4,4,48,512]{3,2,1,0:T(8,128)(2,1)S(1)}, u32[]{:S(2)}, u32[]{:S(2)}) collective-permute-start(bf16[4,4,48,512]{3,2,1,0:T(8,128)(2,1)S(1)} %constant_dynamic-update-slice_fusion.6.refs_12_), channel_id=1, source_target_pairs={{0,4},{4,0},{8,12},{12,8},{16,20},{20,16},{24,28},{28,24},{1,5},{5... | collective-permute-start | bytes 2359304 | tf_op jit(solution)/shard_map/ppermute | solution.py:57
  75.6 7.2 %collective-permute-start.33 = (bf16[128,128]{1,0:T(8,128)(2,1)S(1)}, bf16[128,128]{1,0:T(8,128)(2,1)S(1)}, u32[]{:S(2)}, u32[]{:S(2)}) collective-permute-start(bf16[128,128]{1,0:T(8,128)(2,1)S(1)} %get-tuple-element.121), channel_id=1, source_target_pairs={{4,0},{8,4},{12,8},{16,12},{20,16},{24,20},{28,24},{5,1},{9,5},{13... | collective-permute-start | bytes 98312 | tf_op jit(solution)/shard_map/ppermute | solution.py:37
  77.6 6.5 %collective-permute-start.34 = (bf16[128,128]{1,0:T(8,128)(2,1)S(1)}, bf16[128,128]{1,0:T(8,128)(2,1)S(1)}, u32[]{:S(2)}, u32[]{:S(2)}) collective-permute-start(bf16[128,128]{1,0:T(8,128)(2,1)S(1)} %get-tuple-element.122), channel_id=1, source_target_pairs={{8,0},{12,4},{16,8},{20,12},{24,16},{28,20},{9,1},{13,5},{17,9},{2... | collective-permute-start | bytes 98312 | tf_op jit(solution)/shard_map/ppermute | solution.py:37
  79.2 12.5 %collective-permute-start.32 = (bf16[128,256]{1,0:T(8,128)(2,1)S(1)}, bf16[128,256]{1,0:T(8,128)(2,1)S(1)}, u32[]{:S(2)}, u32[]{:S(2)}) collective-permute-start(bf16[128,256]{1,0:T(8,128)(2,1)S(1)} %shard_map.92.gq_ref.refs_0_), channel_id=1, source_target_pairs={{0,1},{1,2},{2,3},{3,0},{4,5},{5,6},{6,7},{7,4},{8,9},{9,10},{10,1... | collective-permute-start | bytes 196616 | tf_op jit(solution)/shard_map/ppermute | solution.py:44
  79.3 12.4 %collective-permute-start.31 = (bf16[128,256]{1,0:T(8,128)(2,1)S(1)}, bf16[128,256]{1,0:T(8,128)(2,1)S(1)}, u32[]{:S(2)}, u32[]{:S(2)}) collective-permute-start(bf16[128,256]{1,0:T(8,128)(2,1)S(1)} %shard_map.92.gq_ref.refs_0_), channel_id=1, source_target_pairs={{0,2},{1,3},{2,0},{3,1},{4,6},{5,7},{6,4},{7,5},{8,10},{9,11},{10,... | collective-permute-start | bytes 196616 | tf_op jit(solution)/shard_map/ppermute | solution.py:44
  82.1 9.5 %collective-permute-start.30 = (bf16[128,256]{1,0:T(8,128)(2,1)S(1)}, bf16[128,256]{1,0:T(8,128)(2,1)S(1)}, u32[]{:S(2)}, u32[]{:S(2)}) collective-permute-start(bf16[128,256]{1,0:T(8,128)(2,1)S(1)} %shard_map.92.gq_ref.refs_0_), channel_id=1, source_target_pairs={{0,3},{1,0},{2,1},{3,2},{4,7},{5,4},{6,5},{7,6},{8,11},{9,8},{10,9... | collective-permute-start | bytes 196616 | tf_op jit(solution)/shard_map/ppermute | solution.py:44
  82.8 8.1 %collective-permute-start.35 = (bf16[128,128]{1,0:T(8,128)(2,1)S(1)}, bf16[128,128]{1,0:T(8,128)(2,1)S(1)}, u32[]{:S(2)}, u32[]{:S(2)}) collective-permute-start(bf16[128,128]{1,0:T(8,128)(2,1)S(1)} %get-tuple-element.123), channel_id=1, source_target_pairs={{12,0},{16,4},{20,8},{24,12},{28,16},{13,1},{17,5},{21,9},{25,13},... | collective-permute-start | bytes 98312 | tf_op jit(solution)/shard_map/ppermute | solution.py:37
  84.1 7.6 %collective-permute-start.36 = (bf16[128,128]{1,0:T(8,128)(2,1)S(1)}, bf16[128,128]{1,0:T(8,128)(2,1)S(1)}, u32[]{:S(2)}, u32[]{:S(2)}) collective-permute-start(bf16[128,128]{1,0:T(8,128)(2,1)S(1)} %get-tuple-element.124), channel_id=1, source_target_pairs={{16,0},{20,4},{24,8},{28,12},{17,1},{21,5},{25,9},{29,13},{18,2},{... | collective-permute-start | bytes 98312 | tf_op jit(solution)/shard_map/ppermute | solution.py:37
  91.7 5.5 %copy-start = (bf16[128,2048]{1,0:T(8,128)(2,1)S(1)}, bf16[128,2048]{1,0:T(8,128)(2,1)}, u32[]{:S(2)}) copy-start(bf16[128,2048]{1,0:T(8,128)(2,1)} %refs_14_.1) | copy-start | bytes 1572868
  91.7 5.5 %copy-start.1 = (bf16[128,2048]{1,0:T(8,128)(2,1)S(1)}, bf16[128,2048]{1,0:T(8,128)(2,1)}, u32[]{:S(2)}) copy-start(bf16[128,2048]{1,0:T(8,128)(2,1)} %up_ref.3) | copy-start | bytes 1572868
  91.7 5.5 %copy-start.2 = (f32[2048]{0:T(1024)S(1)}, f32[2048]{0:T(1024)}, u32[]{:S(2)}) copy-start(f32[2048]{0:T(1024)} %param.10) | copy-start | bytes 24580
  91.8 2.9 %collective-permute-start.39 = (bf16[144,128]{1,0:T(8,128)(2,1)S(1)}, bf16[144,128]{1,0:T(8,128)(2,1)S(1)}, u32[]{:S(2)}, u32[]{:S(2)}) collective-permute-start(bf16[144,128]{1,0:T(8,128)(2,1)S(1)} %shard_map.93.refs_4_), channel_id=1, source_target_pairs={{0,1},{1,2},{2,3},{3,0},{4,5},{5,6},{6,7},{7,4},{8,9},{9,10},{10,1... | collective-permute-start | bytes 110600 | tf_op jit(solution)/shard_map/ppermute | solution.py:44
  92.7 3.7 %collective-permute-start.38 = (bf16[144,128]{1,0:T(8,128)(2,1)S(1)}, bf16[144,128]{1,0:T(8,128)(2,1)S(1)}, u32[]{:S(2)}, u32[]{:S(2)}) collective-permute-start(bf16[144,128]{1,0:T(8,128)(2,1)S(1)} %shard_map.93.refs_4_), channel_id=1, source_target_pairs={{0,2},{1,3},{2,0},{3,1},{4,6},{5,7},{6,4},{7,5},{8,10},{9,11},{10,... | collective-permute-start | bytes 110600 | tf_op jit(solution)/shard_map/ppermute | solution.py:44
  94.2 2.9 %collective-permute-start.37 = (bf16[144,128]{1,0:T(8,128)(2,1)S(1)}, bf16[144,128]{1,0:T(8,128)(2,1)S(1)}, u32[]{:S(2)}, u32[]{:S(2)}) collective-permute-start(bf16[144,128]{1,0:T(8,128)(2,1)S(1)} %shard_map.93.refs_4_), channel_id=1, source_target_pairs={{0,3},{1,0},{2,1},{3,2},{4,7},{5,4},{6,5},{7,6},{8,11},{9,8},{10,9... | collective-permute-start | bytes 110600 | tf_op jit(solution)/shard_map/ppermute | solution.py:44
  114.2 4.9 %collective-permute-start.42 = (bf16[128,512]{1,0:T(8,128)(2,1)S(1)}, bf16[128,512]{1,0:T(8,128)(2,1)S(1)}, u32[]{:S(2)}, u32[]{:S(2)}) collective-permute-start(bf16[128,512]{1,0:T(8,128)(2,1)S(1)} %shard_map.95.refs_0_), channel_id=1, source_target_pairs={{0,1},{1,2},{2,3},{3,0},{4,5},{5,6},{6,7},{7,4},{8,9},{9,10},{10,1... | collective-permute-start | bytes 393224 | tf_op jit(solution)/shard_map/ppermute | solution.py:44
  114.7 10.8 %collective-permute-start.41 = (bf16[128,512]{1,0:T(8,128)(2,1)S(1)}, bf16[128,512]{1,0:T(8,128)(2,1)S(1)}, u32[]{:S(2)}, u32[]{:S(2)}) collective-permute-start(bf16[128,512]{1,0:T(8,128)(2,1)S(1)} %shard_map.95.refs_0_), channel_id=1, source_target_pairs={{0,2},{1,3},{2,0},{3,1},{4,6},{5,7},{6,4},{7,5},{8,10},{9,11},{10,... | collective-permute-start | bytes 393224 | tf_op jit(solution)/shard_map/ppermute | solution.py:44
  117.0 12.3 %collective-permute-start.40 = (bf16[128,512]{1,0:T(8,128)(2,1)S(1)}, bf16[128,512]{1,0:T(8,128)(2,1)S(1)}, u32[]{:S(2)}, u32[]{:S(2)}) collective-permute-start(bf16[128,512]{1,0:T(8,128)(2,1)S(1)} %shard_map.95.refs_0_), channel_id=1, source_target_pairs={{0,3},{1,0},{2,1},{3,2},{4,7},{5,4},{6,5},{7,6},{8,11},{9,8},{10,9... | collective-permute-start | bytes 393224 | tf_op jit(solution)/shard_map/ppermute | solution.py:44

commit v2 on v1

--- a/solution.py
+++ b/solution.py
@@ -131,29 +131,27 @@
 
 def start_body(heads, hidden_ref, inv_ref, qw_ref, ow_ref, up_ref, z_ref, ao_ref, gain_ref, ln_ref,
                qf_ref, qt_ref, go_ref, nt_ref, aot_ref, scaled_ref, norms_ref,
-               qw_tile, ow_tile, up_tile, z_tile, ao_tile, gain_tile, sems):
+               ow_tile, up_tile, z_tile, ao_tile, gain_tile, sems):
     copies = [
         pltpu.make_async_copy(source, target, sems.at[i])
         for i, (source, target) in enumerate(
-            ((ow_ref, ow_tile), (up_ref, up_tile), (z_ref, z_tile), (qw_ref, qw_tile),
-             (ao_ref, ao_tile), (gain_ref, gain_tile), (ln_ref, norms_ref))
+            ((ow_ref, ow_tile), (up_ref, up_tile), (z_ref, z_tile), (ao_ref, ao_tile),
+             (gain_ref, gain_tile), (ln_ref, norms_ref))
         )
     ]
     for copy in copies:
         copy.start()
-    for copy in copies[:3]:
-        copy.wait()
-    out = lax.dot_general(up_tile[...], ow_tile[...], NT, preferred_element_type=F32)
-    go_ref[...] = lanes_of(out.T, heads)
-    base = lax.dot_general(z_tile[...], ow_tile[...], NT, preferred_element_type=F32)
-    nt_ref[...] = lanes_of((base * inv_ref[:, :1]).T, heads)
-    copies[3].wait()
-    qf = jnp.dot(hidden_ref[...], qw_tile[...], preferred_element_type=F32)
+    qf = jnp.dot(hidden_ref[...], qw_ref[...], preferred_element_type=F32)
     qf_ref[...] = qf
     qt_ref[...] = lanes_of(qf.T, heads).astype(BF16)
-    for copy in copies[4:]:
+    for copy in copies:
         copy.wait()
-    scaled_ref[...] = (ow_tile[...].astype(F32) * gain_tile[...]).astype(BF16)
+    weight = ow_tile[...]
+    out = lax.dot_general(up_tile[...], weight, NT, preferred_element_type=F32)
+    go_ref[...] = lanes_of(out.T, heads)
+    base = lax.dot_general(z_tile[...], weight, NT, preferred_element_type=F32)
+    nt_ref[...] = lanes_of((base * inv_ref[:, :1]).T, heads)
+    scaled_ref[...] = (weight.astype(F32) * gain_tile[...]).astype(BF16)
     aot_ref[...] = lanes_of(ao_tile[...].astype(F32).T, heads)
 
 
@@ -425,20 +423,19 @@
         6 * rows * width * wide,
         4 * width * (2 * rows + wide),
         14,
-        in_specs=[vmem] * 2 + [hbm] * 7,
+        in_specs=[vmem] * 3 + [hbm] * 6,
         scratch_shapes=[
-            pltpu.VMEM((width, wide), BF16),
             pltpu.VMEM((wide, width), BF16),
             pltpu.VMEM((rows, width), BF16),
             pltpu.VMEM((rows, width), BF16),
             pltpu.VMEM((rows, wide), BF16),
             pltpu.VMEM((1, width), F32),
-            pltpu.SemaphoreType.DMA((7,)),
+            pltpu.SemaphoreType.DMA((6,)),
         ],
     )(
         hidden,
         inv,
-        pinned(query_weight),
+        query_weight,
         pinned(output_weight),
         pinned(upstream),
         pinned(fixed_point),

time: 131 us -> 131 us (level)
  starting transfers between devices: 62.8 us -> 64.2 us
where the time goes in v2:
time: 131 us
  starting transfers between devices  64.2 us (49%)
  waiting for transfers between devices  35.2 us (27%)
  Pallas kernels  15.8 us (12%)
  blocking collectives  14.9 us (11%)
    ppermute x16, starting transfers between devices, shifted(): lax.ppermute(value, axis, [(source, source + steps) for source in range(i...  32.7 us
    ppermute x21, starting transfers between devices, rotated(): lax.ppermute(value, axis, [(i, (i - step) % count) for i in range(count)])  26 us
    ppermute x21, waiting for transfers between devices, rotated(): lax.ppermute(value, axis, [(i, (i - step) % count) for i in range(count)])  23.3 us
    all_to_all x1, blocking collectives, shards(): totals = lax.all_to_all(totals, ('seq', 'head'), 0, 0)  14.9 us
    ppermute x16, waiting for transfers between devices, shifted(): lax.ppermute(value, axis, [(source, source + steps) for source in range(i...  11.8 us
    pallas_call x2, Pallas kernels, shards(): local_call(functools.partial(next_body, heads, parts, scale, step == 1),...  3.82 us
    ppermute x3, starting transfers between devices, doubled(): near.append(lax.ppermute(near[0], axis, pairs))  2.72 us
    pallas_call x1, Pallas kernels, shards(): local_call(functools.partial(start_body, heads), [shape_of((rows, wide),...  2.67 us
  transfers between devices with their start and end apart: 43, of which 18 were waited for; matrix products, arithmetic and copies ran while one was open for 0% of the time, Pallas kernels for 7%

profile of v2, /device:TPU:9, one launch (start us, length us, event | category | flops | bytes accessed | tf_op | source)
XLA Modules:
  0.0 130.9 jit_solution(6676256867792390073)
XLA Ops:
  0.0 2.2 %shard_map.82 = (bf16[48,2048]{1,0:T(8,128)(2,1)S(1)}, bf16[128,2048]{1,0:T(8,128)(2,1)S(1)}, bf16[128,128]{1,0:T(8,128)(2,1)S(1)}, f32[128,128]{1,0:T(8,128)S(1)}, f32[128,128]{1,0:T(8,128)S(1)}) custom-call(s32[1]{0:T(128)} %bitcast.2.block_ref, bf16[2048,256]{1,0:T(8,128)(2,1)} %qw_ref.3, bf16[2048,128]{1,0:T(8,128)(2,1)} %kvw_ref.1, ...), custom_call_target="tpu_custom_call" | custom-call | flops 75497472 | bytes 1572864 | tf_op jit(solution)/shard_map/pallas_call | solution.py:382
  2.2 1.4 %collective-permute-start.6 = (bf16[48,2048]{1,0:T(8,128)(2,1)S(1)}, bf16[48,2048]{1,0:T(8,128)(2,1)S(1)}, u32[]{:S(2)}, u32[]{:S(2)}) collective-permute-start(bf16[48,2048]{1,0:T(8,128)(2,1)S(1)} %get-tuple-element.87), channel_id=1, source_target_pairs={{0,1},{1,2},{2,3},{3,0},{4,5},{5,6},{6,7},{7,4},{8,9},{9,10},{10,1... | collective-permute-start | bytes 589832 | tf_op jit(solution)/shard_map/ppermute | solution.py:44
  3.5 1.1 collective-permute-start.5
  4.6 1.4 %collective-permute-start.4 = (bf16[48,2048]{1,0:T(8,128)(2,1)S(1)}, bf16[48,2048]{1,0:T(8,128)(2,1)S(1)}, u32[]{:S(2)}, u32[]{:S(2)}) collective-permute-start(bf16[48,2048]{1,0:T(8,128)(2,1)S(1)} %get-tuple-element.87), channel_id=1, source_target_pairs={{0,3},{1,0},{2,1},{3,2},{4,7},{5,4},{6,5},{7,6},{8,11},{9,8},{10,9... | collective-permute-start | bytes 589832 | tf_op jit(solution)/shard_map/ppermute | solution.py:44
  6.0 4.5 %collective-permute-start.3 = (bf16[128,128]{1,0:T(8,128)(2,1)S(1)}, bf16[128,128]{1,0:T(8,128)(2,1)S(1)}, u32[]{:S(2)}, u32[]{:S(2)}) collective-permute-start(bf16[128,128]{1,0:T(8,128)(2,1)S(1)} %get-tuple-element.71.refs_4_), channel_id=1, source_target_pairs={{0,4},{4,8},{8,12},{12,16},{16,20},{20,24},{24,28},{1,5},{5,9},{9,... | collective-permute-start | bytes 98312 | tf_op jit(solution)/shard_map/ppermute | solution.py:37
  10.5 3.1 %collective-permute-start.2 = (bf16[128,128]{1,0:T(8,128)(2,1)S(1)}, bf16[128,128]{1,0:T(8,128)(2,1)S(1)}, u32[]{:S(2)}, u32[]{:S(2)}) collective-permute-start(bf16[128,128]{1,0:T(8,128)(2,1)S(1)} %get-tuple-element.71.refs_4_), channel_id=1, source_target_pairs={{0,8},{4,12},{8,16},{12,20},{16,24},{20,28},{1,9},{5,13},{9,17},{1... | collective-permute-start | bytes 98312 | tf_op jit(solution)/shard_map/ppermute | solution.py:37
  13.6 3.0 %collective-permute-start.1 = (bf16[128,128]{1,0:T(8,128)(2,1)S(1)}, bf16[128,128]{1,0:T(8,128)(2,1)S(1)}, u32[]{:S(2)}, u32[]{:S(2)}) collective-permute-start(bf16[128,128]{1,0:T(8,128)(2,1)S(1)} %get-tuple-element.71.refs_4_), channel_id=1, source_target_pairs={{0,12},{4,16},{8,20},{12,24},{16,28},{1,13},{5,17},{9,21},{13,25},... | collective-permute-start | bytes 98312 | tf_op jit(solution)/shard_map/ppermute | solution.py:37
  16.7 2.5 %collective-permute-start = (bf16[128,128]{1,0:T(8,128)(2,1)S(1)}, bf16[128,128]{1,0:T(8,128)(2,1)S(1)}, u32[]{:S(2)}, u32[]{:S(2)}) collective-permute-start(bf16[128,128]{1,0:T(8,128)(2,1)S(1)} %get-tuple-element.71.refs_4_), channel_id=1, source_target_pairs={{0,16},{4,20},{8,24},{12,28},{1,17},{5,21},{9,25},{13,29},{2,18},{... | collective-permute-start | bytes 98312 | tf_op jit(solution)/shard_map/ppermute | solution.py:37
  19.2 2.7 %shard_map.83 = (f32[128,256]{1,0:T(8,128)S(1)}, bf16[64,512]{1,0:T(8,128)(2,1)S(1)}, f32[64,512]{1,0:T(8,128)S(1)}, f32[64,512]{1,0:T(8,128)S(1)}, f32[64,512]{...) custom-call(bf16[128,2048]{1,0:T(8,128)(2,1)S(1)} %get-tuple-element.72.hidden_ref, ...), custom_call_target="tpu_custom_call" | custom-call | flops 402653184 | bytes 4194304 | tf_op jit(solution)/shard_map/pallas_call | solution.py:412
  21.9 1.1 shard_map.84
  24.5 2.8 %collective-permute-start.7 = (bf16[128,128]{1,0:T(8,128)(2,1)S(1)}, bf16[128,128]{1,0:T(8,128)(2,1)S(1)}, u32[]{:S(2)}, u32[]{:S(2)}) collective-permute-start(bf16[128,128]{1,0:T(8,128)(2,1)S(1)} %get-tuple-element.90), channel_id=1, source_target_pairs={{4,0},{8,4},{12,8},{16,12},{20,16},{24,20},{28,24},{5,1},{9,5},{13... | collective-permute-start | bytes 98312 | tf_op jit(solution)/shard_map/ppermute | solution.py:37
  27.2 1.3 collective-permute-start.8
  28.5 1.3 collective-permute-start.9
  29.8 1.3 collective-permute-start.10
  32.2 2.9 %collective-permute-done.9.refs_2_ = bf16[128,128]{1,0:T(8,128)(2,1)S(1)} collective-permute-done((bf16[128,128]{1,0:T(8,128)(2,1)S(1)}, bf16[128,128]{1,0:T(8,128)(2,1)S(1)}, u32[]{:S(2)}, u32[]{:S(2)}) %collective-permute-start.9) | collective-permute-done | bytes 32800 | tf_op jit(solution)/shard_map/ppermute | solution.py:37
  36.0 1.8 %collective-permute-start.15 = (bf16[2,4,48,256]{3,2,1,0:T(8,128)(2,1)S(1)}, bf16[2,4,48,256]{3,2,1,0:T(8,128)(2,1)S(1)}, u32[]{:S(2)}, u32[]{:S(2)}) collective-permute-start(bf16[2,4,48,256]{3,2,1,0:T(8,128)(2,1)S(1)} %constant_dynamic-update-slice_fusion), channel_id=1, source_target_pairs={{0,8},{4,12},{8,0},{12,4},{16,24},{20,28},{24,16},{28,20},{1,9},{5... | collective-permute-start | bytes 589832 | tf_op jit(solution)/shard_map/ppermute | solution.py:58
  37.8 1.1 collective-permute-start.12
  39.3 3.1 %collective-permute-start.13 = (bf16[144,384]{1,0:T(8,128)(2,1)S(1)}, bf16[144,384]{1,0:T(8,128)(2,1)S(1)}, u32[]{:S(2)}, u32[]{:S(2)}) collective-permute-start(bf16[144,384]{1,0:T(8,128)(2,1)S(1)} %shard_map.87.refs_0_), channel_id=1, source_target_pairs={{0,2},{1,3},{2,0},{3,1},{4,6},{5,7},{6,4},{7,5},{8,10},{9,11},{10,... | collective-permute-start | bytes 331784 | tf_op jit(solution)/shard_map/ppermute | solution.py:44
  42.5 1.4 %collective-permute-start.16 = (bf16[4,4,48,256]{3,2,1,0:T(8,128)(2,1)S(1)}, bf16[4,4,48,256]{3,2,1,0:T(8,128)(2,1)S(1)}, u32[]{:S(2)}, u32[]{:S(2)}) collective-permute-start(bf16[4,4,48,256]{3,2,1,0:T(8,128)(2,1)S(1)} %constant_dynamic-update-slice_fusion.2.refs_10_), channel_id=1, source_target_pairs={{0,4},{4,0},{8,12},{12,8},{16,20},{20,16},{24,28},{28,24},{1,5},{5... | collective-permute-start | bytes 1179656 | tf_op jit(solution)/shard_map/ppermute | solution.py:57
  43.9 1.6 %collective-permute-done.14.refs_3_ = bf16[144,384]{1,0:T(8,128)(2,1)S(1)} collective-permute-done((bf16[144,384]{1,0:T(8,128)(2,1)S(1)}, bf16[144,384]{1,0:T(8,128)(2,1)S(1)}, u32[]{:S(2)}, u32[]{:S(2)}) %collective-permute-start.14) | collective-permute-done | bytes 110624 | tf_op jit(solution)/shard_map/ppermute | solution.py:44
  45.5 2.9 %collective-permute-done.13.refs_2_ = bf16[144,384]{1,0:T(8,128)(2,1)S(1)} collective-permute-done((bf16[144,384]{1,0:T(8,128)(2,1)S(1)}, bf16[144,384]{1,0:T(8,128)(2,1)S(1)}, u32[]{:S(2)}, u32[]{:S(2)}) %collective-permute-start.13) | collective-permute-done | bytes 110624 | tf_op jit(solution)/shard_map/ppermute | solution.py:44
  49.4 1.9 %shard_map.88 = (bf16[640,512]{1,0:T(8,128)(2,1)S(1)}, f32[128,128]{1,0:T(8,128)S(1)}, bf16[4,128,384]{2,1,0:T(8,128)(2,1)S(1)}, f32[16,128]{1,0:T(8,128)S(1)}, ...) custom-call(s32[2]{0:T(128)S(1)} %pad_add_fusion.spot_ref, ...), custom_call_target="tpu_custom_call" | custom-call | flops 226492416 | bytes 1441792 | tf_op jit(solution)/shard_map/pallas_call | solution.py:495
  51.3 3.3 %collective-permute-start.20 = (bf16[128,128]{1,0:T(8,128)(2,1)S(1)}, bf16[128,128]{1,0:T(8,128)(2,1)S(1)}, u32[]{:S(2)}, u32[]{:S(2)}) collective-permute-start(bf16[128,128]{1,0:T(8,128)(2,1)S(1)} %get-tuple-element.108), channel_id=1, source_target_pairs={{4,0},{8,4},{12,8},{16,12},{20,16},{24,20},{28,24},{5,1},{9,5},{13... | collective-permute-start | bytes 98312 | tf_op jit(solution)/shard_map/ppermute | solution.py:37
  54.6 1.3 collective-permute-start.21
  55.9 1.3 collective-permute-start.22
  57.2 1.3 collective-permute-start.23
  58.8 1.2 collective-permute-done.20.refs_0_
  60.7 3.3 %collective-permute-start.18 = (bf16[128,256]{1,0:T(8,128)(2,1)S(1)}, bf16[128,256]{1,0:T(8,128)(2,1)S(1)}, u32[]{:S(2)}, u32[]{:S(2)}) collective-permute-start(bf16[128,256]{1,0:T(8,128)(2,1)S(1)} %shard_map.89.gq_ref.refs_0_), channel_id=1, source_target_pairs={{0,2},{1,3},{2,0},{3,1},{4,6},{5,7},{6,4},{7,5},{8,10},{9,11},{10,... | collective-permute-start | bytes 196616 | tf_op jit(solution)/shard_map/ppermute | solution.py:44
  65.6 3.2 %collective-permute-start.25 = (bf16[144,128]{1,0:T(8,128)(2,1)S(1)}, bf16[144,128]{1,0:T(8,128)(2,1)S(1)}, u32[]{:S(2)}, u32[]{:S(2)}) collective-permute-start(bf16[144,128]{1,0:T(8,128)(2,1)S(1)} %shard_map.90.refs_4_), channel_id=1, source_target_pairs={{0,2},{1,3},{2,0},{3,1},{4,6},{5,7},{6,4},{7,5},{8,10},{9,11},{10,... | collective-permute-start | bytes 110600 | tf_op jit(solution)/shard_map/ppermute | solution.py:44
  69.7 1.9 %collective-permute-done.25.refs_6_ = bf16[144,128]{1,0:T(8,128)(2,1)S(1)} collective-permute-done((bf16[144,128]{1,0:T(8,128)(2,1)S(1)}, bf16[144,128]{1,0:T(8,128)(2,1)S(1)}, u32[]{:S(2)}, u32[]{:S(2)}) %collective-permute-start.25) | collective-permute-done | bytes 36896 | tf_op jit(solution)/shard_map/ppermute | solution.py:44
  71.7 0.9 collective-permute-done.24.refs_5_
  73.4 1.9 %shard_map.91 = (bf16[640,512]{1,0:T(8,128)(2,1)S(1)}, f32[128,128]{1,0:T(8,128)S(1)}, bf16[4,128,384]{2,1,0:T(8,128)(2,1)S(1)}, f32[16,128]{1,0:T(8,128)S(1)}, ...) custom-call(s32[2]{0:T(128)S(1)} %pad_add_fusion.spot_ref, ...), custom_call_target="tpu_custom_call" | custom-call | flops 226492416 | bytes 1441792 | tf_op jit(solution)/shard_map/pallas_call | solution.py:495
  75.3 1.9 %collective-permute-start.33 = (bf16[128,128]{1,0:T(8,128)(2,1)S(1)}, bf16[128,128]{1,0:T(8,128)(2,1)S(1)}, u32[]{:S(2)}, u32[]{:S(2)}) collective-permute-start(bf16[128,128]{1,0:T(8,128)(2,1)S(1)} %get-tuple-element.121), channel_id=1, source_target_pairs={{4,0},{8,4},{12,8},{16,12},{20,16},{24,20},{28,24},{5,1},{9,5},{13... | collective-permute-start | bytes 98312 | tf_op jit(solution)/shard_map/ppermute | solution.py:37
  77.2 1.3 collective-permute-start.34
  78.9 2.7 %collective-permute-start.31 = (bf16[128,256]{1,0:T(8,128)(2,1)S(1)}, bf16[128,256]{1,0:T(8,128)(2,1)S(1)}, u32[]{:S(2)}, u32[]{:S(2)}) collective-permute-start(bf16[128,256]{1,0:T(8,128)(2,1)S(1)} %shard_map.92.gq_ref.refs_0_), channel_id=1, source_target_pairs={{0,2},{1,3},{2,0},{3,1},{4,6},{5,7},{6,4},{7,5},{8,10},{9,11},{10,... | collective-permute-start | bytes 196616 | tf_op jit(solution)/shard_map/ppermute | solution.py:44
  82.3 1.3 collective-permute-start.35
  83.6 1.3 collective-permute-start.36
  84.9 5.5 %collective-permute-done.35.refs_2_ = bf16[128,128]{1,0:T(8,128)(2,1)S(1)} collective-permute-done((bf16[128,128]{1,0:T(8,128)(2,1)S(1)}, bf16[128,128]{1,0:T(8,128)(2,1)S(1)}, u32[]{:S(2)}, u32[]{:S(2)}) %collective-permute-start.35) | collective-permute-done | bytes 32800 | tf_op jit(solution)/shard_map/ppermute | solution.py:37
  91.4 1.0 collective-permute-start.39
  92.4 1.5 %collective-permute-start.38 = (bf16[144,128]{1,0:T(8,128)(2,1)S(1)}, bf16[144,128]{1,0:T(8,128)(2,1)S(1)}, u32[]{:S(2)}, u32[]{:S(2)}) collective-permute-start(bf16[144,128]{1,0:T(8,128)(2,1)S(1)} %shard_map.93.refs_4_), channel_id=1, source_target_pairs={{0,2},{1,3},{2,0},{3,1},{4,6},{5,7},{6,4},{7,5},{8,10},{9,11},{10,... | collective-permute-start | bytes 110600 | tf_op jit(solution)/shard_map/ppermute | solution.py:44
  94.3 1.9 %collective-permute-done.38.refs_6_ = bf16[144,128]{1,0:T(8,128)(2,1)S(1)} collective-permute-done((bf16[144,128]{1,0:T(8,128)(2,1)S(1)}, bf16[144,128]{1,0:T(8,128)(2,1)S(1)}, u32[]{:S(2)}, u32[]{:S(2)}) %collective-permute-start.38) | collective-permute-done | bytes 36896 | tf_op jit(solution)/shard_map/ppermute | solution.py:44
  96.8 1.9 %shard_map.94 = (f32[3,128,512]{2,1,0:T(8,128)S(1)}, f32[32,8,128]{2,1,0:T(8,128)S(1)}) custom-call(s32[2]{0:T(128)S(1)} %pad_add_fusion.spot_ref, bf16[128,256]{1,0:T(8,128)(2,1)S(1)} %shard_map.92.gq_ref.refs_0_, bf16[128,256]{1,0:T(8,128)(2,1)S(1)} %collective-permute-done.30.refs_1_, bf16[128,256]{1,0:T(8,128)(2,1)S(1)} %collective-permute-done.31.refs_2_, ...), custom_call_target="tpu_custom_call" | custom-call | flops 603979776 | bytes 1572864 | tf_op jit(solution)/shard_map/pallas_call | solution.py:534
  98.6 14.9 %all_to_all.5.tot_ref = f32[32,8,128]{2,1,0:T(8,128)S(1)} all-to-all(f32[32,8,128]{2,1,0:T(8,128)S(1)} %get-tuple-element.135), channel_id=1, replica_groups=mesh['seq'=8,'head'=4] {'seq','head'}, dimensions={0} | all-to-all | bytes 262144 | tf_op jit(solution)/shard_map/all_to_all | solution.py:550
  114.8 2.2 %collective-permute-start.41 = (bf16[128,512]{1,0:T(8,128)(2,1)S(1)}, bf16[128,512]{1,0:T(8,128)(2,1)S(1)}, u32[]{:S(2)}, u32[]{:S(2)}) collective-permute-start(bf16[128,512]{1,0:T(8,128)(2,1)S(1)} %shard_map.95.refs_0_), channel_id=1, source_target_pairs={{0,2},{1,3},{2,0},{3,1},{4,6},{5,7},{6,4},{7,5},{8,10},{9,11},{10,... | collective-permute-start | bytes 393224 | tf_op jit(solution)/shard_map/ppermute | solution.py:44
  117.1 2.2 %collective-permute-done.42.refs_3_ = bf16[128,512]{1,0:T(8,128)(2,1)S(1)} collective-permute-done((bf16[128,512]{1,0:T(8,128)(2,1)S(1)}, bf16[128,512]{1,0:T(8,128)(2,1)S(1)}, u32[]{:S(2)}, u32[]{:S(2)}) %collective-permute-start.42) | collective-permute-done | bytes 131104 | tf_op jit(solution)/shard_map/ppermute | solution.py:44
  119.2 6.4 %collective-permute-done.41.refs_2_ = bf16[128,512]{1,0:T(8,128)(2,1)S(1)} collective-permute-done((bf16[128,512]{1,0:T(8,128)(2,1)S(1)}, bf16[128,512]{1,0:T(8,128)(2,1)S(1)}, u32[]{:S(2)}, u32[]{:S(2)}) %collective-permute-start.41) | collective-permute-done | bytes 131104 | tf_op jit(solution)/shard_map/ppermute | solution.py:44
  125.7 3.7 %collective-permute-done.40.refs_1_ = bf16[128,512]{1,0:T(8,128)(2,1)S(1)} collective-permute-done((bf16[128,512]{1,0:T(8,128)(2,1)S(1)}, bf16[128,512]{1,0:T(8,128)(2,1)S(1)}, u32[]{:S(2)}, u32[]{:S(2)}) %collective-permute-start.40) | collective-permute-done | bytes 131104 | tf_op jit(solution)/shard_map/ppermute | solution.py:44
  129.3 1.6 %shard_map.96 = f32[128,2048]{1,0:T(8,128)} custom-call(s32[2]{0:T(128)S(1)} %pad_add_fusion.spot_ref, bf16[128,512]{1,0:T(8,128)(2,1)S(1)} %shard_map.95.refs_0_, bf16[128,512]{1,0:T(8,128)(2,1)S(1)} %collective-permute-done.40.refs_1_, bf16[128,512]{1,0:T(8,128)(2,1)S(1)} %collective-permute-done.41.refs_2_, ...), custom_call_target="tpu_custom_call" | custom-call | bytes 1572864 | tf_op jit(solution)/shard_map/pallas_call | solution.py:562
  (73 shorter events, 13.4 us)
Async XLA Ops:
  0.0 19.2 %copy-start.2 = (bf16[2048,256]{1,0:T(8,128)(2,1)S(1)}, bf16[2048,256]{1,0:T(8,128)(2,1)}, u32[]{:S(2)}) copy-start(bf16[2048,256]{1,0:T(8,128)(2,1)} %qw_ref.3) | copy-start | bytes 3145732
  2.2 20.9 %collective-permute-start.6 = (bf16[48,2048]{1,0:T(8,128)(2,1)S(1)}, bf16[48,2048]{1,0:T(8,128)(2,1)S(1)}, u32[]{:S(2)}, u32[]{:S(2)}) collective-permute-start(bf16[48,2048]{1,0:T(8,128)(2,1)S(1)} %get-tuple-element.87), channel_id=1, source_target_pairs={{0,1},{1,2},{2,3},{3,0},{4,5},{5,6},{6,7},{7,4},{8,9},{9,10},{10,1... | collective-permute-start | bytes 589832 | tf_op jit(solution)/shard_map/ppermute | solution.py:44
  3.5 19.6 %collective-permute-start.5 = (bf16[48,2048]{1,0:T(8,128)(2,1)S(1)}, bf16[48,2048]{1,0:T(8,128)(2,1)S(1)}, u32[]{:S(2)}, u32[]{:S(2)}) collective-permute-start(bf16[48,2048]{1,0:T(8,128)(2,1)S(1)} %get-tuple-element.87), channel_id=1, source_target_pairs={{0,2},{1,3},{2,0},{3,1},{4,6},{5,7},{6,4},{7,5},{8,10},{9,11},{10,... | collective-permute-start | bytes 589832 | tf_op jit(solution)/shard_map/ppermute | solution.py:44
  4.6 18.5 %collective-permute-start.4 = (bf16[48,2048]{1,0:T(8,128)(2,1)S(1)}, bf16[48,2048]{1,0:T(8,128)(2,1)S(1)}, u32[]{:S(2)}, u32[]{:S(2)}) collective-permute-start(bf16[48,2048]{1,0:T(8,128)(2,1)S(1)} %get-tuple-element.87), channel_id=1, source_target_pairs={{0,3},{1,0},{2,1},{3,2},{4,7},{5,4},{6,5},{7,6},{8,11},{9,8},{10,9... | collective-permute-start | bytes 589832 | tf_op jit(solution)/shard_map/ppermute | solution.py:44
  6.0 7.6 %collective-permute-start.3 = (bf16[128,128]{1,0:T(8,128)(2,1)S(1)}, bf16[128,128]{1,0:T(8,128)(2,1)S(1)}, u32[]{:S(2)}, u32[]{:S(2)}) collective-permute-start(bf16[128,128]{1,0:T(8,128)(2,1)S(1)} %get-tuple-element.71.refs_4_), channel_id=1, source_target_pairs={{0,4},{4,8},{8,12},{12,16},{16,20},{20,24},{24,28},{1,5},{5,9},{9,... | collective-permute-start | bytes 98312 | tf_op jit(solution)/shard_map/ppermute | solution.py:37
  10.5 6.1 %collective-permute-start.2 = (bf16[128,128]{1,0:T(8,128)(2,1)S(1)}, bf16[128,128]{1,0:T(8,128)(2,1)S(1)}, u32[]{:S(2)}, u32[]{:S(2)}) collective-permute-start(bf16[128,128]{1,0:T(8,128)(2,1)S(1)} %get-tuple-element.71.refs_4_), channel_id=1, source_target_pairs={{0,8},{4,12},{8,16},{12,20},{16,24},{20,28},{1,9},{5,13},{9,17},{1... | collective-permute-start | bytes 98312 | tf_op jit(solution)/shard_map/ppermute | solution.py:37
  13.6 8.3 %collective-permute-start.1 = (bf16[128,128]{1,0:T(8,128)(2,1)S(1)}, bf16[128,128]{1,0:T(8,128)(2,1)S(1)}, u32[]{:S(2)}, u32[]{:S(2)}) collective-permute-start(bf16[128,128]{1,0:T(8,128)(2,1)S(1)} %get-tuple-element.71.refs_4_), channel_id=1, source_target_pairs={{0,12},{4,16},{8,20},{12,24},{16,28},{1,13},{5,17},{9,21},{13,25},... | collective-permute-start | bytes 98312 | tf_op jit(solution)/shard_map/ppermute | solution.py:37
  16.7 5.2 %collective-permute-start = (bf16[128,128]{1,0:T(8,128)(2,1)S(1)}, bf16[128,128]{1,0:T(8,128)(2,1)S(1)}, u32[]{:S(2)}, u32[]{:S(2)}) collective-permute-start(bf16[128,128]{1,0:T(8,128)(2,1)S(1)} %get-tuple-element.71.refs_4_), channel_id=1, source_target_pairs={{0,16},{4,20},{8,24},{12,28},{1,17},{5,21},{9,25},{13,29},{2,18},{... | collective-permute-start | bytes 98312 | tf_op jit(solution)/shard_map/ppermute | solution.py:37
  23.7 12.1 %collective-permute-start.11 = (bf16[1,4,48,256]{3,2,1,0:T(8,128)(2,1)S(1)}, bf16[1,4,48,256]{3,2,1,0:T(8,128)(2,1)S(1)}, u32[]{:S(2)}, u32[]{:S(2)}) collective-permute-start(bf16[1,4,48,256]{3,2,1,0:T(8,128)(2,1)S(1)} %bitcast.14), channel_id=1, source_target_pairs={{0,16},{4,20},{8,24},{12,28},{16,0},{20,4},{24,8},{28,12},{1,17},{... | collective-permute-start | bytes 294920 | tf_op jit(solution)/shard_map/ppermute | solution.py:522
  24.5 7.0 %collective-permute-start.7 = (bf16[128,128]{1,0:T(8,128)(2,1)S(1)}, bf16[128,128]{1,0:T(8,128)(2,1)S(1)}, u32[]{:S(2)}, u32[]{:S(2)}) collective-permute-start(bf16[128,128]{1,0:T(8,128)(2,1)S(1)} %get-tuple-element.90), channel_id=1, source_target_pairs={{4,0},{8,4},{12,8},{16,12},{20,16},{24,20},{28,24},{5,1},{9,5},{13... | collective-permute-start | bytes 98312 | tf_op jit(solution)/shard_map/ppermute | solution.py:37
  27.2 5.0 %collective-permute-start.8 = (bf16[128,128]{1,0:T(8,128)(2,1)S(1)}, bf16[128,128]{1,0:T(8,128)(2,1)S(1)}, u32[]{:S(2)}, u32[]{:S(2)}) collective-permute-start(bf16[128,128]{1,0:T(8,128)(2,1)S(1)} %get-tuple-element.91), channel_id=1, source_target_pairs={{8,0},{12,4},{16,8},{20,12},{24,16},{28,20},{9,1},{13,5},{17,9},{2... | collective-permute-start | bytes 98312 | tf_op jit(solution)/shard_map/ppermute | solution.py:37
  28.5 6.6 %collective-permute-start.9 = (bf16[128,128]{1,0:T(8,128)(2,1)S(1)}, bf16[128,128]{1,0:T(8,128)(2,1)S(1)}, u32[]{:S(2)}, u32[]{:S(2)}) collective-permute-start(bf16[128,128]{1,0:T(8,128)(2,1)S(1)} %get-tuple-element.92), channel_id=1, source_target_pairs={{12,0},{16,4},{20,8},{24,12},{28,16},{13,1},{17,5},{21,9},{25,13},... | collective-permute-start | bytes 98312 | tf_op jit(solution)/shard_map/ppermute | solution.py:37
  29.8 6.0 %collective-permute-start.10 = (bf16[128,128]{1,0:T(8,128)(2,1)S(1)}, bf16[128,128]{1,0:T(8,128)(2,1)S(1)}, u32[]{:S(2)}, u32[]{:S(2)}) collective-permute-start(bf16[128,128]{1,0:T(8,128)(2,1)S(1)} %get-tuple-element.93), channel_id=1, source_target_pairs={{16,0},{20,4},{24,8},{28,12},{17,1},{21,5},{25,9},{29,13},{18,2},{... | collective-permute-start | bytes 98312 | tf_op jit(solution)/shard_map/ppermute | solution.py:37
  36.0 6.5 %collective-permute-start.15 = (bf16[2,4,48,256]{3,2,1,0:T(8,128)(2,1)S(1)}, bf16[2,4,48,256]{3,2,1,0:T(8,128)(2,1)S(1)}, u32[]{:S(2)}, u32[]{:S(2)}) collective-permute-start(bf16[2,4,48,256]{3,2,1,0:T(8,128)(2,1)S(1)} %constant_dynamic-update-slice_fusion), channel_id=1, source_target_pairs={{0,8},{4,12},{8,0},{12,4},{16,24},{20,28},{24,16},{28,20},{1,9},{5... | collective-permute-start | bytes 589832 | tf_op jit(solution)/shard_map/ppermute | solution.py:58
  37.8 4.7 %collective-permute-start.12 = (bf16[144,384]{1,0:T(8,128)(2,1)S(1)}, bf16[144,384]{1,0:T(8,128)(2,1)S(1)}, u32[]{:S(2)}, u32[]{:S(2)}) collective-permute-start(bf16[144,384]{1,0:T(8,128)(2,1)S(1)} %shard_map.87.refs_0_), channel_id=1, source_target_pairs={{0,3},{1,0},{2,1},{3,2},{4,7},{5,4},{6,5},{7,6},{8,11},{9,8},{10,9... | collective-permute-start | bytes 331784 | tf_op jit(solution)/shard_map/ppermute | solution.py:44
  38.9 6.5 %collective-permute-start.14 = (bf16[144,384]{1,0:T(8,128)(2,1)S(1)}, bf16[144,384]{1,0:T(8,128)(2,1)S(1)}, u32[]{:S(2)}, u32[]{:S(2)}) collective-permute-start(bf16[144,384]{1,0:T(8,128)(2,1)S(1)} %shard_map.87.refs_0_), channel_id=1, source_target_pairs={{0,1},{1,2},{2,3},{3,0},{4,5},{5,6},{6,7},{7,4},{8,9},{9,10},{10,1... | collective-permute-start | bytes 331784 | tf_op jit(solution)/shard_map/ppermute | solution.py:44
  39.3 9.0 %collective-permute-start.13 = (bf16[144,384]{1,0:T(8,128)(2,1)S(1)}, bf16[144,384]{1,0:T(8,128)(2,1)S(1)}, u32[]{:S(2)}, u32[]{:S(2)}) collective-permute-start(bf16[144,384]{1,0:T(8,128)(2,1)S(1)} %shard_map.87.refs_0_), channel_id=1, source_target_pairs={{0,2},{1,3},{2,0},{3,1},{4,6},{5,7},{6,4},{7,5},{8,10},{9,11},{10,... | collective-permute-start | bytes 331784 | tf_op jit(solution)/shard_map/ppermute | solution.py:44
  42.5 5.8 %collective-permute-start.27 = (bf16[1,4,48,512]{3,2,1,0:T(8,128)(2,1)S(1)}, bf16[1,4,48,512]{3,2,1,0:T(8,128)(2,1)S(1)}, u32[]{:S(2)}, u32[]{:S(2)}) collective-permute-start(bf16[1,4,48,512]{3,2,1,0:T(8,128)(2,1)S(1)} %dynamic-slice_bitcast_fusion), channel_id=1, source_target_pairs={{0,16},{4,20},{8,24},{12,28},{16,0},{20,4},{24,8},{28,12},{1,17},{... | collective-permute-start | bytes 589832 | tf_op jit(solution)/shard_map/ppermute | solution.py:58
  42.5 6.8 %collective-permute-start.16 = (bf16[4,4,48,256]{3,2,1,0:T(8,128)(2,1)S(1)}, bf16[4,4,48,256]{3,2,1,0:T(8,128)(2,1)S(1)}, u32[]{:S(2)}, u32[]{:S(2)}) collective-permute-start(bf16[4,4,48,256]{3,2,1,0:T(8,128)(2,1)S(1)} %constant_dynamic-update-slice_fusion.2.refs_10_), channel_id=1, source_target_pairs={{0,4},{4,0},{8,12},{12,8},{16,20},{20,16},{24,28},{28,24},{1,5},{5... | collective-permute-start | bytes 1179656 | tf_op jit(solution)/shard_map/ppermute | solution.py:57
  48.4 17.2 %collective-permute-start.28 = (bf16[2,4,48,512]{3,2,1,0:T(8,128)(2,1)S(1)}, bf16[2,4,48,512]{3,2,1,0:T(8,128)(2,1)S(1)}, u32[]{:S(2)}, u32[]{:S(2)}) collective-permute-start(bf16[2,4,48,512]{3,2,1,0:T(8,128)(2,1)S(1)} %constant_dynamic-update-slice_fusion.4), channel_id=1, source_target_pairs={{0,8},{4,12},{8,0},{12,4},{16,24},{20,28},{24,16},{28,20},{1,9},{5... | collective-permute-start | bytes 1179656 | tf_op jit(solution)/shard_map/ppermute | solution.py:58
  51.3 8.7 %collective-permute-start.20 = (bf16[128,128]{1,0:T(8,128)(2,1)S(1)}, bf16[128,128]{1,0:T(8,128)(2,1)S(1)}, u32[]{:S(2)}, u32[]{:S(2)}) collective-permute-start(bf16[128,128]{1,0:T(8,128)(2,1)S(1)} %get-tuple-element.108), channel_id=1, source_target_pairs={{4,0},{8,4},{12,8},{16,12},{20,16},{24,20},{28,24},{5,1},{9,5},{13... | collective-permute-start | bytes 98312 | tf_op jit(solution)/shard_map/ppermute | solution.py:37
  54.6 6.1 %collective-permute-start.21 = (bf16[128,128]{1,0:T(8,128)(2,1)S(1)}, bf16[128,128]{1,0:T(8,128)(2,1)S(1)}, u32[]{:S(2)}, u32[]{:S(2)}) collective-permute-start(bf16[128,128]{1,0:T(8,128)(2,1)S(1)} %get-tuple-element.109), channel_id=1, source_target_pairs={{8,0},{12,4},{16,8},{20,12},{24,16},{28,20},{9,1},{13,5},{17,9},{2... | collective-permute-start | bytes 98312 | tf_op jit(solution)/shard_map/ppermute | solution.py:37
  55.9 8.1 %collective-permute-start.22 = (bf16[128,128]{1,0:T(8,128)(2,1)S(1)}, bf16[128,128]{1,0:T(8,128)(2,1)S(1)}, u32[]{:S(2)}, u32[]{:S(2)}) collective-permute-start(bf16[128,128]{1,0:T(8,128)(2,1)S(1)} %get-tuple-element.110), channel_id=1, source_target_pairs={{12,0},{16,4},{20,8},{24,12},{28,16},{13,1},{17,5},{21,9},{25,13},... | collective-permute-start | bytes 98312 | tf_op jit(solution)/shard_map/ppermute | solution.py:37
  57.2 7.5 %collective-permute-start.23 = (bf16[128,128]{1,0:T(8,128)(2,1)S(1)}, bf16[128,128]{1,0:T(8,128)(2,1)S(1)}, u32[]{:S(2)}, u32[]{:S(2)}) collective-permute-start(bf16[128,128]{1,0:T(8,128)(2,1)S(1)} %get-tuple-element.111), channel_id=1, source_target_pairs={{16,0},{20,4},{24,8},{28,12},{17,1},{21,5},{25,9},{29,13},{18,2},{... | collective-permute-start | bytes 98312 | tf_op jit(solution)/shard_map/ppermute | solution.py:37
  60.0 8.9 %collective-permute-start.19 = (bf16[128,256]{1,0:T(8,128)(2,1)S(1)}, bf16[128,256]{1,0:T(8,128)(2,1)S(1)}, u32[]{:S(2)}, u32[]{:S(2)}) collective-permute-start(bf16[128,256]{1,0:T(8,128)(2,1)S(1)} %shard_map.89.gq_ref.refs_0_), channel_id=1, source_target_pairs={{0,1},{1,2},{2,3},{3,0},{4,5},{5,6},{6,7},{7,4},{8,9},{9,10},{10,1... | collective-permute-start | bytes 196616 | tf_op jit(solution)/shard_map/ppermute | solution.py:44
  60.7 8.2 %collective-permute-start.18 = (bf16[128,256]{1,0:T(8,128)(2,1)S(1)}, bf16[128,256]{1,0:T(8,128)(2,1)S(1)}, u32[]{:S(2)}, u32[]{:S(2)}) collective-permute-start(bf16[128,256]{1,0:T(8,128)(2,1)S(1)} %shard_map.89.gq_ref.refs_0_), channel_id=1, source_target_pairs={{0,2},{1,3},{2,0},{3,1},{4,6},{5,7},{6,4},{7,5},{8,10},{9,11},{10,... | collective-permute-start | bytes 196616 | tf_op jit(solution)/shard_map/ppermute | solution.py:44
  64.0 5.2 %collective-permute-start.17 = (bf16[128,256]{1,0:T(8,128)(2,1)S(1)}, bf16[128,256]{1,0:T(8,128)(2,1)S(1)}, u32[]{:S(2)}, u32[]{:S(2)}) collective-permute-start(bf16[128,256]{1,0:T(8,128)(2,1)S(1)} %shard_map.89.gq_ref.refs_0_), channel_id=1, source_target_pairs={{0,3},{1,0},{2,1},{3,2},{4,7},{5,4},{6,5},{7,6},{8,11},{9,8},{10,9... | collective-permute-start | bytes 196616 | tf_op jit(solution)/shard_map/ppermute | solution.py:44
  64.8 4.9 %collective-permute-start.26 = (bf16[144,128]{1,0:T(8,128)(2,1)S(1)}, bf16[144,128]{1,0:T(8,128)(2,1)S(1)}, u32[]{:S(2)}, u32[]{:S(2)}) collective-permute-start(bf16[144,128]{1,0:T(8,128)(2,1)S(1)} %shard_map.90.refs_4_), channel_id=1, source_target_pairs={{0,1},{1,2},{2,3},{3,0},{4,5},{5,6},{6,7},{7,4},{8,9},{9,10},{10,1... | collective-permute-start | bytes 110600 | tf_op jit(solution)/shard_map/ppermute | solution.py:44
  65.6 6.1 %collective-permute-start.25 = (bf16[144,128]{1,0:T(8,128)(2,1)S(1)}, bf16[144,128]{1,0:T(8,128)(2,1)S(1)}, u32[]{:S(2)}, u32[]{:S(2)}) collective-permute-start(bf16[144,128]{1,0:T(8,128)(2,1)S(1)} %shard_map.90.refs_4_), channel_id=1, source_target_pairs={{0,2},{1,3},{2,0},{3,1},{4,6},{5,7},{6,4},{7,5},{8,10},{9,11},{10,... | collective-permute-start | bytes 110600 | tf_op jit(solution)/shard_map/ppermute | solution.py:44
  68.9 3.8 %collective-permute-start.24 = (bf16[144,128]{1,0:T(8,128)(2,1)S(1)}, bf16[144,128]{1,0:T(8,128)(2,1)S(1)}, u32[]{:S(2)}, u32[]{:S(2)}) collective-permute-start(bf16[144,128]{1,0:T(8,128)(2,1)S(1)} %shard_map.90.refs_4_), channel_id=1, source_target_pairs={{0,3},{1,0},{2,1},{3,2},{4,7},{5,4},{6,5},{7,6},{8,11},{9,8},{10,9... | collective-permute-start | bytes 110600 | tf_op jit(solution)/shard_map/ppermute | solution.py:44
  72.7 5.8 %collective-permute-start.29 = (bf16[4,4,48,512]{3,2,1,0:T(8,128)(2,1)S(1)}, bf16[4,4,48,512]{3,2,1,0:T(8,128)(2,1)S(1)}, u32[]{:S(2)}, u32[]{:S(2)}) collective-permute-start(bf16[4,4,48,512]{3,2,1,0:T(8,128)(2,1)S(1)} %constant_dynamic-update-slice_fusion.6.refs_12_), channel_id=1, source_target_pairs={{0,4},{4,0},{8,12},{12,8},{16,20},{20,16},{24,28},{28,24},{1,5},{5... | collective-permute-start | bytes 2359304 | tf_op jit(solution)/shard_map/ppermute | solution.py:57
  75.3 7.1 %collective-permute-start.33 = (bf16[128,128]{1,0:T(8,128)(2,1)S(1)}, bf16[128,128]{1,0:T(8,128)(2,1)S(1)}, u32[]{:S(2)}, u32[]{:S(2)}) collective-permute-start(bf16[128,128]{1,0:T(8,128)(2,1)S(1)} %get-tuple-element.121), channel_id=1, source_target_pairs={{4,0},{8,4},{12,8},{16,12},{20,16},{24,20},{28,24},{5,1},{9,5},{13... | collective-permute-start | bytes 98312 | tf_op jit(solution)/shard_map/ppermute | solution.py:37
  77.2 6.4 %collective-permute-start.34 = (bf16[128,128]{1,0:T(8,128)(2,1)S(1)}, bf16[128,128]{1,0:T(8,128)(2,1)S(1)}, u32[]{:S(2)}, u32[]{:S(2)}) collective-permute-start(bf16[128,128]{1,0:T(8,128)(2,1)S(1)} %get-tuple-element.122), channel_id=1, source_target_pairs={{8,0},{12,4},{16,8},{20,12},{24,16},{28,20},{9,1},{13,5},{17,9},{2... | collective-permute-start | bytes 98312 | tf_op jit(solution)/shard_map/ppermute | solution.py:37
  78.8 12.4 %collective-permute-start.32 = (bf16[128,256]{1,0:T(8,128)(2,1)S(1)}, bf16[128,256]{1,0:T(8,128)(2,1)S(1)}, u32[]{:S(2)}, u32[]{:S(2)}) collective-permute-start(bf16[128,256]{1,0:T(8,128)(2,1)S(1)} %shard_map.92.gq_ref.refs_0_), channel_id=1, source_target_pairs={{0,1},{1,2},{2,3},{3,0},{4,5},{5,6},{6,7},{7,4},{8,9},{9,10},{10,1... | collective-permute-start | bytes 196616 | tf_op jit(solution)/shard_map/ppermute | solution.py:44
  78.9 12.3 %collective-permute-start.31 = (bf16[128,256]{1,0:T(8,128)(2,1)S(1)}, bf16[128,256]{1,0:T(8,128)(2,1)S(1)}, u32[]{:S(2)}, u32[]{:S(2)}) collective-permute-start(bf16[128,256]{1,0:T(8,128)(2,1)S(1)} %shard_map.92.gq_ref.refs_0_), channel_id=1, source_target_pairs={{0,2},{1,3},{2,0},{3,1},{4,6},{5,7},{6,4},{7,5},{8,10},{9,11},{10,... | collective-permute-start | bytes 196616 | tf_op jit(solution)/shard_map/ppermute | solution.py:44
  81.6 9.6 %collective-permute-start.30 = (bf16[128,256]{1,0:T(8,128)(2,1)S(1)}, bf16[128,256]{1,0:T(8,128)(2,1)S(1)}, u32[]{:S(2)}, u32[]{:S(2)}) collective-permute-start(bf16[128,256]{1,0:T(8,128)(2,1)S(1)} %shard_map.92.gq_ref.refs_0_), channel_id=1, source_target_pairs={{0,3},{1,0},{2,1},{3,2},{4,7},{5,4},{6,5},{7,6},{8,11},{9,8},{10,9... | collective-permute-start | bytes 196616 | tf_op jit(solution)/shard_map/ppermute | solution.py:44
  82.3 8.1 %collective-permute-start.35 = (bf16[128,128]{1,0:T(8,128)(2,1)S(1)}, bf16[128,128]{1,0:T(8,128)(2,1)S(1)}, u32[]{:S(2)}, u32[]{:S(2)}) collective-permute-start(bf16[128,128]{1,0:T(8,128)(2,1)S(1)} %get-tuple-element.123), channel_id=1, source_target_pairs={{12,0},{16,4},{20,8},{24,12},{28,16},{13,1},{17,5},{21,9},{25,13},... | collective-permute-start | bytes 98312 | tf_op jit(solution)/shard_map/ppermute | solution.py:37
  83.6 7.6 %collective-permute-start.36 = (bf16[128,128]{1,0:T(8,128)(2,1)S(1)}, bf16[128,128]{1,0:T(8,128)(2,1)S(1)}, u32[]{:S(2)}, u32[]{:S(2)}) collective-permute-start(bf16[128,128]{1,0:T(8,128)(2,1)S(1)} %get-tuple-element.124), channel_id=1, source_target_pairs={{16,0},{20,4},{24,8},{28,12},{17,1},{21,5},{25,9},{29,13},{18,2},{... | collective-permute-start | bytes 98312 | tf_op jit(solution)/shard_map/ppermute | solution.py:37
  91.2 5.5 %copy-start = (bf16[128,2048]{1,0:T(8,128)(2,1)S(1)}, bf16[128,2048]{1,0:T(8,128)(2,1)}, u32[]{:S(2)}) copy-start(bf16[128,2048]{1,0:T(8,128)(2,1)} %refs_14_.1) | copy-start | bytes 1572868
  91.2 5.5 %copy-start.1 = (bf16[128,2048]{1,0:T(8,128)(2,1)S(1)}, bf16[128,2048]{1,0:T(8,128)(2,1)}, u32[]{:S(2)}) copy-start(bf16[128,2048]{1,0:T(8,128)(2,1)} %up_ref.3) | copy-start | bytes 1572868
  91.2 5.5 %copy-start.3 = (f32[2048]{0:T(1024)S(1)}, f32[2048]{0:T(1024)}, u32[]{:S(2)}) copy-start(f32[2048]{0:T(1024)} %param.10) | copy-start | bytes 24580
  91.4 2.9 %collective-permute-start.39 = (bf16[144,128]{1,0:T(8,128)(2,1)S(1)}, bf16[144,128]{1,0:T(8,128)(2,1)S(1)}, u32[]{:S(2)}, u32[]{:S(2)}) collective-permute-start(bf16[144,128]{1,0:T(8,128)(2,1)S(1)} %shard_map.93.refs_4_), channel_id=1, source_target_pairs={{0,1},{1,2},{2,3},{3,0},{4,5},{5,6},{6,7},{7,4},{8,9},{9,10},{10,1... | collective-permute-start | bytes 110600 | tf_op jit(solution)/shard_map/ppermute | solution.py:44
  92.4 3.7 %collective-permute-start.38 = (bf16[144,128]{1,0:T(8,128)(2,1)S(1)}, bf16[144,128]{1,0:T(8,128)(2,1)S(1)}, u32[]{:S(2)}, u32[]{:S(2)}) collective-permute-start(bf16[144,128]{1,0:T(8,128)(2,1)S(1)} %shard_map.93.refs_4_), channel_id=1, source_target_pairs={{0,2},{1,3},{2,0},{3,1},{4,6},{5,7},{6,4},{7,5},{8,10},{9,11},{10,... | collective-permute-start | bytes 110600 | tf_op jit(solution)/shard_map/ppermute | solution.py:44
  93.9 2.8 %collective-permute-start.37 = (bf16[144,128]{1,0:T(8,128)(2,1)S(1)}, bf16[144,128]{1,0:T(8,128)(2,1)S(1)}, u32[]{:S(2)}, u32[]{:S(2)}) collective-permute-start(bf16[144,128]{1,0:T(8,128)(2,1)S(1)} %shard_map.93.refs_4_), channel_id=1, source_target_pairs={{0,3},{1,0},{2,1},{3,2},{4,7},{5,4},{6,5},{7,6},{8,11},{9,8},{10,9... | collective-permute-start | bytes 110600 | tf_op jit(solution)/shard_map/ppermute | solution.py:44
  114.3 4.9 %collective-permute-start.42 = (bf16[128,512]{1,0:T(8,128)(2,1)S(1)}, bf16[128,512]{1,0:T(8,128)(2,1)S(1)}, u32[]{:S(2)}, u32[]{:S(2)}) collective-permute-start(bf16[128,512]{1,0:T(8,128)(2,1)S(1)} %shard_map.95.refs_0_), channel_id=1, source_target_pairs={{0,1},{1,2},{2,3},{3,0},{4,5},{5,6},{6,7},{7,4},{8,9},{9,10},{10,1... | collective-permute-start | bytes 393224 | tf_op jit(solution)/shard_map/ppermute | solution.py:44
  114.8 10.8 %collective-permute-start.41 = (bf16[128,512]{1,0:T(8,128)(2,1)S(1)}, bf16[128,512]{1,0:T(8,128)(2,1)S(1)}, u32[]{:S(2)}, u32[]{:S(2)}) collective-permute-start(bf16[128,512]{1,0:T(8,128)(2,1)S(1)} %shard_map.95.refs_0_), channel_id=1, source_target_pairs={{0,2},{1,3},{2,0},{3,1},{4,6},{5,7},{6,4},{7,5},{8,10},{9,11},{10,... | collective-permute-start | bytes 393224 | tf_op jit(solution)/shard_map/ppermute | solution.py:44
  117.1 12.3 %collective-permute-start.40 = (bf16[128,512]{1,0:T(8,128)(2,1)S(1)}, bf16[128,512]{1,0:T(8,128)(2,1)S(1)}, u32[]{:S(2)}, u32[]{:S(2)}) collective-permute-start(bf16[128,512]{1,0:T(8,128)(2,1)S(1)} %shard_map.95.refs_0_), channel_id=1, source_target_pairs={{0,3},{1,0},{2,1},{3,2},{4,7},{5,4},{6,5},{7,6},{8,11},{9,8},{10,9... | collective-permute-start | bytes 393224 | tf_op jit(solution)/shard_map/ppermute | solution.py:44

commit v3 on v2

--- a/solution.py
+++ b/solution.py
@@ -463,7 +463,7 @@
         arrived = [shifted(term, "seq", -offset - 1) for offset, term in enumerate(terms)]
         ahead = rotated(gq, "head") if split else []
         if step in (2,):
-            arrived = list(lax.optimization_barrier((tuple(arrived), tuple(ahead[1:1+3])))[0])
+            arrived = list(lax.optimization_barrier((tuple(arrived), tuple(ahead[1:1+2])))[0])
         if not split:
             arrived = list(lax.optimization_barrier((tuple(arrived), near[1]))[0])
         msg = local_call(

time: 131 us -> 130 us (level)
  waiting for transfers between devices: 35.2 us -> 33.5 us
    ppermute x16, waiting for transfers between devices: 11.8 us -> 10.2 us  [shifted(): lax.ppermute(value, axis, [(source, source + steps) for source in range(i...]
where the time goes in v3:
time: 130 us; the launch traced here: 129 us
  starting transfers between devices  65.4 us (50%)
  waiting for transfers between devices  33.5 us (26%)
  Pallas kernels  15.8 us (12%)
  blocking collectives  13.8 us (11%)
    ppermute x16, starting transfers between devices, shifted(): lax.ppermute(value, axis, [(source, source + steps) for source in range(i...  32.7 us
    ppermute x21, starting transfers between devices, rotated(): lax.ppermute(value, axis, [(i, (i - step) % count) for i in range(count)])  27.2 us
    ppermute x21, waiting for transfers between devices, rotated(): lax.ppermute(value, axis, [(i, (i - step) % count) for i in range(count)])  23.3 us
    all_to_all x1, blocking collectives, shards(): totals = lax.all_to_all(totals, ('seq', 'head'), 0, 0)  13.8 us
    ppermute x16, waiting for transfers between devices, shifted(): lax.ppermute(value, axis, [(source, source + steps) for source in range(i...  10.2 us
    pallas_call x2, Pallas kernels, shards(): local_call(functools.partial(next_body, heads, parts, scale, step == 1),...  3.82 us
    ppermute x3, starting transfers between devices, doubled(): near.append(lax.ppermute(near[0], axis, pairs))  2.72 us
    pallas_call x1, Pallas kernels, shards(): local_call(functools.partial(start_body, heads), [shape_of((rows, wide),...  2.67 us
  transfers between devices with their start and end apart: 43, of which 18 were waited for; matrix products, arithmetic and copies ran while one was open for 0% of the time, Pallas kernels for 7%

profile of v3, /device:TPU:9, one launch (start us, length us, event | category | flops | bytes accessed | tf_op | source)
XLA Modules:
  0.0 129.3 jit_solution(11403152624907524537)
XLA Ops:
  0.0 2.2 %shard_map.82 = (bf16[48,2048]{1,0:T(8,128)(2,1)S(1)}, bf16[128,2048]{1,0:T(8,128)(2,1)S(1)}, bf16[128,128]{1,0:T(8,128)(2,1)S(1)}, f32[128,128]{1,0:T(8,128)S(1)}, f32[128,128]{1,0:T(8,128)S(1)}) custom-call(s32[1]{0:T(128)} %bitcast.2.block_ref, bf16[2048,256]{1,0:T(8,128)(2,1)} %qw_ref.3, bf16[2048,128]{1,0:T(8,128)(2,1)} %kvw_ref.1, ...), custom_call_target="tpu_custom_call" | custom-call | flops 75497472 | bytes 1572864 | tf_op jit(solution)/shard_map/pallas_call | solution.py:382
  2.2 1.4 %collective-permute-start.6 = (bf16[48,2048]{1,0:T(8,128)(2,1)S(1)}, bf16[48,2048]{1,0:T(8,128)(2,1)S(1)}, u32[]{:S(2)}, u32[]{:S(2)}) collective-permute-start(bf16[48,2048]{1,0:T(8,128)(2,1)S(1)} %get-tuple-element.87), channel_id=1, source_target_pairs={{0,1},{1,2},{2,3},{3,0},{4,5},{5,6},{6,7},{7,4},{8,9},{9,10},{10,1... | collective-permute-start | bytes 589832 | tf_op jit(solution)/shard_map/ppermute | solution.py:44
  3.5 1.1 collective-permute-start.5
  4.6 1.4 %collective-permute-start.4 = (bf16[48,2048]{1,0:T(8,128)(2,1)S(1)}, bf16[48,2048]{1,0:T(8,128)(2,1)S(1)}, u32[]{:S(2)}, u32[]{:S(2)}) collective-permute-start(bf16[48,2048]{1,0:T(8,128)(2,1)S(1)} %get-tuple-element.87), channel_id=1, source_target_pairs={{0,3},{1,0},{2,1},{3,2},{4,7},{5,4},{6,5},{7,6},{8,11},{9,8},{10,9... | collective-permute-start | bytes 589832 | tf_op jit(solution)/shard_map/ppermute | solution.py:44
  6.0 4.5 %collective-permute-start.3 = (bf16[128,128]{1,0:T(8,128)(2,1)S(1)}, bf16[128,128]{1,0:T(8,128)(2,1)S(1)}, u32[]{:S(2)}, u32[]{:S(2)}) collective-permute-start(bf16[128,128]{1,0:T(8,128)(2,1)S(1)} %get-tuple-element.71.refs_4_), channel_id=1, source_target_pairs={{0,4},{4,8},{8,12},{12,16},{16,20},{20,24},{24,28},{1,5},{5,9},{9,... | collective-permute-start | bytes 98312 | tf_op jit(solution)/shard_map/ppermute | solution.py:37
  10.5 3.1 %collective-permute-start.2 = (bf16[128,128]{1,0:T(8,128)(2,1)S(1)}, bf16[128,128]{1,0:T(8,128)(2,1)S(1)}, u32[]{:S(2)}, u32[]{:S(2)}) collective-permute-start(bf16[128,128]{1,0:T(8,128)(2,1)S(1)} %get-tuple-element.71.refs_4_), channel_id=1, source_target_pairs={{0,8},{4,12},{8,16},{12,20},{16,24},{20,28},{1,9},{5,13},{9,17},{1... | collective-permute-start | bytes 98312 | tf_op jit(solution)/shard_map/ppermute | solution.py:37
  13.6 3.0 %collective-permute-start.1 = (bf16[128,128]{1,0:T(8,128)(2,1)S(1)}, bf16[128,128]{1,0:T(8,128)(2,1)S(1)}, u32[]{:S(2)}, u32[]{:S(2)}) collective-permute-start(bf16[128,128]{1,0:T(8,128)(2,1)S(1)} %get-tuple-element.71.refs_4_), channel_id=1, source_target_pairs={{0,12},{4,16},{8,20},{12,24},{16,28},{1,13},{5,17},{9,21},{13,25},... | collective-permute-start | bytes 98312 | tf_op jit(solution)/shard_map/ppermute | solution.py:37
  16.7 2.5 %collective-permute-start = (bf16[128,128]{1,0:T(8,128)(2,1)S(1)}, bf16[128,128]{1,0:T(8,128)(2,1)S(1)}, u32[]{:S(2)}, u32[]{:S(2)}) collective-permute-start(bf16[128,128]{1,0:T(8,128)(2,1)S(1)} %get-tuple-element.71.refs_4_), channel_id=1, source_target_pairs={{0,16},{4,20},{8,24},{12,28},{1,17},{5,21},{9,25},{13,29},{2,18},{... | collective-permute-start | bytes 98312 | tf_op jit(solution)/shard_map/ppermute | solution.py:37
  19.2 2.7 %shard_map.83 = (f32[128,256]{1,0:T(8,128)S(1)}, bf16[64,512]{1,0:T(8,128)(2,1)S(1)}, f32[64,512]{1,0:T(8,128)S(1)}, f32[64,512]{1,0:T(8,128)S(1)}, f32[64,512]{...) custom-call(bf16[128,2048]{1,0:T(8,128)(2,1)S(1)} %get-tuple-element.72.hidden_ref, ...), custom_call_target="tpu_custom_call" | custom-call | flops 402653184 | bytes 4194304 | tf_op jit(solution)/shard_map/pallas_call | solution.py:412
  21.9 1.1 shard_map.84
  24.5 2.8 %collective-permute-start.7 = (bf16[128,128]{1,0:T(8,128)(2,1)S(1)}, bf16[128,128]{1,0:T(8,128)(2,1)S(1)}, u32[]{:S(2)}, u32[]{:S(2)}) collective-permute-start(bf16[128,128]{1,0:T(8,128)(2,1)S(1)} %get-tuple-element.90), channel_id=1, source_target_pairs={{4,0},{8,4},{12,8},{16,12},{20,16},{24,20},{28,24},{5,1},{9,5},{13... | collective-permute-start | bytes 98312 | tf_op jit(solution)/shard_map/ppermute | solution.py:37
  27.2 1.3 collective-permute-start.8
  28.5 1.3 collective-permute-start.9
  29.8 1.3 collective-permute-start.10
  32.2 2.9 %collective-permute-done.9.refs_2_ = bf16[128,128]{1,0:T(8,128)(2,1)S(1)} collective-permute-done((bf16[128,128]{1,0:T(8,128)(2,1)S(1)}, bf16[128,128]{1,0:T(8,128)(2,1)S(1)}, u32[]{:S(2)}, u32[]{:S(2)}) %collective-permute-start.9) | collective-permute-done | bytes 32800 | tf_op jit(solution)/shard_map/ppermute | solution.py:37
  36.0 1.8 %collective-permute-start.15 = (bf16[2,4,48,256]{3,2,1,0:T(8,128)(2,1)S(1)}, bf16[2,4,48,256]{3,2,1,0:T(8,128)(2,1)S(1)}, u32[]{:S(2)}, u32[]{:S(2)}) collective-permute-start(bf16[2,4,48,256]{3,2,1,0:T(8,128)(2,1)S(1)} %constant_dynamic-update-slice_fusion), channel_id=1, source_target_pairs={{0,8},{4,12},{8,0},{12,4},{16,24},{20,28},{24,16},{28,20},{1,9},{5... | collective-permute-start | bytes 589832 | tf_op jit(solution)/shard_map/ppermute | solution.py:58
  37.8 1.1 collective-permute-start.12
  39.3 3.1 %collective-permute-start.13 = (bf16[144,384]{1,0:T(8,128)(2,1)S(1)}, bf16[144,384]{1,0:T(8,128)(2,1)S(1)}, u32[]{:S(2)}, u32[]{:S(2)}) collective-permute-start(bf16[144,384]{1,0:T(8,128)(2,1)S(1)} %shard_map.87.refs_0_), channel_id=1, source_target_pairs={{0,2},{1,3},{2,0},{3,1},{4,6},{5,7},{6,4},{7,5},{8,10},{9,11},{10,... | collective-permute-start | bytes 331784 | tf_op jit(solution)/shard_map/ppermute | solution.py:44
  42.5 1.4 %collective-permute-start.16 = (bf16[4,4,48,256]{3,2,1,0:T(8,128)(2,1)S(1)}, bf16[4,4,48,256]{3,2,1,0:T(8,128)(2,1)S(1)}, u32[]{:S(2)}, u32[]{:S(2)}) collective-permute-start(bf16[4,4,48,256]{3,2,1,0:T(8,128)(2,1)S(1)} %constant_dynamic-update-slice_fusion.2.refs_10_), channel_id=1, source_target_pairs={{0,4},{4,0},{8,12},{12,8},{16,20},{20,16},{24,28},{28,24},{1,5},{5... | collective-permute-start | bytes 1179656 | tf_op jit(solution)/shard_map/ppermute | solution.py:57
  43.9 1.6 %collective-permute-done.14.refs_3_ = bf16[144,384]{1,0:T(8,128)(2,1)S(1)} collective-permute-done((bf16[144,384]{1,0:T(8,128)(2,1)S(1)}, bf16[144,384]{1,0:T(8,128)(2,1)S(1)}, u32[]{:S(2)}, u32[]{:S(2)}) %collective-permute-start.14) | collective-permute-done | bytes 110624 | tf_op jit(solution)/shard_map/ppermute | solution.py:44
  45.5 2.9 %collective-permute-done.13.refs_2_ = bf16[144,384]{1,0:T(8,128)(2,1)S(1)} collective-permute-done((bf16[144,384]{1,0:T(8,128)(2,1)S(1)}, bf16[144,384]{1,0:T(8,128)(2,1)S(1)}, u32[]{:S(2)}, u32[]{:S(2)}) %collective-permute-start.13) | collective-permute-done | bytes 110624 | tf_op jit(solution)/shard_map/ppermute | solution.py:44
  49.4 1.9 %shard_map.88 = (bf16[640,512]{1,0:T(8,128)(2,1)S(1)}, f32[128,128]{1,0:T(8,128)S(1)}, bf16[4,128,384]{2,1,0:T(8,128)(2,1)S(1)}, f32[16,128]{1,0:T(8,128)S(1)}, ...) custom-call(s32[2]{0:T(128)S(1)} %pad_add_fusion.spot_ref, ...), custom_call_target="tpu_custom_call" | custom-call | flops 226492416 | bytes 1441792 | tf_op jit(solution)/shard_map/pallas_call | solution.py:495
  51.3 3.3 %collective-permute-start.20 = (bf16[128,128]{1,0:T(8,128)(2,1)S(1)}, bf16[128,128]{1,0:T(8,128)(2,1)S(1)}, u32[]{:S(2)}, u32[]{:S(2)}) collective-permute-start(bf16[128,128]{1,0:T(8,128)(2,1)S(1)} %get-tuple-element.108), channel_id=1, source_target_pairs={{4,0},{8,4},{12,8},{16,12},{20,16},{24,20},{28,24},{5,1},{9,5},{13... | collective-permute-start | bytes 98312 | tf_op jit(solution)/shard_map/ppermute | solution.py:37
  54.6 1.3 collective-permute-start.21
  55.9 1.3 collective-permute-start.22
  57.2 1.3 collective-permute-start.23
  58.8 1.2 collective-permute-done.20.refs_0_
  60.7 3.3 %collective-permute-start.18 = (bf16[128,256]{1,0:T(8,128)(2,1)S(1)}, bf16[128,256]{1,0:T(8,128)(2,1)S(1)}, u32[]{:S(2)}, u32[]{:S(2)}) collective-permute-start(bf16[128,256]{1,0:T(8,128)(2,1)S(1)} %shard_map.89.gq_ref.refs_0_), channel_id=1, source_target_pairs={{0,2},{1,3},{2,0},{3,1},{4,6},{5,7},{6,4},{7,5},{8,10},{9,11},{10,... | collective-permute-start | bytes 196616 | tf_op jit(solution)/shard_map/ppermute | solution.py:44
  65.6 3.2 %collective-permute-start.25 = (bf16[144,128]{1,0:T(8,128)(2,1)S(1)}, bf16[144,128]{1,0:T(8,128)(2,1)S(1)}, u32[]{:S(2)}, u32[]{:S(2)}) collective-permute-start(bf16[144,128]{1,0:T(8,128)(2,1)S(1)} %shard_map.90.refs_4_), channel_id=1, source_target_pairs={{0,2},{1,3},{2,0},{3,1},{4,6},{5,7},{6,4},{7,5},{8,10},{9,11},{10,... | collective-permute-start | bytes 110600 | tf_op jit(solution)/shard_map/ppermute | solution.py:44
  69.7 1.9 %collective-permute-done.25.refs_6_ = bf16[144,128]{1,0:T(8,128)(2,1)S(1)} collective-permute-done((bf16[144,128]{1,0:T(8,128)(2,1)S(1)}, bf16[144,128]{1,0:T(8,128)(2,1)S(1)}, u32[]{:S(2)}, u32[]{:S(2)}) %collective-permute-start.25) | collective-permute-done | bytes 36896 | tf_op jit(solution)/shard_map/ppermute | solution.py:44
  73.4 1.9 %shard_map.91 = (bf16[640,512]{1,0:T(8,128)(2,1)S(1)}, f32[128,128]{1,0:T(8,128)S(1)}, bf16[4,128,384]{2,1,0:T(8,128)(2,1)S(1)}, f32[16,128]{1,0:T(8,128)S(1)}, ...) custom-call(s32[2]{0:T(128)S(1)} %pad_add_fusion.spot_ref, ...), custom_call_target="tpu_custom_call" | custom-call | flops 226492416 | bytes 1441792 | tf_op jit(solution)/shard_map/pallas_call | solution.py:495
  75.3 1.9 %collective-permute-start.33 = (bf16[128,128]{1,0:T(8,128)(2,1)S(1)}, bf16[128,128]{1,0:T(8,128)(2,1)S(1)}, u32[]{:S(2)}, u32[]{:S(2)}) collective-permute-start(bf16[128,128]{1,0:T(8,128)(2,1)S(1)} %get-tuple-element.121), channel_id=1, source_target_pairs={{4,0},{8,4},{12,8},{16,12},{20,16},{24,20},{28,24},{5,1},{9,5},{13... | collective-permute-start | bytes 98312 | tf_op jit(solution)/shard_map/ppermute | solution.py:37
  77.5 2.1 %collective-permute-start.31 = (bf16[128,256]{1,0:T(8,128)(2,1)S(1)}, bf16[128,256]{1,0:T(8,128)(2,1)S(1)}, u32[]{:S(2)}, u32[]{:S(2)}) collective-permute-start(bf16[128,256]{1,0:T(8,128)(2,1)S(1)} %shard_map.92.gq_ref.refs_0_), channel_id=1, source_target_pairs={{0,2},{1,3},{2,0},{3,1},{4,6},{5,7},{6,4},{7,5},{8,10},{9,11},{10,... | collective-permute-start | bytes 196616 | tf_op jit(solution)/shard_map/ppermute | solution.py:44
  79.6 1.3 collective-permute-start.34
  80.9 1.3 collective-permute-start.35
  82.2 1.3 collective-permute-start.36
  84.5 1.4 %collective-permute-start.32 = (bf16[128,256]{1,0:T(8,128)(2,1)S(1)}, bf16[128,256]{1,0:T(8,128)(2,1)S(1)}, u32[]{:S(2)}, u32[]{:S(2)}) collective-permute-start(bf16[128,256]{1,0:T(8,128)(2,1)S(1)} %shard_map.92.gq_ref.refs_0_), channel_id=1, source_target_pairs={{0,1},{1,2},{2,3},{3,0},{4,5},{5,6},{6,7},{7,4},{8,9},{9,10},{10,1... | collective-permute-start | bytes 196616 | tf_op jit(solution)/shard_map/ppermute | solution.py:44
  85.9 2.5 %collective-permute-done.35.refs_2_ = bf16[128,128]{1,0:T(8,128)(2,1)S(1)} collective-permute-done((bf16[128,128]{1,0:T(8,128)(2,1)S(1)}, bf16[128,128]{1,0:T(8,128)(2,1)S(1)}, u32[]{:S(2)}, u32[]{:S(2)}) %collective-permute-start.35) | collective-permute-done | bytes 32800 | tf_op jit(solution)/shard_map/ppermute | solution.py:37
  89.6 1.8 %collective-permute-start.39 = (bf16[144,128]{1,0:T(8,128)(2,1)S(1)}, bf16[144,128]{1,0:T(8,128)(2,1)S(1)}, u32[]{:S(2)}, u32[]{:S(2)}) collective-permute-start(bf16[144,128]{1,0:T(8,128)(2,1)S(1)} %shard_map.93.refs_4_), channel_id=1, source_target_pairs={{0,1},{1,2},{2,3},{3,0},{4,5},{5,6},{6,7},{7,4},{8,9},{9,10},{10,1... | collective-permute-start | bytes 110600 | tf_op jit(solution)/shard_map/ppermute | solution.py:44
  91.4 2.0 %collective-permute-start.38 = (bf16[144,128]{1,0:T(8,128)(2,1)S(1)}, bf16[144,128]{1,0:T(8,128)(2,1)S(1)}, u32[]{:S(2)}, u32[]{:S(2)}) collective-permute-start(bf16[144,128]{1,0:T(8,128)(2,1)S(1)} %shard_map.93.refs_4_), channel_id=1, source_target_pairs={{0,2},{1,3},{2,0},{3,1},{4,6},{5,7},{6,4},{7,5},{8,10},{9,11},{10,... | collective-permute-start | bytes 110600 | tf_op jit(solution)/shard_map/ppermute | solution.py:44
  93.4 1.7 %collective-permute-done.38.refs_6_ = bf16[144,128]{1,0:T(8,128)(2,1)S(1)} collective-permute-done((bf16[144,128]{1,0:T(8,128)(2,1)S(1)}, bf16[144,128]{1,0:T(8,128)(2,1)S(1)}, u32[]{:S(2)}, u32[]{:S(2)}) %collective-permute-start.38) | collective-permute-done | bytes 36896 | tf_op jit(solution)/shard_map/ppermute | solution.py:44
  96.2 1.9 %shard_map.94 = (f32[3,128,512]{2,1,0:T(8,128)S(1)}, f32[32,8,128]{2,1,0:T(8,128)S(1)}) custom-call(s32[2]{0:T(128)S(1)} %pad_add_fusion.spot_ref, bf16[128,256]{1,0:T(8,128)(2,1)S(1)} %shard_map.92.gq_ref.refs_0_, bf16[128,256]{1,0:T(8,128)(2,1)S(1)} %collective-permute-done.30.refs_1_, bf16[128,256]{1,0:T(8,128)(2,1)S(1)} %collective-permute-done.31.refs_2_, ...), custom_call_target="tpu_custom_call" | custom-call | flops 603979776 | bytes 1572864 | tf_op jit(solution)/shard_map/pallas_call | solution.py:534
  98.1 13.8 %all_to_all.5.tot_ref = f32[32,8,128]{2,1,0:T(8,128)S(1)} all-to-all(f32[32,8,128]{2,1,0:T(8,128)S(1)} %get-tuple-element.135), channel_id=1, replica_groups=mesh['seq'=8,'head'=4] {'seq','head'}, dimensions={0} | all-to-all | bytes 262144 | tf_op jit(solution)/shard_map/all_to_all | solution.py:550
  113.2 2.2 %collective-permute-start.41 = (bf16[128,512]{1,0:T(8,128)(2,1)S(1)}, bf16[128,512]{1,0:T(8,128)(2,1)S(1)}, u32[]{:S(2)}, u32[]{:S(2)}) collective-permute-start(bf16[128,512]{1,0:T(8,128)(2,1)S(1)} %shard_map.95.refs_0_), channel_id=1, source_target_pairs={{0,2},{1,3},{2,0},{3,1},{4,6},{5,7},{6,4},{7,5},{8,10},{9,11},{10,... | collective-permute-start | bytes 393224 | tf_op jit(solution)/shard_map/ppermute | solution.py:44
  115.5 2.2 %collective-permute-done.42.refs_3_ = bf16[128,512]{1,0:T(8,128)(2,1)S(1)} collective-permute-done((bf16[128,512]{1,0:T(8,128)(2,1)S(1)}, bf16[128,512]{1,0:T(8,128)(2,1)S(1)}, u32[]{:S(2)}, u32[]{:S(2)}) %collective-permute-start.42) | collective-permute-done | bytes 131104 | tf_op jit(solution)/shard_map/ppermute | solution.py:44
  117.7 6.4 %collective-permute-done.41.refs_2_ = bf16[128,512]{1,0:T(8,128)(2,1)S(1)} collective-permute-done((bf16[128,512]{1,0:T(8,128)(2,1)S(1)}, bf16[128,512]{1,0:T(8,128)(2,1)S(1)}, u32[]{:S(2)}, u32[]{:S(2)}) %collective-permute-start.41) | collective-permute-done | bytes 131104 | tf_op jit(solution)/shard_map/ppermute | solution.py:44
  124.1 3.7 %collective-permute-done.40.refs_1_ = bf16[128,512]{1,0:T(8,128)(2,1)S(1)} collective-permute-done((bf16[128,512]{1,0:T(8,128)(2,1)S(1)}, bf16[128,512]{1,0:T(8,128)(2,1)S(1)}, u32[]{:S(2)}, u32[]{:S(2)}) %collective-permute-start.40) | collective-permute-done | bytes 131104 | tf_op jit(solution)/shard_map/ppermute | solution.py:44
  127.8 1.6 %shard_map.96 = f32[128,2048]{1,0:T(8,128)} custom-call(s32[2]{0:T(128)S(1)} %pad_add_fusion.spot_ref, bf16[128,512]{1,0:T(8,128)(2,1)S(1)} %shard_map.95.refs_0_, bf16[128,512]{1,0:T(8,128)(2,1)S(1)} %collective-permute-done.40.refs_1_, bf16[128,512]{1,0:T(8,128)(2,1)S(1)} %collective-permute-done.41.refs_2_, ...), custom_call_target="tpu_custom_call" | custom-call | bytes 1572864 | tf_op jit(solution)/shard_map/pallas_call | solution.py:562
  (73 shorter events, 15.0 us)
Async XLA Ops:
  0.0 19.2 %copy-start.2 = (bf16[2048,256]{1,0:T(8,128)(2,1)S(1)}, bf16[2048,256]{1,0:T(8,128)(2,1)}, u32[]{:S(2)}) copy-start(bf16[2048,256]{1,0:T(8,128)(2,1)} %qw_ref.3) | copy-start | bytes 3145732
  2.2 20.9 %collective-permute-start.6 = (bf16[48,2048]{1,0:T(8,128)(2,1)S(1)}, bf16[48,2048]{1,0:T(8,128)(2,1)S(1)}, u32[]{:S(2)}, u32[]{:S(2)}) collective-permute-start(bf16[48,2048]{1,0:T(8,128)(2,1)S(1)} %get-tuple-element.87), channel_id=1, source_target_pairs={{0,1},{1,2},{2,3},{3,0},{4,5},{5,6},{6,7},{7,4},{8,9},{9,10},{10,1... | collective-permute-start | bytes 589832 | tf_op jit(solution)/shard_map/ppermute | solution.py:44
  3.5 19.6 %collective-permute-start.5 = (bf16[48,2048]{1,0:T(8,128)(2,1)S(1)}, bf16[48,2048]{1,0:T(8,128)(2,1)S(1)}, u32[]{:S(2)}, u32[]{:S(2)}) collective-permute-start(bf16[48,2048]{1,0:T(8,128)(2,1)S(1)} %get-tuple-element.87), channel_id=1, source_target_pairs={{0,2},{1,3},{2,0},{3,1},{4,6},{5,7},{6,4},{7,5},{8,10},{9,11},{10,... | collective-permute-start | bytes 589832 | tf_op jit(solution)/shard_map/ppermute | solution.py:44
  4.6 18.5 %collective-permute-start.4 = (bf16[48,2048]{1,0:T(8,128)(2,1)S(1)}, bf16[48,2048]{1,0:T(8,128)(2,1)S(1)}, u32[]{:S(2)}, u32[]{:S(2)}) collective-permute-start(bf16[48,2048]{1,0:T(8,128)(2,1)S(1)} %get-tuple-element.87), channel_id=1, source_target_pairs={{0,3},{1,0},{2,1},{3,2},{4,7},{5,4},{6,5},{7,6},{8,11},{9,8},{10,9... | collective-permute-start | bytes 589832 | tf_op jit(solution)/shard_map/ppermute | solution.py:44
  6.0 7.6 %collective-permute-start.3 = (bf16[128,128]{1,0:T(8,128)(2,1)S(1)}, bf16[128,128]{1,0:T(8,128)(2,1)S(1)}, u32[]{:S(2)}, u32[]{:S(2)}) collective-permute-start(bf16[128,128]{1,0:T(8,128)(2,1)S(1)} %get-tuple-element.71.refs_4_), channel_id=1, source_target_pairs={{0,4},{4,8},{8,12},{12,16},{16,20},{20,24},{24,28},{1,5},{5,9},{9,... | collective-permute-start | bytes 98312 | tf_op jit(solution)/shard_map/ppermute | solution.py:37
  10.5 6.1 %collective-permute-start.2 = (bf16[128,128]{1,0:T(8,128)(2,1)S(1)}, bf16[128,128]{1,0:T(8,128)(2,1)S(1)}, u32[]{:S(2)}, u32[]{:S(2)}) collective-permute-start(bf16[128,128]{1,0:T(8,128)(2,1)S(1)} %get-tuple-element.71.refs_4_), channel_id=1, source_target_pairs={{0,8},{4,12},{8,16},{12,20},{16,24},{20,28},{1,9},{5,13},{9,17},{1... | collective-permute-start | bytes 98312 | tf_op jit(solution)/shard_map/ppermute | solution.py:37
  13.6 8.3 %collective-permute-start.1 = (bf16[128,128]{1,0:T(8,128)(2,1)S(1)}, bf16[128,128]{1,0:T(8,128)(2,1)S(1)}, u32[]{:S(2)}, u32[]{:S(2)}) collective-permute-start(bf16[128,128]{1,0:T(8,128)(2,1)S(1)} %get-tuple-element.71.refs_4_), channel_id=1, source_target_pairs={{0,12},{4,16},{8,20},{12,24},{16,28},{1,13},{5,17},{9,21},{13,25},... | collective-permute-start | bytes 98312 | tf_op jit(solution)/shard_map/ppermute | solution.py:37
  16.7 5.2 %collective-permute-start = (bf16[128,128]{1,0:T(8,128)(2,1)S(1)}, bf16[128,128]{1,0:T(8,128)(2,1)S(1)}, u32[]{:S(2)}, u32[]{:S(2)}) collective-permute-start(bf16[128,128]{1,0:T(8,128)(2,1)S(1)} %get-tuple-element.71.refs_4_), channel_id=1, source_target_pairs={{0,16},{4,20},{8,24},{12,28},{1,17},{5,21},{9,25},{13,29},{2,18},{... | collective-permute-start | bytes 98312 | tf_op jit(solution)/shard_map/ppermute | solution.py:37
  23.7 12.1 %collective-permute-start.11 = (bf16[1,4,48,256]{3,2,1,0:T(8,128)(2,1)S(1)}, bf16[1,4,48,256]{3,2,1,0:T(8,128)(2,1)S(1)}, u32[]{:S(2)}, u32[]{:S(2)}) collective-permute-start(bf16[1,4,48,256]{3,2,1,0:T(8,128)(2,1)S(1)} %bitcast.14), channel_id=1, source_target_pairs={{0,16},{4,20},{8,24},{12,28},{16,0},{20,4},{24,8},{28,12},{1,17},{... | collective-permute-start | bytes 294920 | tf_op jit(solution)/shard_map/ppermute | solution.py:522
  24.5 7.0 %collective-permute-start.7 = (bf16[128,128]{1,0:T(8,128)(2,1)S(1)}, bf16[128,128]{1,0:T(8,128)(2,1)S(1)}, u32[]{:S(2)}, u32[]{:S(2)}) collective-permute-start(bf16[128,128]{1,0:T(8,128)(2,1)S(1)} %get-tuple-element.90), channel_id=1, source_target_pairs={{4,0},{8,4},{12,8},{16,12},{20,16},{24,20},{28,24},{5,1},{9,5},{13... | collective-permute-start | bytes 98312 | tf_op jit(solution)/shard_map/ppermute | solution.py:37
  27.2 5.0 %collective-permute-start.8 = (bf16[128,128]{1,0:T(8,128)(2,1)S(1)}, bf16[128,128]{1,0:T(8,128)(2,1)S(1)}, u32[]{:S(2)}, u32[]{:S(2)}) collective-permute-start(bf16[128,128]{1,0:T(8,128)(2,1)S(1)} %get-tuple-element.91), channel_id=1, source_target_pairs={{8,0},{12,4},{16,8},{20,12},{24,16},{28,20},{9,1},{13,5},{17,9},{2... | collective-permute-start | bytes 98312 | tf_op jit(solution)/shard_map/ppermute | solution.py:37
  28.5 6.6 %collective-permute-start.9 = (bf16[128,128]{1,0:T(8,128)(2,1)S(1)}, bf16[128,128]{1,0:T(8,128)(2,1)S(1)}, u32[]{:S(2)}, u32[]{:S(2)}) collective-permute-start(bf16[128,128]{1,0:T(8,128)(2,1)S(1)} %get-tuple-element.92), channel_id=1, source_target_pairs={{12,0},{16,4},{20,8},{24,12},{28,16},{13,1},{17,5},{21,9},{25,13},... | collective-permute-start | bytes 98312 | tf_op jit(solution)/shard_map/ppermute | solution.py:37
  29.8 6.0 %collective-permute-start.10 = (bf16[128,128]{1,0:T(8,128)(2,1)S(1)}, bf16[128,128]{1,0:T(8,128)(2,1)S(1)}, u32[]{:S(2)}, u32[]{:S(2)}) collective-permute-start(bf16[128,128]{1,0:T(8,128)(2,1)S(1)} %get-tuple-element.93), channel_id=1, source_target_pairs={{16,0},{20,4},{24,8},{28,12},{17,1},{21,5},{25,9},{29,13},{18,2},{... | collective-permute-start | bytes 98312 | tf_op jit(solution)/shard_map/ppermute | solution.py:37
  36.0 6.5 %collective-permute-start.15 = (bf16[2,4,48,256]{3,2,1,0:T(8,128)(2,1)S(1)}, bf16[2,4,48,256]{3,2,1,0:T(8,128)(2,1)S(1)}, u32[]{:S(2)}, u32[]{:S(2)}) collective-permute-start(bf16[2,4,48,256]{3,2,1,0:T(8,128)(2,1)S(1)} %constant_dynamic-update-slice_fusion), channel_id=1, source_target_pairs={{0,8},{4,12},{8,0},{12,4},{16,24},{20,28},{24,16},{28,20},{1,9},{5... | collective-permute-start | bytes 589832 | tf_op jit(solution)/shard_map/ppermute | solution.py:58
  37.8 4.7 %collective-permute-start.12 = (bf16[144,384]{1,0:T(8,128)(2,1)S(1)}, bf16[144,384]{1,0:T(8,128)(2,1)S(1)}, u32[]{:S(2)}, u32[]{:S(2)}) collective-permute-start(bf16[144,384]{1,0:T(8,128)(2,1)S(1)} %shard_map.87.refs_0_), channel_id=1, source_target_pairs={{0,3},{1,0},{2,1},{3,2},{4,7},{5,4},{6,5},{7,6},{8,11},{9,8},{10,9... | collective-permute-start | bytes 331784 | tf_op jit(solution)/shard_map/ppermute | solution.py:44
  38.9 6.5 %collective-permute-start.14 = (bf16[144,384]{1,0:T(8,128)(2,1)S(1)}, bf16[144,384]{1,0:T(8,128)(2,1)S(1)}, u32[]{:S(2)}, u32[]{:S(2)}) collective-permute-start(bf16[144,384]{1,0:T(8,128)(2,1)S(1)} %shard_map.87.refs_0_), channel_id=1, source_target_pairs={{0,1},{1,2},{2,3},{3,0},{4,5},{5,6},{6,7},{7,4},{8,9},{9,10},{10,1... | collective-permute-start | bytes 331784 | tf_op jit(solution)/shard_map/ppermute | solution.py:44
  39.3 9.0 %collective-permute-start.13 = (bf16[144,384]{1,0:T(8,128)(2,1)S(1)}, bf16[144,384]{1,0:T(8,128)(2,1)S(1)}, u32[]{:S(2)}, u32[]{:S(2)}) collective-permute-start(bf16[144,384]{1,0:T(8,128)(2,1)S(1)} %shard_map.87.refs_0_), channel_id=1, source_target_pairs={{0,2},{1,3},{2,0},{3,1},{4,6},{5,7},{6,4},{7,5},{8,10},{9,11},{10,... | collective-permute-start | bytes 331784 | tf_op jit(solution)/shard_map/ppermute | solution.py:44
  42.5 5.8 %collective-permute-start.27 = (bf16[1,4,48,512]{3,2,1,0:T(8,128)(2,1)S(1)}, bf16[1,4,48,512]{3,2,1,0:T(8,128)(2,1)S(1)}, u32[]{:S(2)}, u32[]{:S(2)}) collective-permute-start(bf16[1,4,48,512]{3,2,1,0:T(8,128)(2,1)S(1)} %dynamic-slice_bitcast_fusion), channel_id=1, source_target_pairs={{0,16},{4,20},{8,24},{12,28},{16,0},{20,4},{24,8},{28,12},{1,17},{... | collective-permute-start | bytes 589832 | tf_op jit(solution)/shard_map/ppermute | solution.py:58
  42.5 6.8 %collective-permute-start.16 = (bf16[4,4,48,256]{3,2,1,0:T(8,128)(2,1)S(1)}, bf16[4,4,48,256]{3,2,1,0:T(8,128)(2,1)S(1)}, u32[]{:S(2)}, u32[]{:S(2)}) collective-permute-start(bf16[4,4,48,256]{3,2,1,0:T(8,128)(2,1)S(1)} %constant_dynamic-update-slice_fusion.2.refs_10_), channel_id=1, source_target_pairs={{0,4},{4,0},{8,12},{12,8},{16,20},{20,16},{24,28},{28,24},{1,5},{5... | collective-permute-start | bytes 1179656 | tf_op jit(solution)/shard_map/ppermute | solution.py:57
  48.4 17.2 %collective-permute-start.28 = (bf16[2,4,48,512]{3,2,1,0:T(8,128)(2,1)S(1)}, bf16[2,4,48,512]{3,2,1,0:T(8,128)(2,1)S(1)}, u32[]{:S(2)}, u32[]{:S(2)}) collective-permute-start(bf16[2,4,48,512]{3,2,1,0:T(8,128)(2,1)S(1)} %constant_dynamic-update-slice_fusion.4), channel_id=1, source_target_pairs={{0,8},{4,12},{8,0},{12,4},{16,24},{20,28},{24,16},{28,20},{1,9},{5... | collective-permute-start | bytes 1179656 | tf_op jit(solution)/shard_map/ppermute | solution.py:58
  51.3 8.7 %collective-permute-start.20 = (bf16[128,128]{1,0:T(8,128)(2,1)S(1)}, bf16[128,128]{1,0:T(8,128)(2,1)S(1)}, u32[]{:S(2)}, u32[]{:S(2)}) collective-permute-start(bf16[128,128]{1,0:T(8,128)(2,1)S(1)} %get-tuple-element.108), channel_id=1, source_target_pairs={{4,0},{8,4},{12,8},{16,12},{20,16},{24,20},{28,24},{5,1},{9,5},{13... | collective-permute-start | bytes 98312 | tf_op jit(solution)/shard_map/ppermute | solution.py:37
  54.6 6.1 %collective-permute-start.21 = (bf16[128,128]{1,0:T(8,128)(2,1)S(1)}, bf16[128,128]{1,0:T(8,128)(2,1)S(1)}, u32[]{:S(2)}, u32[]{:S(2)}) collective-permute-start(bf16[128,128]{1,0:T(8,128)(2,1)S(1)} %get-tuple-element.109), channel_id=1, source_target_pairs={{8,0},{12,4},{16,8},{20,12},{24,16},{28,20},{9,1},{13,5},{17,9},{2... | collective-permute-start | bytes 98312 | tf_op jit(solution)/shard_map/ppermute | solution.py:37
  55.9 8.1 %collective-permute-start.22 = (bf16[128,128]{1,0:T(8,128)(2,1)S(1)}, bf16[128,128]{1,0:T(8,128)(2,1)S(1)}, u32[]{:S(2)}, u32[]{:S(2)}) collective-permute-start(bf16[128,128]{1,0:T(8,128)(2,1)S(1)} %get-tuple-element.110), channel_id=1, source_target_pairs={{12,0},{16,4},{20,8},{24,12},{28,16},{13,1},{17,5},{21,9},{25,13},... | collective-permute-start | bytes 98312 | tf_op jit(solution)/shard_map/ppermute | solution.py:37
  57.2 7.5 %collective-permute-start.23 = (bf16[128,128]{1,0:T(8,128)(2,1)S(1)}, bf16[128,128]{1,0:T(8,128)(2,1)S(1)}, u32[]{:S(2)}, u32[]{:S(2)}) collective-permute-start(bf16[128,128]{1,0:T(8,128)(2,1)S(1)} %get-tuple-element.111), channel_id=1, source_target_pairs={{16,0},{20,4},{24,8},{28,12},{17,1},{21,5},{25,9},{29,13},{18,2},{... | collective-permute-start | bytes 98312 | tf_op jit(solution)/shard_map/ppermute | solution.py:37
  60.0 8.9 %collective-permute-start.19 = (bf16[128,256]{1,0:T(8,128)(2,1)S(1)}, bf16[128,256]{1,0:T(8,128)(2,1)S(1)}, u32[]{:S(2)}, u32[]{:S(2)}) collective-permute-start(bf16[128,256]{1,0:T(8,128)(2,1)S(1)} %shard_map.89.gq_ref.refs_0_), channel_id=1, source_target_pairs={{0,1},{1,2},{2,3},{3,0},{4,5},{5,6},{6,7},{7,4},{8,9},{9,10},{10,1... | collective-permute-start | bytes 196616 | tf_op jit(solution)/shard_map/ppermute | solution.py:44
  60.7 8.2 %collective-permute-start.18 = (bf16[128,256]{1,0:T(8,128)(2,1)S(1)}, bf16[128,256]{1,0:T(8,128)(2,1)S(1)}, u32[]{:S(2)}, u32[]{:S(2)}) collective-permute-start(bf16[128,256]{1,0:T(8,128)(2,1)S(1)} %shard_map.89.gq_ref.refs_0_), channel_id=1, source_target_pairs={{0,2},{1,3},{2,0},{3,1},{4,6},{5,7},{6,4},{7,5},{8,10},{9,11},{10,... | collective-permute-start | bytes 196616 | tf_op jit(solution)/shard_map/ppermute | solution.py:44
  64.0 5.2 %collective-permute-start.17 = (bf16[128,256]{1,0:T(8,128)(2,1)S(1)}, bf16[128,256]{1,0:T(8,128)(2,1)S(1)}, u32[]{:S(2)}, u32[]{:S(2)}) collective-permute-start(bf16[128,256]{1,0:T(8,128)(2,1)S(1)} %shard_map.89.gq_ref.refs_0_), channel_id=1, source_target_pairs={{0,3},{1,0},{2,1},{3,2},{4,7},{5,4},{6,5},{7,6},{8,11},{9,8},{10,9... | collective-permute-start | bytes 196616 | tf_op jit(solution)/shard_map/ppermute | solution.py:44
  64.8 4.9 %collective-permute-start.26 = (bf16[144,128]{1,0:T(8,128)(2,1)S(1)}, bf16[144,128]{1,0:T(8,128)(2,1)S(1)}, u32[]{:S(2)}, u32[]{:S(2)}) collective-permute-start(bf16[144,128]{1,0:T(8,128)(2,1)S(1)} %shard_map.90.refs_4_), channel_id=1, source_target_pairs={{0,1},{1,2},{2,3},{3,0},{4,5},{5,6},{6,7},{7,4},{8,9},{9,10},{10,1... | collective-permute-start | bytes 110600 | tf_op jit(solution)/shard_map/ppermute | solution.py:44
  65.6 6.1 %collective-permute-start.25 = (bf16[144,128]{1,0:T(8,128)(2,1)S(1)}, bf16[144,128]{1,0:T(8,128)(2,1)S(1)}, u32[]{:S(2)}, u32[]{:S(2)}) collective-permute-start(bf16[144,128]{1,0:T(8,128)(2,1)S(1)} %shard_map.90.refs_4_), channel_id=1, source_target_pairs={{0,2},{1,3},{2,0},{3,1},{4,6},{5,7},{6,4},{7,5},{8,10},{9,11},{10,... | collective-permute-start | bytes 110600 | tf_op jit(solution)/shard_map/ppermute | solution.py:44
  68.8 3.8 %collective-permute-start.24 = (bf16[144,128]{1,0:T(8,128)(2,1)S(1)}, bf16[144,128]{1,0:T(8,128)(2,1)S(1)}, u32[]{:S(2)}, u32[]{:S(2)}) collective-permute-start(bf16[144,128]{1,0:T(8,128)(2,1)S(1)} %shard_map.90.refs_4_), channel_id=1, source_target_pairs={{0,3},{1,0},{2,1},{3,2},{4,7},{5,4},{6,5},{7,6},{8,11},{9,8},{10,9... | collective-permute-start | bytes 110600 | tf_op jit(solution)/shard_map/ppermute | solution.py:44
  72.7 4.5 %collective-permute-start.29 = (bf16[4,4,48,512]{3,2,1,0:T(8,128)(2,1)S(1)}, bf16[4,4,48,512]{3,2,1,0:T(8,128)(2,1)S(1)}, u32[]{:S(2)}, u32[]{:S(2)}) collective-permute-start(bf16[4,4,48,512]{3,2,1,0:T(8,128)(2,1)S(1)} %constant_dynamic-update-slice_fusion.6.refs_12_), channel_id=1, source_target_pairs={{0,4},{4,0},{8,12},{12,8},{16,20},{20,16},{24,28},{28,24},{1,5},{5... | collective-permute-start | bytes 2359304 | tf_op jit(solution)/shard_map/ppermute | solution.py:57
  75.3 6.9 %collective-permute-start.33 = (bf16[128,128]{1,0:T(8,128)(2,1)S(1)}, bf16[128,128]{1,0:T(8,128)(2,1)S(1)}, u32[]{:S(2)}, u32[]{:S(2)}) collective-permute-start(bf16[128,128]{1,0:T(8,128)(2,1)S(1)} %get-tuple-element.121), channel_id=1, source_target_pairs={{4,0},{8,4},{12,8},{16,12},{20,16},{24,20},{28,24},{5,1},{9,5},{13... | collective-permute-start | bytes 98312 | tf_op jit(solution)/shard_map/ppermute | solution.py:37
  77.5 12.0 %collective-permute-start.31 = (bf16[128,256]{1,0:T(8,128)(2,1)S(1)}, bf16[128,256]{1,0:T(8,128)(2,1)S(1)}, u32[]{:S(2)}, u32[]{:S(2)}) collective-permute-start(bf16[128,256]{1,0:T(8,128)(2,1)S(1)} %shard_map.92.gq_ref.refs_0_), channel_id=1, source_target_pairs={{0,2},{1,3},{2,0},{3,1},{4,6},{5,7},{6,4},{7,5},{8,10},{9,11},{10,... | collective-permute-start | bytes 196616 | tf_op jit(solution)/shard_map/ppermute | solution.py:44
  79.6 9.9 %collective-permute-start.30 = (bf16[128,256]{1,0:T(8,128)(2,1)S(1)}, bf16[128,256]{1,0:T(8,128)(2,1)S(1)}, u32[]{:S(2)}, u32[]{:S(2)}) collective-permute-start(bf16[128,256]{1,0:T(8,128)(2,1)S(1)} %shard_map.92.gq_ref.refs_0_), channel_id=1, source_target_pairs={{0,3},{1,0},{2,1},{3,2},{4,7},{5,4},{6,5},{7,6},{8,11},{9,8},{10,9... | collective-permute-start | bytes 196616 | tf_op jit(solution)/shard_map/ppermute | solution.py:44
  79.6 4.9 %collective-permute-start.34 = (bf16[128,128]{1,0:T(8,128)(2,1)S(1)}, bf16[128,128]{1,0:T(8,128)(2,1)S(1)}, u32[]{:S(2)}, u32[]{:S(2)}) collective-permute-start(bf16[128,128]{1,0:T(8,128)(2,1)S(1)} %get-tuple-element.122), channel_id=1, source_target_pairs={{8,0},{12,4},{16,8},{20,12},{24,16},{28,20},{9,1},{13,5},{17,9},{2... | collective-permute-start | bytes 98312 | tf_op jit(solution)/shard_map/ppermute | solution.py:37
  80.9 7.6 %collective-permute-start.35 = (bf16[128,128]{1,0:T(8,128)(2,1)S(1)}, bf16[128,128]{1,0:T(8,128)(2,1)S(1)}, u32[]{:S(2)}, u32[]{:S(2)}) collective-permute-start(bf16[128,128]{1,0:T(8,128)(2,1)S(1)} %get-tuple-element.123), channel_id=1, source_target_pairs={{12,0},{16,4},{20,8},{24,12},{28,16},{13,1},{17,5},{21,9},{25,13},... | collective-permute-start | bytes 98312 | tf_op jit(solution)/shard_map/ppermute | solution.py:37
  82.2 7.3 %collective-permute-start.36 = (bf16[128,128]{1,0:T(8,128)(2,1)S(1)}, bf16[128,128]{1,0:T(8,128)(2,1)S(1)}, u32[]{:S(2)}, u32[]{:S(2)}) collective-permute-start(bf16[128,128]{1,0:T(8,128)(2,1)S(1)} %get-tuple-element.124), channel_id=1, source_target_pairs={{16,0},{20,4},{24,8},{28,12},{17,1},{21,5},{25,9},{29,13},{18,2},{... | collective-permute-start | bytes 98312 | tf_op jit(solution)/shard_map/ppermute | solution.py:37
  84.5 8.9 %collective-permute-start.32 = (bf16[128,256]{1,0:T(8,128)(2,1)S(1)}, bf16[128,256]{1,0:T(8,128)(2,1)S(1)}, u32[]{:S(2)}, u32[]{:S(2)}) collective-permute-start(bf16[128,256]{1,0:T(8,128)(2,1)S(1)} %shard_map.92.gq_ref.refs_0_), channel_id=1, source_target_pairs={{0,1},{1,2},{2,3},{3,0},{4,5},{5,6},{6,7},{7,4},{8,9},{9,10},{10,1... | collective-permute-start | bytes 196616 | tf_op jit(solution)/shard_map/ppermute | solution.py:44
  89.5 6.7 %copy-start = (bf16[128,2048]{1,0:T(8,128)(2,1)S(1)}, bf16[128,2048]{1,0:T(8,128)(2,1)}, u32[]{:S(2)}) copy-start(bf16[128,2048]{1,0:T(8,128)(2,1)} %refs_14_.1) | copy-start | bytes 1572868
  89.5 6.7 %copy-start.1 = (bf16[128,2048]{1,0:T(8,128)(2,1)S(1)}, bf16[128,2048]{1,0:T(8,128)(2,1)}, u32[]{:S(2)}) copy-start(bf16[128,2048]{1,0:T(8,128)(2,1)} %up_ref.3) | copy-start | bytes 1572868
  89.5 6.7 %copy-start.3 = (f32[2048]{0:T(1024)S(1)}, f32[2048]{0:T(1024)}, u32[]{:S(2)}) copy-start(f32[2048]{0:T(1024)} %param.10) | copy-start | bytes 24580
  89.6 3.8 %collective-permute-start.39 = (bf16[144,128]{1,0:T(8,128)(2,1)S(1)}, bf16[144,128]{1,0:T(8,128)(2,1)S(1)}, u32[]{:S(2)}, u32[]{:S(2)}) collective-permute-start(bf16[144,128]{1,0:T(8,128)(2,1)S(1)} %shard_map.93.refs_4_), channel_id=1, source_target_pairs={{0,1},{1,2},{2,3},{3,0},{4,5},{5,6},{6,7},{7,4},{8,9},{9,10},{10,1... | collective-permute-start | bytes 110600 | tf_op jit(solution)/shard_map/ppermute | solution.py:44
  91.4 3.7 %collective-permute-start.38 = (bf16[144,128]{1,0:T(8,128)(2,1)S(1)}, bf16[144,128]{1,0:T(8,128)(2,1)S(1)}, u32[]{:S(2)}, u32[]{:S(2)}) collective-permute-start(bf16[144,128]{1,0:T(8,128)(2,1)S(1)} %shard_map.93.refs_4_), channel_id=1, source_target_pairs={{0,2},{1,3},{2,0},{3,1},{4,6},{5,7},{6,4},{7,5},{8,10},{9,11},{10,... | collective-permute-start | bytes 110600 | tf_op jit(solution)/shard_map/ppermute | solution.py:44
  93.4 2.8 %collective-permute-start.37 = (bf16[144,128]{1,0:T(8,128)(2,1)S(1)}, bf16[144,128]{1,0:T(8,128)(2,1)S(1)}, u32[]{:S(2)}, u32[]{:S(2)}) collective-permute-start(bf16[144,128]{1,0:T(8,128)(2,1)S(1)} %shard_map.93.refs_4_), channel_id=1, source_target_pairs={{0,3},{1,0},{2,1},{3,2},{4,7},{5,4},{6,5},{7,6},{8,11},{9,8},{10,9... | collective-permute-start | bytes 110600 | tf_op jit(solution)/shard_map/ppermute | solution.py:44
  112.7 4.9 %collective-permute-start.42 = (bf16[128,512]{1,0:T(8,128)(2,1)S(1)}, bf16[128,512]{1,0:T(8,128)(2,1)S(1)}, u32[]{:S(2)}, u32[]{:S(2)}) collective-permute-start(bf16[128,512]{1,0:T(8,128)(2,1)S(1)} %shard_map.95.refs_0_), channel_id=1, source_target_pairs={{0,1},{1,2},{2,3},{3,0},{4,5},{5,6},{6,7},{7,4},{8,9},{9,10},{10,1... | collective-permute-start | bytes 393224 | tf_op jit(solution)/shard_map/ppermute | solution.py:44
  113.2 10.8 %collective-permute-start.41 = (bf16[128,512]{1,0:T(8,128)(2,1)S(1)}, bf16[128,512]{1,0:T(8,128)(2,1)S(1)}, u32[]{:S(2)}, u32[]{:S(2)}) collective-permute-start(bf16[128,512]{1,0:T(8,128)(2,1)S(1)} %shard_map.95.refs_0_), channel_id=1, source_target_pairs={{0,2},{1,3},{2,0},{3,1},{4,6},{5,7},{6,4},{7,5},{8,10},{9,11},{10,... | collective-permute-start | bytes 393224 | tf_op jit(solution)/shard_map/ppermute | solution.py:44
  115.5 12.3 %collective-permute-start.40 = (bf16[128,512]{1,0:T(8,128)(2,1)S(1)}, bf16[128,512]{1,0:T(8,128)(2,1)S(1)}, u32[]{:S(2)}, u32[]{:S(2)}) collective-permute-start(bf16[128,512]{1,0:T(8,128)(2,1)S(1)} %shard_map.95.refs_0_), channel_id=1, source_target_pairs={{0,3},{1,0},{2,1},{3,2},{4,7},{5,4},{6,5},{7,6},{8,11},{9,8},{10,9... | collective-permute-start | bytes 393224 | tf_op jit(solution)/shard_map/ppermute | solution.py:44

commit v4 on v3

--- a/solution.py
+++ b/solution.py
@@ -462,8 +462,8 @@
         )(kt, score)
         arrived = [shifted(term, "seq", -offset - 1) for offset, term in enumerate(terms)]
         ahead = rotated(gq, "head") if split else []
-        if step in (2,):
-            arrived = list(lax.optimization_barrier((tuple(arrived), tuple(ahead[1:1+2])))[0])
+        if step:
+            arrived = list(lax.optimization_barrier((tuple(arrived), tuple(ahead[1 : 1 + (2 if step == 2 else 1)])))[0])
         if not split:
             arrived = list(lax.optimization_barrier((tuple(arrived), near[1]))[0])
         msg = local_call(

time: 130 us -> 132 us (1.015)
  waiting for transfers between devices: 33.5 us -> 37.7 us
  blocking collectives: 13.8 us -> 12 us
    ppermute x16, waiting for transfers between devices: 10.2 us -> 13.1 us  [shifted(): lax.ppermute(value, axis, [(source, source + steps) for source in range(i...]
    all_to_all x1, blocking collectives: 13.8 us -> 12 us  [shards(): totals = lax.all_to_all(totals, ('seq', 'head'), 0, 0)]
    ppermute x21, starting transfers between devices: 27.2 us -> 25.6 us  [rotated(): lax.ppermute(value, axis, [(i, (i - step) % count) for i in range(count)])]
  transfers between devices with their start and end apart: 43 -> 43, of which waited for: 18 -> 19; matrix products, arithmetic and copies ran while one was open for 0% -> 0% of each run, Pallas kernels for 7% -> 7%
where the time goes in v4:
time: 132 us; the launch traced here: 131 us
  starting transfers between devices  64.9 us (49%)
  waiting for transfers between devices  37.7 us (29%)
  Pallas kernels  15.8 us (12%)
  blocking collectives  12 us (9%)
    ppermute x16, starting transfers between devices, shifted(): lax.ppermute(value, axis, [(source, source + steps) for source in range(i...  32.7 us
    ppermute x21, starting transfers between devices, rotated(): lax.ppermute(value, axis, [(i, (i - step) % count) for i in range(count)])  25.6 us
    ppermute x21, waiting for transfers between devices, rotated(): lax.ppermute(value, axis, [(i, (i - step) % count) for i in range(count)])  24.5 us
    ppermute x16, waiting for transfers between devices, shifted(): lax.ppermute(value, axis, [(source, source + steps) for source in range(i...  13.1 us
    all_to_all x1, blocking collectives, shards(): totals = lax.all_to_all(totals, ('seq', 'head'), 0, 0)  12 us
    pallas_call x2, Pallas kernels, shards(): local_call(functools.partial(next_body, heads, parts, scale, step == 1),...  3.82 us
    ppermute x2, starting transfers between devices, doubled(): return near + [lax.ppermute(near[0], axis, pairs)]  3.13 us
    ppermute x3, starting transfers between devices, doubled(): near.append(lax.ppermute(near[0], axis, pairs))  2.72 us
  transfers between devices with their start and end apart: 43, of which 19 were waited for; matrix products, arithmetic and copies ran while one was open for 0% of the time, Pallas kernels for 7%

profile of v4, /device:TPU:9, one launch (start us, length us, event | category | flops | bytes accessed | tf_op | source)
XLA Modules:
  0.0 131.2 jit_solution(2234681382992452903)
XLA Ops:
  0.0 2.2 %shard_map.82 = (bf16[48,2048]{1,0:T(8,128)(2,1)S(1)}, bf16[128,2048]{1,0:T(8,128)(2,1)S(1)}, bf16[128,128]{1,0:T(8,128)(2,1)S(1)}, f32[128,128]{1,0:T(8,128)S(1)}, f32[128,128]{1,0:T(8,128)S(1)}) custom-call(s32[1]{0:T(128)} %bitcast.2.block_ref, bf16[2048,256]{1,0:T(8,128)(2,1)} %qw_ref.3, bf16[2048,128]{1,0:T(8,128)(2,1)} %kvw_ref.1, ...), custom_call_target="tpu_custom_call" | custom-call | flops 75497472 | bytes 1572864 | tf_op jit(solution)/shard_map/pallas_call | solution.py:382
  2.2 1.4 %collective-permute-start.6 = (bf16[48,2048]{1,0:T(8,128)(2,1)S(1)}, bf16[48,2048]{1,0:T(8,128)(2,1)S(1)}, u32[]{:S(2)}, u32[]{:S(2)}) collective-permute-start(bf16[48,2048]{1,0:T(8,128)(2,1)S(1)} %get-tuple-element.91), channel_id=1, source_target_pairs={{0,1},{1,2},{2,3},{3,0},{4,5},{5,6},{6,7},{7,4},{8,9},{9,10},{10,1... | collective-permute-start | bytes 589832 | tf_op jit(solution)/shard_map/ppermute | solution.py:44
  4.6 1.4 %collective-permute-start.4 = (bf16[48,2048]{1,0:T(8,128)(2,1)S(1)}, bf16[48,2048]{1,0:T(8,128)(2,1)S(1)}, u32[]{:S(2)}, u32[]{:S(2)}) collective-permute-start(bf16[48,2048]{1,0:T(8,128)(2,1)S(1)} %get-tuple-element.91), channel_id=1, source_target_pairs={{0,3},{1,0},{2,1},{3,2},{4,7},{5,4},{6,5},{7,6},{8,11},{9,8},{10,9... | collective-permute-start | bytes 589832 | tf_op jit(solution)/shard_map/ppermute | solution.py:44
  6.0 4.5 %collective-permute-start.3 = (bf16[128,128]{1,0:T(8,128)(2,1)S(1)}, bf16[128,128]{1,0:T(8,128)(2,1)S(1)}, u32[]{:S(2)}, u32[]{:S(2)}) collective-permute-start(bf16[128,128]{1,0:T(8,128)(2,1)S(1)} %get-tuple-element.75.refs_4_), channel_id=1, source_target_pairs={{0,4},{4,8},{8,12},{12,16},{16,20},{20,24},{24,28},{1,5},{5,9},{9,... | collective-permute-start | bytes 98312 | tf_op jit(solution)/shard_map/ppermute | solution.py:37
  10.5 3.1 %collective-permute-start.2 = (bf16[128,128]{1,0:T(8,128)(2,1)S(1)}, bf16[128,128]{1,0:T(8,128)(2,1)S(1)}, u32[]{:S(2)}, u32[]{:S(2)}) collective-permute-start(bf16[128,128]{1,0:T(8,128)(2,1)S(1)} %get-tuple-element.75.refs_4_), channel_id=1, source_target_pairs={{0,8},{4,12},{8,16},{12,20},{16,24},{20,28},{1,9},{5,13},{9,17},{1... | collective-permute-start | bytes 98312 | tf_op jit(solution)/shard_map/ppermute | solution.py:37
  13.6 3.0 %collective-permute-start.1 = (bf16[128,128]{1,0:T(8,128)(2,1)S(1)}, bf16[128,128]{1,0:T(8,128)(2,1)S(1)}, u32[]{:S(2)}, u32[]{:S(2)}) collective-permute-start(bf16[128,128]{1,0:T(8,128)(2,1)S(1)} %get-tuple-element.75.refs_4_), channel_id=1, source_target_pairs={{0,12},{4,16},{8,20},{12,24},{16,28},{1,13},{5,17},{9,21},{13,25},... | collective-permute-start | bytes 98312 | tf_op jit(solution)/shard_map/ppermute | solution.py:37
  16.7 2.5 %collective-permute-start = (bf16[128,128]{1,0:T(8,128)(2,1)S(1)}, bf16[128,128]{1,0:T(8,128)(2,1)S(1)}, u32[]{:S(2)}, u32[]{:S(2)}) collective-permute-start(bf16[128,128]{1,0:T(8,128)(2,1)S(1)} %get-tuple-element.75.refs_4_), channel_id=1, source_target_pairs={{0,16},{4,20},{8,24},{12,28},{1,17},{5,21},{9,25},{13,29},{2,18},{... | collective-permute-start | bytes 98312 | tf_op jit(solution)/shard_map/ppermute | solution.py:37
  19.2 2.7 %shard_map.83 = (f32[128,256]{1,0:T(8,128)S(1)}, bf16[64,512]{1,0:T(8,128)(2,1)S(1)}, f32[64,512]{1,0:T(8,128)S(1)}, f32[64,512]{1,0:T(8,128)S(1)}, f32[64,512]{...) custom-call(bf16[128,2048]{1,0:T(8,128)(2,1)S(1)} %get-tuple-element.76.hidden_ref, ...), custom_call_target="tpu_custom_call" | custom-call | flops 402653184 | bytes 4194304 | tf_op jit(solution)/shard_map/pallas_call | solution.py:412
  24.5 2.8 %collective-permute-start.7 = (bf16[128,128]{1,0:T(8,128)(2,1)S(1)}, bf16[128,128]{1,0:T(8,128)(2,1)S(1)}, u32[]{:S(2)}, u32[]{:S(2)}) collective-permute-start(bf16[128,128]{1,0:T(8,128)(2,1)S(1)} %get-tuple-element.94), channel_id=1, source_target_pairs={{4,0},{8,4},{12,8},{16,12},{20,16},{24,20},{28,24},{5,1},{9,5},{13... | collective-permute-start | bytes 98312 | tf_op jit(solution)/shard_map/ppermute | solution.py:37
  27.2 1.3 collective-permute-start.8
  28.5 1.3 collective-permute-start.9
  29.8 1.3 collective-permute-start.10
  32.2 2.9 %collective-permute-done.9.refs_2_ = bf16[128,128]{1,0:T(8,128)(2,1)S(1)} collective-permute-done((bf16[128,128]{1,0:T(8,128)(2,1)S(1)}, bf16[128,128]{1,0:T(8,128)(2,1)S(1)}, u32[]{:S(2)}, u32[]{:S(2)}) %collective-permute-start.9) | collective-permute-done | bytes 32800 | tf_op jit(solution)/shard_map/ppermute | solution.py:37
  36.0 1.8 %collective-permute-start.15 = (bf16[2,4,48,256]{3,2,1,0:T(8,128)(2,1)S(1)}, bf16[2,4,48,256]{3,2,1,0:T(8,128)(2,1)S(1)}, u32[]{:S(2)}, u32[]{:S(2)}) collective-permute-start(bf16[2,4,48,256]{3,2,1,0:T(8,128)(2,1)S(1)} %constant_dynamic-update-slice_fusion), channel_id=1, source_target_pairs={{0,8},{4,12},{8,0},{12,4},{16,24},{20,28},{24,16},{28,20},{1,9},{5... | collective-permute-start | bytes 589832 | tf_op jit(solution)/shard_map/ppermute | solution.py:58
  39.3 3.1 %collective-permute-start.13 = (bf16[144,384]{1,0:T(8,128)(2,1)S(1)}, bf16[144,384]{1,0:T(8,128)(2,1)S(1)}, u32[]{:S(2)}, u32[]{:S(2)}) collective-permute-start(bf16[144,384]{1,0:T(8,128)(2,1)S(1)} %shard_map.87.refs_0_), channel_id=1, source_target_pairs={{0,2},{1,3},{2,0},{3,1},{4,6},{5,7},{6,4},{7,5},{8,10},{9,11},{10,... | collective-permute-start | bytes 331784 | tf_op jit(solution)/shard_map/ppermute | solution.py:44
  42.5 1.4 %collective-permute-start.16 = (bf16[4,4,48,256]{3,2,1,0:T(8,128)(2,1)S(1)}, bf16[4,4,48,256]{3,2,1,0:T(8,128)(2,1)S(1)}, u32[]{:S(2)}, u32[]{:S(2)}) collective-permute-start(bf16[4,4,48,256]{3,2,1,0:T(8,128)(2,1)S(1)} %constant_dynamic-update-slice_fusion.2.refs_10_), channel_id=1, source_target_pairs={{0,4},{4,0},{8,12},{12,8},{16,20},{20,16},{24,28},{28,24},{1,5},{5... | collective-permute-start | bytes 1179656 | tf_op jit(solution)/shard_map/ppermute | solution.py:57
  43.9 1.6 %collective-permute-done.14.refs_3_ = bf16[144,384]{1,0:T(8,128)(2,1)S(1)} collective-permute-done((bf16[144,384]{1,0:T(8,128)(2,1)S(1)}, bf16[144,384]{1,0:T(8,128)(2,1)S(1)}, u32[]{:S(2)}, u32[]{:S(2)}) %collective-permute-start.14) | collective-permute-done | bytes 110624 | tf_op jit(solution)/shard_map/ppermute | solution.py:44
  45.5 2.9 %collective-permute-done.13.refs_2_ = bf16[144,384]{1,0:T(8,128)(2,1)S(1)} collective-permute-done((bf16[144,384]{1,0:T(8,128)(2,1)S(1)}, bf16[144,384]{1,0:T(8,128)(2,1)S(1)}, u32[]{:S(2)}, u32[]{:S(2)}) %collective-permute-start.13) | collective-permute-done | bytes 110624 | tf_op jit(solution)/shard_map/ppermute | solution.py:44
  49.4 1.9 %shard_map.88 = (bf16[640,512]{1,0:T(8,128)(2,1)S(1)}, f32[128,128]{1,0:T(8,128)S(1)}, bf16[4,128,384]{2,1,0:T(8,128)(2,1)S(1)}, f32[16,128]{1,0:T(8,128)S(1)}, ...) custom-call(s32[2]{0:T(128)S(1)} %pad_add_fusion.spot_ref, ...), custom_call_target="tpu_custom_call" | custom-call | flops 226492416 | bytes 1441792 | tf_op jit(solution)/shard_map/pallas_call | solution.py:495
  51.3 3.3 %collective-permute-start.20 = (bf16[128,128]{1,0:T(8,128)(2,1)S(1)}, bf16[128,128]{1,0:T(8,128)(2,1)S(1)}, u32[]{:S(2)}, u32[]{:S(2)}) collective-permute-start(bf16[128,128]{1,0:T(8,128)(2,1)S(1)} %get-tuple-element.112), channel_id=1, source_target_pairs={{4,0},{8,4},{12,8},{16,12},{20,16},{24,20},{28,24},{5,1},{9,5},{13... | collective-permute-start | bytes 98312 | tf_op jit(solution)/shard_map/ppermute | solution.py:37
  54.9 1.9 %collective-permute-start.17 = (bf16[128,256]{1,0:T(8,128)(2,1)S(1)}, bf16[128,256]{1,0:T(8,128)(2,1)S(1)}, u32[]{:S(2)}, u32[]{:S(2)}) collective-permute-start(bf16[128,256]{1,0:T(8,128)(2,1)S(1)} %shard_map.89.gq_ref.refs_0_), channel_id=1, source_target_pairs={{0,3},{1,0},{2,1},{3,2},{4,7},{5,4},{6,5},{7,6},{8,11},{9,8},{10,9... | collective-permute-start | bytes 196616 | tf_op jit(solution)/shard_map/ppermute | solution.py:44
  58.1 1.3 collective-permute-start.22
  59.6 1.3 collective-permute-start.23
  62.0 2.8 %collective-permute-done.22.refs_2_ = bf16[128,128]{1,0:T(8,128)(2,1)S(1)} collective-permute-done((bf16[128,128]{1,0:T(8,128)(2,1)S(1)}, bf16[128,128]{1,0:T(8,128)(2,1)S(1)}, u32[]{:S(2)}, u32[]{:S(2)}) %collective-permute-start.22) | collective-permute-done | bytes 32800 | tf_op jit(solution)/shard_map/ppermute | solution.py:37
  66.1 2.5 %collective-permute-start.26 = (bf16[144,128]{1,0:T(8,128)(2,1)S(1)}, bf16[144,128]{1,0:T(8,128)(2,1)S(1)}, u32[]{:S(2)}, u32[]{:S(2)}) collective-permute-start(bf16[144,128]{1,0:T(8,128)(2,1)S(1)} %shard_map.90.refs_4_), channel_id=1, source_target_pairs={{0,1},{1,2},{2,3},{3,0},{4,5},{5,6},{6,7},{7,4},{8,9},{9,10},{10,1... | collective-permute-start | bytes 110600 | tf_op jit(solution)/shard_map/ppermute | solution.py:44
  68.6 1.6 %collective-permute-start.25 = (bf16[144,128]{1,0:T(8,128)(2,1)S(1)}, bf16[144,128]{1,0:T(8,128)(2,1)S(1)}, u32[]{:S(2)}, u32[]{:S(2)}) collective-permute-start(bf16[144,128]{1,0:T(8,128)(2,1)S(1)} %shard_map.90.refs_4_), channel_id=1, source_target_pairs={{0,2},{1,3},{2,0},{3,1},{4,6},{5,7},{6,4},{7,5},{8,10},{9,11},{10,... | collective-permute-start | bytes 110600 | tf_op jit(solution)/shard_map/ppermute | solution.py:44
  70.3 2.0 %collective-permute-done.25.refs_6_ = bf16[144,128]{1,0:T(8,128)(2,1)S(1)} collective-permute-done((bf16[144,128]{1,0:T(8,128)(2,1)S(1)}, bf16[144,128]{1,0:T(8,128)(2,1)S(1)}, u32[]{:S(2)}, u32[]{:S(2)}) %collective-permute-start.25) | collective-permute-done | bytes 36896 | tf_op jit(solution)/shard_map/ppermute | solution.py:44
  72.3 2.0 %collective-permute-done.24.refs_5_ = bf16[144,128]{1,0:T(8,128)(2,1)S(1)} collective-permute-done((bf16[144,128]{1,0:T(8,128)(2,1)S(1)}, bf16[144,128]{1,0:T(8,128)(2,1)S(1)}, u32[]{:S(2)}, u32[]{:S(2)}) %collective-permute-start.24) | collective-permute-done | bytes 36896 | tf_op jit(solution)/shard_map/ppermute | solution.py:44
  74.4 1.8 %collective-permute-start.29 = (bf16[4,4,48,512]{3,2,1,0:T(8,128)(2,1)S(1)}, bf16[4,4,48,512]{3,2,1,0:T(8,128)(2,1)S(1)}, u32[]{:S(2)}, u32[]{:S(2)}) collective-permute-start(bf16[4,4,48,512]{3,2,1,0:T(8,128)(2,1)S(1)} %constant_dynamic-update-slice_fusion.6.refs_12_), channel_id=1, source_target_pairs={{0,4},{4,0},{8,12},{12,8},{16,20},{20,16},{24,28},{28,24},{1,5},{5... | collective-permute-start | bytes 2359304 | tf_op jit(solution)/shard_map/ppermute | solution.py:57
  76.1 1.9 %shard_map.91 = (bf16[640,512]{1,0:T(8,128)(2,1)S(1)}, f32[128,128]{1,0:T(8,128)S(1)}, bf16[4,128,384]{2,1,0:T(8,128)(2,1)S(1)}, f32[16,128]{1,0:T(8,128)S(1)}, ...) custom-call(s32[2]{0:T(128)S(1)} %pad_add_fusion.spot_ref, ...), custom_call_target="tpu_custom_call" | custom-call | flops 226492416 | bytes 1441792 | tf_op jit(solution)/shard_map/pallas_call | solution.py:495
  78.0 1.9 %collective-permute-start.33 = (bf16[128,128]{1,0:T(8,128)(2,1)S(1)}, bf16[128,128]{1,0:T(8,128)(2,1)S(1)}, u32[]{:S(2)}, u32[]{:S(2)}) collective-permute-start(bf16[128,128]{1,0:T(8,128)(2,1)S(1)} %get-tuple-element.129), channel_id=1, source_target_pairs={{4,0},{8,4},{12,8},{16,12},{20,16},{24,20},{28,24},{5,1},{9,5},{13... | collective-permute-start | bytes 98312 | tf_op jit(solution)/shard_map/ppermute | solution.py:37
  80.3 1.6 %collective-permute-start.31 = (bf16[128,256]{1,0:T(8,128)(2,1)S(1)}, bf16[128,256]{1,0:T(8,128)(2,1)S(1)}, u32[]{:S(2)}, u32[]{:S(2)}) collective-permute-start(bf16[128,256]{1,0:T(8,128)(2,1)S(1)} %shard_map.92.gq_ref.refs_0_), channel_id=1, source_target_pairs={{0,2},{1,3},{2,0},{3,1},{4,6},{5,7},{6,4},{7,5},{8,10},{9,11},{10,... | collective-permute-start | bytes 196616 | tf_op jit(solution)/shard_map/ppermute | solution.py:44
  81.9 1.3 collective-permute-start.34
  83.2 1.3 collective-permute-start.35
  84.5 1.3 collective-permute-start.36
  86.7 1.3 %collective-permute-start.32 = (bf16[128,256]{1,0:T(8,128)(2,1)S(1)}, bf16[128,256]{1,0:T(8,128)(2,1)S(1)}, u32[]{:S(2)}, u32[]{:S(2)}) collective-permute-start(bf16[128,256]{1,0:T(8,128)(2,1)S(1)} %shard_map.92.gq_ref.refs_0_), channel_id=1, source_target_pairs={{0,1},{1,2},{2,3},{3,0},{4,5},{5,6},{6,7},{7,4},{8,9},{9,10},{10,1... | collective-permute-start | bytes 196616 | tf_op jit(solution)/shard_map/ppermute | solution.py:44
  88.0 2.8 %collective-permute-done.35.refs_2_ = bf16[128,128]{1,0:T(8,128)(2,1)S(1)} collective-permute-done((bf16[128,128]{1,0:T(8,128)(2,1)S(1)}, bf16[128,128]{1,0:T(8,128)(2,1)S(1)}, u32[]{:S(2)}, u32[]{:S(2)}) %collective-permute-start.35) | collective-permute-done | bytes 32800 | tf_op jit(solution)/shard_map/ppermute | solution.py:37
  91.7 2.1 %collective-permute-start.39 = (bf16[144,128]{1,0:T(8,128)(2,1)S(1)}, bf16[144,128]{1,0:T(8,128)(2,1)S(1)}, u32[]{:S(2)}, u32[]{:S(2)}) collective-permute-start(bf16[144,128]{1,0:T(8,128)(2,1)S(1)} %shard_map.93.refs_4_), channel_id=1, source_target_pairs={{0,1},{1,2},{2,3},{3,0},{4,5},{5,6},{6,7},{7,4},{8,9},{9,10},{10,1... | collective-permute-start | bytes 110600 | tf_op jit(solution)/shard_map/ppermute | solution.py:44
  93.8 2.3 %collective-permute-start.38 = (bf16[144,128]{1,0:T(8,128)(2,1)S(1)}, bf16[144,128]{1,0:T(8,128)(2,1)S(1)}, u32[]{:S(2)}, u32[]{:S(2)}) collective-permute-start(bf16[144,128]{1,0:T(8,128)(2,1)S(1)} %shard_map.93.refs_4_), channel_id=1, source_target_pairs={{0,2},{1,3},{2,0},{3,1},{4,6},{5,7},{6,4},{7,5},{8,10},{9,11},{10,... | collective-permute-start | bytes 110600 | tf_op jit(solution)/shard_map/ppermute | solution.py:44
  96.1 1.7 %collective-permute-done.38.refs_6_ = bf16[144,128]{1,0:T(8,128)(2,1)S(1)} collective-permute-done((bf16[144,128]{1,0:T(8,128)(2,1)S(1)}, bf16[144,128]{1,0:T(8,128)(2,1)S(1)}, u32[]{:S(2)}, u32[]{:S(2)}) %collective-permute-start.38) | collective-permute-done | bytes 36896 | tf_op jit(solution)/shard_map/ppermute | solution.py:44
  97.8 2.0 %collective-permute-done.37.refs_5_ = bf16[144,128]{1,0:T(8,128)(2,1)S(1)} collective-permute-done((bf16[144,128]{1,0:T(8,128)(2,1)S(1)}, bf16[144,128]{1,0:T(8,128)(2,1)S(1)}, u32[]{:S(2)}, u32[]{:S(2)}) %collective-permute-start.37) | collective-permute-done | bytes 36896 | tf_op jit(solution)/shard_map/ppermute | solution.py:44
  99.9 1.9 %shard_map.94 = (f32[3,128,512]{2,1,0:T(8,128)S(1)}, f32[32,8,128]{2,1,0:T(8,128)S(1)}) custom-call(s32[2]{0:T(128)S(1)} %pad_add_fusion.spot_ref, bf16[128,256]{1,0:T(8,128)(2,1)S(1)} %shard_map.92.gq_ref.refs_0_, bf16[128,256]{1,0:T(8,128)(2,1)S(1)} %collective-permute-done.30.refs_1_, bf16[128,256]{1,0:T(8,128)(2,1)S(1)} %collective-permute-done.31.refs_2_, ...), custom_call_target="tpu_custom_call" | custom-call | flops 603979776 | bytes 1572864 | tf_op jit(solution)/shard_map/pallas_call | solution.py:534
  101.7 12.0 %all_to_all.5.tot_ref = f32[32,8,128]{2,1,0:T(8,128)S(1)} all-to-all(f32[32,8,128]{2,1,0:T(8,128)S(1)} %get-tuple-element.143), channel_id=1, replica_groups=mesh['seq'=8,'head'=4] {'seq','head'}, dimensions={0} | all-to-all | bytes 262144 | tf_op jit(solution)/shard_map/all_to_all | solution.py:550
  115.1 2.2 %collective-permute-start.41 = (bf16[128,512]{1,0:T(8,128)(2,1)S(1)}, bf16[128,512]{1,0:T(8,128)(2,1)S(1)}, u32[]{:S(2)}, u32[]{:S(2)}) collective-permute-start(bf16[128,512]{1,0:T(8,128)(2,1)S(1)} %shard_map.95.refs_0_), channel_id=1, source_target_pairs={{0,2},{1,3},{2,0},{3,1},{4,6},{5,7},{6,4},{7,5},{8,10},{9,11},{10,... | collective-permute-start | bytes 393224 | tf_op jit(solution)/shard_map/ppermute | solution.py:44
  117.3 2.2 %collective-permute-done.42.refs_3_ = bf16[128,512]{1,0:T(8,128)(2,1)S(1)} collective-permute-done((bf16[128,512]{1,0:T(8,128)(2,1)S(1)}, bf16[128,512]{1,0:T(8,128)(2,1)S(1)}, u32[]{:S(2)}, u32[]{:S(2)}) %collective-permute-start.42) | collective-permute-done | bytes 131104 | tf_op jit(solution)/shard_map/ppermute | solution.py:44
  119.5 6.4 %collective-permute-done.41.refs_2_ = bf16[128,512]{1,0:T(8,128)(2,1)S(1)} collective-permute-done((bf16[128,512]{1,0:T(8,128)(2,1)S(1)}, bf16[128,512]{1,0:T(8,128)(2,1)S(1)}, u32[]{:S(2)}, u32[]{:S(2)}) %collective-permute-start.41) | collective-permute-done | bytes 131104 | tf_op jit(solution)/shard_map/ppermute | solution.py:44
  125.9 3.7 %collective-permute-done.40.refs_1_ = bf16[128,512]{1,0:T(8,128)(2,1)S(1)} collective-permute-done((bf16[128,512]{1,0:T(8,128)(2,1)S(1)}, bf16[128,512]{1,0:T(8,128)(2,1)S(1)}, u32[]{:S(2)}, u32[]{:S(2)}) %collective-permute-start.40) | collective-permute-done | bytes 131104 | tf_op jit(solution)/shard_map/ppermute | solution.py:44
  129.6 1.6 %shard_map.96 = f32[128,2048]{1,0:T(8,128)} custom-call(s32[2]{0:T(128)S(1)} %pad_add_fusion.spot_ref, bf16[128,512]{1,0:T(8,128)(2,1)S(1)} %shard_map.95.refs_0_, bf16[128,512]{1,0:T(8,128)(2,1)S(1)} %collective-permute-done.40.refs_1_, bf16[128,512]{1,0:T(8,128)(2,1)S(1)} %collective-permute-done.41.refs_2_, ...), custom_call_target="tpu_custom_call" | custom-call | bytes 1572864 | tf_op jit(solution)/shard_map/pallas_call | solution.py:562
  (73 shorter events, 15.9 us)
Async XLA Ops:
  0.0 19.2 %copy-start.2 = (bf16[2048,256]{1,0:T(8,128)(2,1)S(1)}, bf16[2048,256]{1,0:T(8,128)(2,1)}, u32[]{:S(2)}) copy-start(bf16[2048,256]{1,0:T(8,128)(2,1)} %qw_ref.3) | copy-start | bytes 3145732
  2.2 20.9 %collective-permute-start.6 = (bf16[48,2048]{1,0:T(8,128)(2,1)S(1)}, bf16[48,2048]{1,0:T(8,128)(2,1)S(1)}, u32[]{:S(2)}, u32[]{:S(2)}) collective-permute-start(bf16[48,2048]{1,0:T(8,128)(2,1)S(1)} %get-tuple-element.91), channel_id=1, source_target_pairs={{0,1},{1,2},{2,3},{3,0},{4,5},{5,6},{6,7},{7,4},{8,9},{9,10},{10,1... | collective-permute-start | bytes 589832 | tf_op jit(solution)/shard_map/ppermute | solution.py:44
  3.5 19.6 %collective-permute-start.5 = (bf16[48,2048]{1,0:T(8,128)(2,1)S(1)}, bf16[48,2048]{1,0:T(8,128)(2,1)S(1)}, u32[]{:S(2)}, u32[]{:S(2)}) collective-permute-start(bf16[48,2048]{1,0:T(8,128)(2,1)S(1)} %get-tuple-element.91), channel_id=1, source_target_pairs={{0,2},{1,3},{2,0},{3,1},{4,6},{5,7},{6,4},{7,5},{8,10},{9,11},{10,... | collective-permute-start | bytes 589832 | tf_op jit(solution)/shard_map/ppermute | solution.py:44
  4.6 18.5 %collective-permute-start.4 = (bf16[48,2048]{1,0:T(8,128)(2,1)S(1)}, bf16[48,2048]{1,0:T(8,128)(2,1)S(1)}, u32[]{:S(2)}, u32[]{:S(2)}) collective-permute-start(bf16[48,2048]{1,0:T(8,128)(2,1)S(1)} %get-tuple-element.91), channel_id=1, source_target_pairs={{0,3},{1,0},{2,1},{3,2},{4,7},{5,4},{6,5},{7,6},{8,11},{9,8},{10,9... | collective-permute-start | bytes 589832 | tf_op jit(solution)/shard_map/ppermute | solution.py:44
  6.0 7.6 %collective-permute-start.3 = (bf16[128,128]{1,0:T(8,128)(2,1)S(1)}, bf16[128,128]{1,0:T(8,128)(2,1)S(1)}, u32[]{:S(2)}, u32[]{:S(2)}) collective-permute-start(bf16[128,128]{1,0:T(8,128)(2,1)S(1)} %get-tuple-element.75.refs_4_), channel_id=1, source_target_pairs={{0,4},{4,8},{8,12},{12,16},{16,20},{20,24},{24,28},{1,5},{5,9},{9,... | collective-permute-start | bytes 98312 | tf_op jit(solution)/shard_map/ppermute | solution.py:37
  10.5 6.1 %collective-permute-start.2 = (bf16[128,128]{1,0:T(8,128)(2,1)S(1)}, bf16[128,128]{1,0:T(8,128)(2,1)S(1)}, u32[]{:S(2)}, u32[]{:S(2)}) collective-permute-start(bf16[128,128]{1,0:T(8,128)(2,1)S(1)} %get-tuple-element.75.refs_4_), channel_id=1, source_target_pairs={{0,8},{4,12},{8,16},{12,20},{16,24},{20,28},{1,9},{5,13},{9,17},{1... | collective-permute-start | bytes 98312 | tf_op jit(solution)/shard_map/ppermute | solution.py:37
  13.6 8.3 %collective-permute-start.1 = (bf16[128,128]{1,0:T(8,128)(2,1)S(1)}, bf16[128,128]{1,0:T(8,128)(2,1)S(1)}, u32[]{:S(2)}, u32[]{:S(2)}) collective-permute-start(bf16[128,128]{1,0:T(8,128)(2,1)S(1)} %get-tuple-element.75.refs_4_), channel_id=1, source_target_pairs={{0,12},{4,16},{8,20},{12,24},{16,28},{1,13},{5,17},{9,21},{13,25},... | collective-permute-start | bytes 98312 | tf_op jit(solution)/shard_map/ppermute | solution.py:37
  16.7 5.2 %collective-permute-start = (bf16[128,128]{1,0:T(8,128)(2,1)S(1)}, bf16[128,128]{1,0:T(8,128)(2,1)S(1)}, u32[]{:S(2)}, u32[]{:S(2)}) collective-permute-start(bf16[128,128]{1,0:T(8,128)(2,1)S(1)} %get-tuple-element.75.refs_4_), channel_id=1, source_target_pairs={{0,16},{4,20},{8,24},{12,28},{1,17},{5,21},{9,25},{13,29},{2,18},{... | collective-permute-start | bytes 98312 | tf_op jit(solution)/shard_map/ppermute | solution.py:37
  23.7 12.1 %collective-permute-start.11 = (bf16[1,4,48,256]{3,2,1,0:T(8,128)(2,1)S(1)}, bf16[1,4,48,256]{3,2,1,0:T(8,128)(2,1)S(1)}, u32[]{:S(2)}, u32[]{:S(2)}) collective-permute-start(bf16[1,4,48,256]{3,2,1,0:T(8,128)(2,1)S(1)} %bitcast.14), channel_id=1, source_target_pairs={{0,16},{4,20},{8,24},{12,28},{16,0},{20,4},{24,8},{28,12},{1,17},{... | collective-permute-start | bytes 294920 | tf_op jit(solution)/shard_map/ppermute | solution.py:522
  24.5 7.0 %collective-permute-start.7 = (bf16[128,128]{1,0:T(8,128)(2,1)S(1)}, bf16[128,128]{1,0:T(8,128)(2,1)S(1)}, u32[]{:S(2)}, u32[]{:S(2)}) collective-permute-start(bf16[128,128]{1,0:T(8,128)(2,1)S(1)} %get-tuple-element.94), channel_id=1, source_target_pairs={{4,0},{8,4},{12,8},{16,12},{20,16},{24,20},{28,24},{5,1},{9,5},{13... | collective-permute-start | bytes 98312 | tf_op jit(solution)/shard_map/ppermute | solution.py:37
  27.2 5.0 %collective-permute-start.8 = (bf16[128,128]{1,0:T(8,128)(2,1)S(1)}, bf16[128,128]{1,0:T(8,128)(2,1)S(1)}, u32[]{:S(2)}, u32[]{:S(2)}) collective-permute-start(bf16[128,128]{1,0:T(8,128)(2,1)S(1)} %get-tuple-element.95), channel_id=1, source_target_pairs={{8,0},{12,4},{16,8},{20,12},{24,16},{28,20},{9,1},{13,5},{17,9},{2... | collective-permute-start | bytes 98312 | tf_op jit(solution)/shard_map/ppermute | solution.py:37
  28.5 6.6 %collective-permute-start.9 = (bf16[128,128]{1,0:T(8,128)(2,1)S(1)}, bf16[128,128]{1,0:T(8,128)(2,1)S(1)}, u32[]{:S(2)}, u32[]{:S(2)}) collective-permute-start(bf16[128,128]{1,0:T(8,128)(2,1)S(1)} %get-tuple-element.96), channel_id=1, source_target_pairs={{12,0},{16,4},{20,8},{24,12},{28,16},{13,1},{17,5},{21,9},{25,13},... | collective-permute-start | bytes 98312 | tf_op jit(solution)/shard_map/ppermute | solution.py:37
  29.8 6.0 %collective-permute-start.10 = (bf16[128,128]{1,0:T(8,128)(2,1)S(1)}, bf16[128,128]{1,0:T(8,128)(2,1)S(1)}, u32[]{:S(2)}, u32[]{:S(2)}) collective-permute-start(bf16[128,128]{1,0:T(8,128)(2,1)S(1)} %get-tuple-element.97), channel_id=1, source_target_pairs={{16,0},{20,4},{24,8},{28,12},{17,1},{21,5},{25,9},{29,13},{18,2},{... | collective-permute-start | bytes 98312 | tf_op jit(solution)/shard_map/ppermute | solution.py:37
  36.0 6.5 %collective-permute-start.15 = (bf16[2,4,48,256]{3,2,1,0:T(8,128)(2,1)S(1)}, bf16[2,4,48,256]{3,2,1,0:T(8,128)(2,1)S(1)}, u32[]{:S(2)}, u32[]{:S(2)}) collective-permute-start(bf16[2,4,48,256]{3,2,1,0:T(8,128)(2,1)S(1)} %constant_dynamic-update-slice_fusion), channel_id=1, source_target_pairs={{0,8},{4,12},{8,0},{12,4},{16,24},{20,28},{24,16},{28,20},{1,9},{5... | collective-permute-start | bytes 589832 | tf_op jit(solution)/shard_map/ppermute | solution.py:58
  37.8 4.7 %collective-permute-start.12 = (bf16[144,384]{1,0:T(8,128)(2,1)S(1)}, bf16[144,384]{1,0:T(8,128)(2,1)S(1)}, u32[]{:S(2)}, u32[]{:S(2)}) collective-permute-start(bf16[144,384]{1,0:T(8,128)(2,1)S(1)} %shard_map.87.refs_0_), channel_id=1, source_target_pairs={{0,3},{1,0},{2,1},{3,2},{4,7},{5,4},{6,5},{7,6},{8,11},{9,8},{10,9... | collective-permute-start | bytes 331784 | tf_op jit(solution)/shard_map/ppermute | solution.py:44
  38.9 6.5 %collective-permute-start.14 = (bf16[144,384]{1,0:T(8,128)(2,1)S(1)}, bf16[144,384]{1,0:T(8,128)(2,1)S(1)}, u32[]{:S(2)}, u32[]{:S(2)}) collective-permute-start(bf16[144,384]{1,0:T(8,128)(2,1)S(1)} %shard_map.87.refs_0_), channel_id=1, source_target_pairs={{0,1},{1,2},{2,3},{3,0},{4,5},{5,6},{6,7},{7,4},{8,9},{9,10},{10,1... | collective-permute-start | bytes 331784 | tf_op jit(solution)/shard_map/ppermute | solution.py:44
  39.3 9.0 %collective-permute-start.13 = (bf16[144,384]{1,0:T(8,128)(2,1)S(1)}, bf16[144,384]{1,0:T(8,128)(2,1)S(1)}, u32[]{:S(2)}, u32[]{:S(2)}) collective-permute-start(bf16[144,384]{1,0:T(8,128)(2,1)S(1)} %shard_map.87.refs_0_), channel_id=1, source_target_pairs={{0,2},{1,3},{2,0},{3,1},{4,6},{5,7},{6,4},{7,5},{8,10},{9,11},{10,... | collective-permute-start | bytes 331784 | tf_op jit(solution)/shard_map/ppermute | solution.py:44
  42.5 5.8 %collective-permute-start.27 = (bf16[1,4,48,512]{3,2,1,0:T(8,128)(2,1)S(1)}, bf16[1,4,48,512]{3,2,1,0:T(8,128)(2,1)S(1)}, u32[]{:S(2)}, u32[]{:S(2)}) collective-permute-start(bf16[1,4,48,512]{3,2,1,0:T(8,128)(2,1)S(1)} %dynamic-slice_bitcast_fusion), channel_id=1, source_target_pairs={{0,16},{4,20},{8,24},{12,28},{16,0},{20,4},{24,8},{28,12},{1,17},{... | collective-permute-start | bytes 589832 | tf_op jit(solution)/shard_map/ppermute | solution.py:58
  42.5 6.8 %collective-permute-start.16 = (bf16[4,4,48,256]{3,2,1,0:T(8,128)(2,1)S(1)}, bf16[4,4,48,256]{3,2,1,0:T(8,128)(2,1)S(1)}, u32[]{:S(2)}, u32[]{:S(2)}) collective-permute-start(bf16[4,4,48,256]{3,2,1,0:T(8,128)(2,1)S(1)} %constant_dynamic-update-slice_fusion.2.refs_10_), channel_id=1, source_target_pairs={{0,4},{4,0},{8,12},{12,8},{16,20},{20,16},{24,28},{28,24},{1,5},{5... | collective-permute-start | bytes 1179656 | tf_op jit(solution)/shard_map/ppermute | solution.py:57
  48.4 21.9 %collective-permute-start.28 = (bf16[2,4,48,512]{3,2,1,0:T(8,128)(2,1)S(1)}, bf16[2,4,48,512]{3,2,1,0:T(8,128)(2,1)S(1)}, u32[]{:S(2)}, u32[]{:S(2)}) collective-permute-start(bf16[2,4,48,512]{3,2,1,0:T(8,128)(2,1)S(1)} %constant_dynamic-update-slice_fusion.4), channel_id=1, source_target_pairs={{0,8},{4,12},{8,0},{12,4},{16,24},{20,28},{24,16},{28,20},{1,9},{5... | collective-permute-start | bytes 1179656 | tf_op jit(solution)/shard_map/ppermute | solution.py:58
  51.3 8.3 %collective-permute-start.20 = (bf16[128,128]{1,0:T(8,128)(2,1)S(1)}, bf16[128,128]{1,0:T(8,128)(2,1)S(1)}, u32[]{:S(2)}, u32[]{:S(2)}) collective-permute-start(bf16[128,128]{1,0:T(8,128)(2,1)S(1)} %get-tuple-element.112), channel_id=1, source_target_pairs={{4,0},{8,4},{12,8},{16,12},{20,16},{24,20},{28,24},{5,1},{9,5},{13... | collective-permute-start | bytes 98312 | tf_op jit(solution)/shard_map/ppermute | solution.py:37
  54.9 11.1 %collective-permute-start.17 = (bf16[128,256]{1,0:T(8,128)(2,1)S(1)}, bf16[128,256]{1,0:T(8,128)(2,1)S(1)}, u32[]{:S(2)}, u32[]{:S(2)}) collective-permute-start(bf16[128,256]{1,0:T(8,128)(2,1)S(1)} %shard_map.89.gq_ref.refs_0_), channel_id=1, source_target_pairs={{0,3},{1,0},{2,1},{3,2},{4,7},{5,4},{6,5},{7,6},{8,11},{9,8},{10,9... | collective-permute-start | bytes 196616 | tf_op jit(solution)/shard_map/ppermute | solution.py:44
  56.8 5.2 %collective-permute-start.21 = (bf16[128,128]{1,0:T(8,128)(2,1)S(1)}, bf16[128,128]{1,0:T(8,128)(2,1)S(1)}, u32[]{:S(2)}, u32[]{:S(2)}) collective-permute-start(bf16[128,128]{1,0:T(8,128)(2,1)S(1)} %get-tuple-element.113), channel_id=1, source_target_pairs={{8,0},{12,4},{16,8},{20,12},{24,16},{28,20},{9,1},{13,5},{17,9},{2... | collective-permute-start | bytes 98312 | tf_op jit(solution)/shard_map/ppermute | solution.py:37
  58.1 6.7 %collective-permute-start.22 = (bf16[128,128]{1,0:T(8,128)(2,1)S(1)}, bf16[128,128]{1,0:T(8,128)(2,1)S(1)}, u32[]{:S(2)}, u32[]{:S(2)}) collective-permute-start(bf16[128,128]{1,0:T(8,128)(2,1)S(1)} %get-tuple-element.114), channel_id=1, source_target_pairs={{12,0},{16,4},{20,8},{24,12},{28,16},{13,1},{17,5},{21,9},{25,13},... | collective-permute-start | bytes 98312 | tf_op jit(solution)/shard_map/ppermute | solution.py:37
  59.6 6.4 %collective-permute-start.23 = (bf16[128,128]{1,0:T(8,128)(2,1)S(1)}, bf16[128,128]{1,0:T(8,128)(2,1)S(1)}, u32[]{:S(2)}, u32[]{:S(2)}) collective-permute-start(bf16[128,128]{1,0:T(8,128)(2,1)S(1)} %get-tuple-element.115), channel_id=1, source_target_pairs={{16,0},{20,4},{24,8},{28,12},{17,1},{21,5},{25,9},{29,13},{18,2},{... | collective-permute-start | bytes 98312 | tf_op jit(solution)/shard_map/ppermute | solution.py:37
  62.0 8.2 %collective-permute-start.19 = (bf16[128,256]{1,0:T(8,128)(2,1)S(1)}, bf16[128,256]{1,0:T(8,128)(2,1)S(1)}, u32[]{:S(2)}, u32[]{:S(2)}) collective-permute-start(bf16[128,256]{1,0:T(8,128)(2,1)S(1)} %shard_map.89.gq_ref.refs_0_), channel_id=1, source_target_pairs={{0,1},{1,2},{2,3},{3,0},{4,5},{5,6},{6,7},{7,4},{8,9},{9,10},{10,1... | collective-permute-start | bytes 196616 | tf_op jit(solution)/shard_map/ppermute | solution.py:44
  64.8 5.4 %collective-permute-start.18 = (bf16[128,256]{1,0:T(8,128)(2,1)S(1)}, bf16[128,256]{1,0:T(8,128)(2,1)S(1)}, u32[]{:S(2)}, u32[]{:S(2)}) collective-permute-start(bf16[128,256]{1,0:T(8,128)(2,1)S(1)} %shard_map.89.gq_ref.refs_0_), channel_id=1, source_target_pairs={{0,2},{1,3},{2,0},{3,1},{4,6},{5,7},{6,4},{7,5},{8,10},{9,11},{10,... | collective-permute-start | bytes 196616 | tf_op jit(solution)/shard_map/ppermute | solution.py:44
  66.1 4.1 %collective-permute-start.26 = (bf16[144,128]{1,0:T(8,128)(2,1)S(1)}, bf16[144,128]{1,0:T(8,128)(2,1)S(1)}, u32[]{:S(2)}, u32[]{:S(2)}) collective-permute-start(bf16[144,128]{1,0:T(8,128)(2,1)S(1)} %shard_map.90.refs_4_), channel_id=1, source_target_pairs={{0,1},{1,2},{2,3},{3,0},{4,5},{5,6},{6,7},{7,4},{8,9},{9,10},{10,1... | collective-permute-start | bytes 110600 | tf_op jit(solution)/shard_map/ppermute | solution.py:44
  68.6 3.7 %collective-permute-start.25 = (bf16[144,128]{1,0:T(8,128)(2,1)S(1)}, bf16[144,128]{1,0:T(8,128)(2,1)S(1)}, u32[]{:S(2)}, u32[]{:S(2)}) collective-permute-start(bf16[144,128]{1,0:T(8,128)(2,1)S(1)} %shard_map.90.refs_4_), channel_id=1, source_target_pairs={{0,2},{1,3},{2,0},{3,1},{4,6},{5,7},{6,4},{7,5},{8,10},{9,11},{10,... | collective-permute-start | bytes 110600 | tf_op jit(solution)/shard_map/ppermute | solution.py:44
  70.2 4.1 %collective-permute-start.24 = (bf16[144,128]{1,0:T(8,128)(2,1)S(1)}, bf16[144,128]{1,0:T(8,128)(2,1)S(1)}, u32[]{:S(2)}, u32[]{:S(2)}) collective-permute-start(bf16[144,128]{1,0:T(8,128)(2,1)S(1)} %shard_map.90.refs_4_), channel_id=1, source_target_pairs={{0,3},{1,0},{2,1},{3,2},{4,7},{5,4},{6,5},{7,6},{8,11},{9,8},{10,9... | collective-permute-start | bytes 110600 | tf_op jit(solution)/shard_map/ppermute | solution.py:44
  74.4 5.6 %collective-permute-start.29 = (bf16[4,4,48,512]{3,2,1,0:T(8,128)(2,1)S(1)}, bf16[4,4,48,512]{3,2,1,0:T(8,128)(2,1)S(1)}, u32[]{:S(2)}, u32[]{:S(2)}) collective-permute-start(bf16[4,4,48,512]{3,2,1,0:T(8,128)(2,1)S(1)} %constant_dynamic-update-slice_fusion.6.refs_12_), channel_id=1, source_target_pairs={{0,4},{4,0},{8,12},{12,8},{16,20},{20,16},{24,28},{28,24},{1,5},{5... | collective-permute-start | bytes 2359304 | tf_op jit(solution)/shard_map/ppermute | solution.py:57
  78.0 6.5 %collective-permute-start.33 = (bf16[128,128]{1,0:T(8,128)(2,1)S(1)}, bf16[128,128]{1,0:T(8,128)(2,1)S(1)}, u32[]{:S(2)}, u32[]{:S(2)}) collective-permute-start(bf16[128,128]{1,0:T(8,128)(2,1)S(1)} %get-tuple-element.129), channel_id=1, source_target_pairs={{4,0},{8,4},{12,8},{16,12},{20,16},{24,20},{28,24},{5,1},{9,5},{13... | collective-permute-start | bytes 98312 | tf_op jit(solution)/shard_map/ppermute | solution.py:37
  80.3 11.2 %collective-permute-start.31 = (bf16[128,256]{1,0:T(8,128)(2,1)S(1)}, bf16[128,256]{1,0:T(8,128)(2,1)S(1)}, u32[]{:S(2)}, u32[]{:S(2)}) collective-permute-start(bf16[128,256]{1,0:T(8,128)(2,1)S(1)} %shard_map.92.gq_ref.refs_0_), channel_id=1, source_target_pairs={{0,2},{1,3},{2,0},{3,1},{4,6},{5,7},{6,4},{7,5},{8,10},{9,11},{10,... | collective-permute-start | bytes 196616 | tf_op jit(solution)/shard_map/ppermute | solution.py:44
  81.9 9.6 %collective-permute-start.30 = (bf16[128,256]{1,0:T(8,128)(2,1)S(1)}, bf16[128,256]{1,0:T(8,128)(2,1)S(1)}, u32[]{:S(2)}, u32[]{:S(2)}) collective-permute-start(bf16[128,256]{1,0:T(8,128)(2,1)S(1)} %shard_map.92.gq_ref.refs_0_), channel_id=1, source_target_pairs={{0,3},{1,0},{2,1},{3,2},{4,7},{5,4},{6,5},{7,6},{8,11},{9,8},{10,9... | collective-permute-start | bytes 196616 | tf_op jit(solution)/shard_map/ppermute | solution.py:44
  81.9 4.8 %collective-permute-start.34 = (bf16[128,128]{1,0:T(8,128)(2,1)S(1)}, bf16[128,128]{1,0:T(8,128)(2,1)S(1)}, u32[]{:S(2)}, u32[]{:S(2)}) collective-permute-start(bf16[128,128]{1,0:T(8,128)(2,1)S(1)} %get-tuple-element.130), channel_id=1, source_target_pairs={{8,0},{12,4},{16,8},{20,12},{24,16},{28,20},{9,1},{13,5},{17,9},{2... | collective-permute-start | bytes 98312 | tf_op jit(solution)/shard_map/ppermute | solution.py:37
  83.2 7.6 %collective-permute-start.35 = (bf16[128,128]{1,0:T(8,128)(2,1)S(1)}, bf16[128,128]{1,0:T(8,128)(2,1)S(1)}, u32[]{:S(2)}, u32[]{:S(2)}) collective-permute-start(bf16[128,128]{1,0:T(8,128)(2,1)S(1)} %get-tuple-element.131), channel_id=1, source_target_pairs={{12,0},{16,4},{20,8},{24,12},{28,16},{13,1},{17,5},{21,9},{25,13},... | collective-permute-start | bytes 98312 | tf_op jit(solution)/shard_map/ppermute | solution.py:37
  84.5 7.0 %collective-permute-start.36 = (bf16[128,128]{1,0:T(8,128)(2,1)S(1)}, bf16[128,128]{1,0:T(8,128)(2,1)S(1)}, u32[]{:S(2)}, u32[]{:S(2)}) collective-permute-start(bf16[128,128]{1,0:T(8,128)(2,1)S(1)} %get-tuple-element.132), channel_id=1, source_target_pairs={{16,0},{20,4},{24,8},{28,12},{17,1},{21,5},{25,9},{29,13},{18,2},{... | collective-permute-start | bytes 98312 | tf_op jit(solution)/shard_map/ppermute | solution.py:37
  86.7 9.4 %collective-permute-start.32 = (bf16[128,256]{1,0:T(8,128)(2,1)S(1)}, bf16[128,256]{1,0:T(8,128)(2,1)S(1)}, u32[]{:S(2)}, u32[]{:S(2)}) collective-permute-start(bf16[128,256]{1,0:T(8,128)(2,1)S(1)} %shard_map.92.gq_ref.refs_0_), channel_id=1, source_target_pairs={{0,1},{1,2},{2,3},{3,0},{4,5},{5,6},{6,7},{7,4},{8,9},{9,10},{10,1... | collective-permute-start | bytes 196616 | tf_op jit(solution)/shard_map/ppermute | solution.py:44
  91.5 8.4 %copy-start = (bf16[128,2048]{1,0:T(8,128)(2,1)S(1)}, bf16[128,2048]{1,0:T(8,128)(2,1)}, u32[]{:S(2)}) copy-start(bf16[128,2048]{1,0:T(8,128)(2,1)} %refs_14_.1) | copy-start | bytes 1572868
  91.5 8.4 %copy-start.1 = (bf16[128,2048]{1,0:T(8,128)(2,1)S(1)}, bf16[128,2048]{1,0:T(8,128)(2,1)}, u32[]{:S(2)}) copy-start(bf16[128,2048]{1,0:T(8,128)(2,1)} %up_ref.3) | copy-start | bytes 1572868
  91.5 8.3 %copy-start.3 = (f32[2048]{0:T(1024)S(1)}, f32[2048]{0:T(1024)}, u32[]{:S(2)}) copy-start(f32[2048]{0:T(1024)} %param.10) | copy-start | bytes 24580
  91.7 4.4 %collective-permute-start.39 = (bf16[144,128]{1,0:T(8,128)(2,1)S(1)}, bf16[144,128]{1,0:T(8,128)(2,1)S(1)}, u32[]{:S(2)}, u32[]{:S(2)}) collective-permute-start(bf16[144,128]{1,0:T(8,128)(2,1)S(1)} %shard_map.93.refs_4_), channel_id=1, source_target_pairs={{0,1},{1,2},{2,3},{3,0},{4,5},{5,6},{6,7},{7,4},{8,9},{9,10},{10,1... | collective-permute-start | bytes 110600 | tf_op jit(solution)/shard_map/ppermute | solution.py:44
  93.8 4.1 %collective-permute-start.38 = (bf16[144,128]{1,0:T(8,128)(2,1)S(1)}, bf16[144,128]{1,0:T(8,128)(2,1)S(1)}, u32[]{:S(2)}, u32[]{:S(2)}) collective-permute-start(bf16[144,128]{1,0:T(8,128)(2,1)S(1)} %shard_map.93.refs_4_), channel_id=1, source_target_pairs={{0,2},{1,3},{2,0},{3,1},{4,6},{5,7},{6,4},{7,5},{8,10},{9,11},{10,... | collective-permute-start | bytes 110600 | tf_op jit(solution)/shard_map/ppermute | solution.py:44
  96.1 3.8 %collective-permute-start.37 = (bf16[144,128]{1,0:T(8,128)(2,1)S(1)}, bf16[144,128]{1,0:T(8,128)(2,1)S(1)}, u32[]{:S(2)}, u32[]{:S(2)}) collective-permute-start(bf16[144,128]{1,0:T(8,128)(2,1)S(1)} %shard_map.93.refs_4_), channel_id=1, source_target_pairs={{0,3},{1,0},{2,1},{3,2},{4,7},{5,4},{6,5},{7,6},{8,11},{9,8},{10,9... | collective-permute-start | bytes 110600 | tf_op jit(solution)/shard_map/ppermute | solution.py:44
  114.6 4.9 %collective-permute-start.42 = (bf16[128,512]{1,0:T(8,128)(2,1)S(1)}, bf16[128,512]{1,0:T(8,128)(2,1)S(1)}, u32[]{:S(2)}, u32[]{:S(2)}) collective-permute-start(bf16[128,512]{1,0:T(8,128)(2,1)S(1)} %shard_map.95.refs_0_), channel_id=1, source_target_pairs={{0,1},{1,2},{2,3},{3,0},{4,5},{5,6},{6,7},{7,4},{8,9},{9,10},{10,1... | collective-permute-start | bytes 393224 | tf_op jit(solution)/shard_map/ppermute | solution.py:44
  115.1 10.8 %collective-permute-start.41 = (bf16[128,512]{1,0:T(8,128)(2,1)S(1)}, bf16[128,512]{1,0:T(8,128)(2,1)S(1)}, u32[]{:S(2)}, u32[]{:S(2)}) collective-permute-start(bf16[128,512]{1,0:T(8,128)(2,1)S(1)} %shard_map.95.refs_0_), channel_id=1, source_target_pairs={{0,2},{1,3},{2,0},{3,1},{4,6},{5,7},{6,4},{7,5},{8,10},{9,11},{10,... | collective-permute-start | bytes 393224 | tf_op jit(solution)/shard_map/ppermute | solution.py:44
  117.3 12.3 %collective-permute-start.40 = (bf16[128,512]{1,0:T(8,128)(2,1)S(1)}, bf16[128,512]{1,0:T(8,128)(2,1)S(1)}, u32[]{:S(2)}, u32[]{:S(2)}) collective-permute-start(bf16[128,512]{1,0:T(8,128)(2,1)S(1)} %shard_map.95.refs_0_), channel_id=1, source_target_pairs={{0,3},{1,0},{2,1},{3,2},{4,7},{5,4},{6,5},{7,6},{8,11},{9,8},{10,9... | collective-permute-start | bytes 393224 | tf_op jit(solution)/shard_map/ppermute | solution.py:44

commit v5 on v3

--- a/solution.py
+++ b/solution.py
@@ -463,7 +463,7 @@
         arrived = [shifted(term, "seq", -offset - 1) for offset, term in enumerate(terms)]
         ahead = rotated(gq, "head") if split else []
         if step in (2,):
-            arrived = list(lax.optimization_barrier((tuple(arrived), tuple(ahead[1:1+2])))[0])
+            arrived = list(lax.optimization_barrier((tuple(arrived), tuple(ahead[1:1+1])))[0])
         if not split:
             arrived = list(lax.optimization_barrier((tuple(arrived), near[1]))[0])
         msg = local_call(

time: 130 us -> 129 us (level)
  starting transfers between devices: 65.4 us -> 67.8 us
  waiting for transfers between devices: 33.5 us -> 31.6 us
  blocking collectives: 13.8 us -> 12.5 us
    ppermute x16, waiting for transfers between devices: 10.2 us -> 7.48 us  [shifted(): lax.ppermute(value, axis, [(source, source + steps) for source in range(i...]
    ppermute x21, starting transfers between devices: 27.2 us -> 28.9 us  [rotated(): lax.ppermute(value, axis, [(i, (i - step) % count) for i in range(count)])]
where the time goes in v5:
time: 129 us; the launch traced here: 128 us
  starting transfers between devices  67.8 us (53%)
  waiting for transfers between devices  31.6 us (24%)
  Pallas kernels  15.8 us (12%)
  blocking collectives  12.5 us (10%)
    ppermute x16, starting transfers between devices, shifted(): lax.ppermute(value, axis, [(source, source + steps) for source in range(i...  33.4 us
    ppermute x21, starting transfers between devices, rotated(): lax.ppermute(value, axis, [(i, (i - step) % count) for i in range(count)])  28.9 us
    ppermute x21, waiting for transfers between devices, rotated(): lax.ppermute(value, axis, [(i, (i - step) % count) for i in range(count)])  24 us
    all_to_all x1, blocking collectives, shards(): totals = lax.all_to_all(totals, ('seq', 'head'), 0, 0)  12.5 us
    ppermute x16, waiting for transfers between devices, shifted(): lax.ppermute(value, axis, [(source, source + steps) for source in range(i...  7.48 us
    pallas_call x2, Pallas kernels, shards(): local_call(functools.partial(next_body, heads, parts, scale, step == 1),...  3.82 us
    ppermute x3, starting transfers between devices, doubled(): near.append(lax.ppermute(near[0], axis, pairs))  2.72 us
    pallas_call x1, Pallas kernels, shards(): local_call(functools.partial(start_body, heads), [shape_of((rows, wide),...  2.67 us
  transfers between devices with their start and end apart: 43, of which 18 were waited for; matrix products, arithmetic and copies ran while one was open for 0% of the time, Pallas kernels for 7%

profile of v5, /device:TPU:9, one launch (start us, length us, event | category | flops | bytes accessed | tf_op | source)
XLA Modules:
  0.0 128.4 jit_solution(5850297796757844515)
XLA Ops:
  0.0 2.2 %shard_map.82 = (bf16[48,2048]{1,0:T(8,128)(2,1)S(1)}, bf16[128,2048]{1,0:T(8,128)(2,1)S(1)}, bf16[128,128]{1,0:T(8,128)(2,1)S(1)}, f32[128,128]{1,0:T(8,128)S(1)}, f32[128,128]{1,0:T(8,128)S(1)}) custom-call(s32[1]{0:T(128)} %bitcast.2.block_ref, bf16[2048,256]{1,0:T(8,128)(2,1)} %qw_ref.3, bf16[2048,128]{1,0:T(8,128)(2,1)} %kvw_ref.1, ...), custom_call_target="tpu_custom_call" | custom-call | flops 75497472 | bytes 1572864 | tf_op jit(solution)/shard_map/pallas_call | solution.py:382
  2.2 1.4 %collective-permute-start.6 = (bf16[48,2048]{1,0:T(8,128)(2,1)S(1)}, bf16[48,2048]{1,0:T(8,128)(2,1)S(1)}, u32[]{:S(2)}, u32[]{:S(2)}) collective-permute-start(bf16[48,2048]{1,0:T(8,128)(2,1)S(1)} %get-tuple-element.87), channel_id=1, source_target_pairs={{0,1},{1,2},{2,3},{3,0},{4,5},{5,6},{6,7},{7,4},{8,9},{9,10},{10,1... | collective-permute-start | bytes 589832 | tf_op jit(solution)/shard_map/ppermute | solution.py:44
  3.5 1.1 collective-permute-start.5
  4.6 1.4 %collective-permute-start.4 = (bf16[48,2048]{1,0:T(8,128)(2,1)S(1)}, bf16[48,2048]{1,0:T(8,128)(2,1)S(1)}, u32[]{:S(2)}, u32[]{:S(2)}) collective-permute-start(bf16[48,2048]{1,0:T(8,128)(2,1)S(1)} %get-tuple-element.87), channel_id=1, source_target_pairs={{0,3},{1,0},{2,1},{3,2},{4,7},{5,4},{6,5},{7,6},{8,11},{9,8},{10,9... | collective-permute-start | bytes 589832 | tf_op jit(solution)/shard_map/ppermute | solution.py:44
  6.0 4.5 %collective-permute-start.3 = (bf16[128,128]{1,0:T(8,128)(2,1)S(1)}, bf16[128,128]{1,0:T(8,128)(2,1)S(1)}, u32[]{:S(2)}, u32[]{:S(2)}) collective-permute-start(bf16[128,128]{1,0:T(8,128)(2,1)S(1)} %get-tuple-element.71.refs_4_), channel_id=1, source_target_pairs={{0,4},{4,8},{8,12},{12,16},{16,20},{20,24},{24,28},{1,5},{5,9},{9,... | collective-permute-start | bytes 98312 | tf_op jit(solution)/shard_map/ppermute | solution.py:37
  10.5 3.1 %collective-permute-start.2 = (bf16[128,128]{1,0:T(8,128)(2,1)S(1)}, bf16[128,128]{1,0:T(8,128)(2,1)S(1)}, u32[]{:S(2)}, u32[]{:S(2)}) collective-permute-start(bf16[128,128]{1,0:T(8,128)(2,1)S(1)} %get-tuple-element.71.refs_4_), channel_id=1, source_target_pairs={{0,8},{4,12},{8,16},{12,20},{16,24},{20,28},{1,9},{5,13},{9,17},{1... | collective-permute-start | bytes 98312 | tf_op jit(solution)/shard_map/ppermute | solution.py:37
  13.6 3.0 %collective-permute-start.1 = (bf16[128,128]{1,0:T(8,128)(2,1)S(1)}, bf16[128,128]{1,0:T(8,128)(2,1)S(1)}, u32[]{:S(2)}, u32[]{:S(2)}) collective-permute-start(bf16[128,128]{1,0:T(8,128)(2,1)S(1)} %get-tuple-element.71.refs_4_), channel_id=1, source_target_pairs={{0,12},{4,16},{8,20},{12,24},{16,28},{1,13},{5,17},{9,21},{13,25},... | collective-permute-start | bytes 98312 | tf_op jit(solution)/shard_map/ppermute | solution.py:37
  16.7 2.5 %collective-permute-start = (bf16[128,128]{1,0:T(8,128)(2,1)S(1)}, bf16[128,128]{1,0:T(8,128)(2,1)S(1)}, u32[]{:S(2)}, u32[]{:S(2)}) collective-permute-start(bf16[128,128]{1,0:T(8,128)(2,1)S(1)} %get-tuple-element.71.refs_4_), channel_id=1, source_target_pairs={{0,16},{4,20},{8,24},{12,28},{1,17},{5,21},{9,25},{13,29},{2,18},{... | collective-permute-start | bytes 98312 | tf_op jit(solution)/shard_map/ppermute | solution.py:37
  19.2 2.7 %shard_map.83 = (f32[128,256]{1,0:T(8,128)S(1)}, bf16[64,512]{1,0:T(8,128)(2,1)S(1)}, f32[64,512]{1,0:T(8,128)S(1)}, f32[64,512]{1,0:T(8,128)S(1)}, f32[64,512]{...) custom-call(bf16[128,2048]{1,0:T(8,128)(2,1)S(1)} %get-tuple-element.72.hidden_ref, ...), custom_call_target="tpu_custom_call" | custom-call | flops 402653184 | bytes 4194304 | tf_op jit(solution)/shard_map/pallas_call | solution.py:412
  21.9 1.1 shard_map.84
  24.5 2.8 %collective-permute-start.7 = (bf16[128,128]{1,0:T(8,128)(2,1)S(1)}, bf16[128,128]{1,0:T(8,128)(2,1)S(1)}, u32[]{:S(2)}, u32[]{:S(2)}) collective-permute-start(bf16[128,128]{1,0:T(8,128)(2,1)S(1)} %get-tuple-element.90), channel_id=1, source_target_pairs={{4,0},{8,4},{12,8},{16,12},{20,16},{24,20},{28,24},{5,1},{9,5},{13... | collective-permute-start | bytes 98312 | tf_op jit(solution)/shard_map/ppermute | solution.py:37
  27.2 1.3 %collective-permute-start.8 = (bf16[128,128]{1,0:T(8,128)(2,1)S(1)}, bf16[128,128]{1,0:T(8,128)(2,1)S(1)}, u32[]{:S(2)}, u32[]{:S(2)}) collective-permute-start(bf16[128,128]{1,0:T(8,128)(2,1)S(1)} %get-tuple-element.91), channel_id=1, source_target_pairs={{8,0},{12,4},{16,8},{20,12},{24,16},{28,20},{9,1},{13,5},{17,9},{2... | collective-permute-start | bytes 98312 | tf_op jit(solution)/shard_map/ppermute | solution.py:37
  28.5 1.3 %collective-permute-start.9 = (bf16[128,128]{1,0:T(8,128)(2,1)S(1)}, bf16[128,128]{1,0:T(8,128)(2,1)S(1)}, u32[]{:S(2)}, u32[]{:S(2)}) collective-permute-start(bf16[128,128]{1,0:T(8,128)(2,1)S(1)} %get-tuple-element.92), channel_id=1, source_target_pairs={{12,0},{16,4},{20,8},{24,12},{28,16},{13,1},{17,5},{21,9},{25,13},... | collective-permute-start | bytes 98312 | tf_op jit(solution)/shard_map/ppermute | solution.py:37
  29.8 1.3 %collective-permute-start.10 = (bf16[128,128]{1,0:T(8,128)(2,1)S(1)}, bf16[128,128]{1,0:T(8,128)(2,1)S(1)}, u32[]{:S(2)}, u32[]{:S(2)}) collective-permute-start(bf16[128,128]{1,0:T(8,128)(2,1)S(1)} %get-tuple-element.93), channel_id=1, source_target_pairs={{16,0},{20,4},{24,8},{28,12},{17,1},{21,5},{25,9},{29,13},{18,2},{... | collective-permute-start | bytes 98312 | tf_op jit(solution)/shard_map/ppermute | solution.py:37
  32.2 2.9 %collective-permute-done.9.refs_2_ = bf16[128,128]{1,0:T(8,128)(2,1)S(1)} collective-permute-done((bf16[128,128]{1,0:T(8,128)(2,1)S(1)}, bf16[128,128]{1,0:T(8,128)(2,1)S(1)}, u32[]{:S(2)}, u32[]{:S(2)}) %collective-permute-start.9) | collective-permute-done | bytes 32800 | tf_op jit(solution)/shard_map/ppermute | solution.py:37
  36.0 1.8 %collective-permute-start.15 = (bf16[2,4,48,256]{3,2,1,0:T(8,128)(2,1)S(1)}, bf16[2,4,48,256]{3,2,1,0:T(8,128)(2,1)S(1)}, u32[]{:S(2)}, u32[]{:S(2)}) collective-permute-start(bf16[2,4,48,256]{3,2,1,0:T(8,128)(2,1)S(1)} %constant_dynamic-update-slice_fusion), channel_id=1, source_target_pairs={{0,8},{4,12},{8,0},{12,4},{16,24},{20,28},{24,16},{28,20},{1,9},{5... | collective-permute-start | bytes 589832 | tf_op jit(solution)/shard_map/ppermute | solution.py:58
  37.8 1.1 collective-permute-start.12
  39.3 3.1 %collective-permute-start.13 = (bf16[144,384]{1,0:T(8,128)(2,1)S(1)}, bf16[144,384]{1,0:T(8,128)(2,1)S(1)}, u32[]{:S(2)}, u32[]{:S(2)}) collective-permute-start(bf16[144,384]{1,0:T(8,128)(2,1)S(1)} %shard_map.87.refs_0_), channel_id=1, source_target_pairs={{0,2},{1,3},{2,0},{3,1},{4,6},{5,7},{6,4},{7,5},{8,10},{9,11},{10,... | collective-permute-start | bytes 331784 | tf_op jit(solution)/shard_map/ppermute | solution.py:44
  42.5 1.4 %collective-permute-start.16 = (bf16[4,4,48,256]{3,2,1,0:T(8,128)(2,1)S(1)}, bf16[4,4,48,256]{3,2,1,0:T(8,128)(2,1)S(1)}, u32[]{:S(2)}, u32[]{:S(2)}) collective-permute-start(bf16[4,4,48,256]{3,2,1,0:T(8,128)(2,1)S(1)} %constant_dynamic-update-slice_fusion.2.refs_10_), channel_id=1, source_target_pairs={{0,4},{4,0},{8,12},{12,8},{16,20},{20,16},{24,28},{28,24},{1,5},{5... | collective-permute-start | bytes 1179656 | tf_op jit(solution)/shard_map/ppermute | solution.py:57
  43.9 1.6 %collective-permute-done.14.refs_3_ = bf16[144,384]{1,0:T(8,128)(2,1)S(1)} collective-permute-done((bf16[144,384]{1,0:T(8,128)(2,1)S(1)}, bf16[144,384]{1,0:T(8,128)(2,1)S(1)}, u32[]{:S(2)}, u32[]{:S(2)}) %collective-permute-start.14) | collective-permute-done | bytes 110624 | tf_op jit(solution)/shard_map/ppermute | solution.py:44
  45.5 2.9 %collective-permute-done.13.refs_2_ = bf16[144,384]{1,0:T(8,128)(2,1)S(1)} collective-permute-done((bf16[144,384]{1,0:T(8,128)(2,1)S(1)}, bf16[144,384]{1,0:T(8,128)(2,1)S(1)}, u32[]{:S(2)}, u32[]{:S(2)}) %collective-permute-start.13) | collective-permute-done | bytes 110624 | tf_op jit(solution)/shard_map/ppermute | solution.py:44
  49.4 1.9 %shard_map.88 = (bf16[640,512]{1,0:T(8,128)(2,1)S(1)}, f32[128,128]{1,0:T(8,128)S(1)}, bf16[4,128,384]{2,1,0:T(8,128)(2,1)S(1)}, f32[16,128]{1,0:T(8,128)S(1)}, ...) custom-call(s32[2]{0:T(128)S(1)} %pad_add_fusion.spot_ref, ...), custom_call_target="tpu_custom_call" | custom-call | flops 226492416 | bytes 1441792 | tf_op jit(solution)/shard_map/pallas_call | solution.py:495
  51.3 3.3 %collective-permute-start.20 = (bf16[128,128]{1,0:T(8,128)(2,1)S(1)}, bf16[128,128]{1,0:T(8,128)(2,1)S(1)}, u32[]{:S(2)}, u32[]{:S(2)}) collective-permute-start(bf16[128,128]{1,0:T(8,128)(2,1)S(1)} %get-tuple-element.108), channel_id=1, source_target_pairs={{4,0},{8,4},{12,8},{16,12},{20,16},{24,20},{28,24},{5,1},{9,5},{13... | collective-permute-start | bytes 98312 | tf_op jit(solution)/shard_map/ppermute | solution.py:37
  54.6 1.3 %collective-permute-start.21 = (bf16[128,128]{1,0:T(8,128)(2,1)S(1)}, bf16[128,128]{1,0:T(8,128)(2,1)S(1)}, u32[]{:S(2)}, u32[]{:S(2)}) collective-permute-start(bf16[128,128]{1,0:T(8,128)(2,1)S(1)} %get-tuple-element.109), channel_id=1, source_target_pairs={{8,0},{12,4},{16,8},{20,12},{24,16},{28,20},{9,1},{13,5},{17,9},{2... | collective-permute-start | bytes 98312 | tf_op jit(solution)/shard_map/ppermute | solution.py:37
  55.9 1.3 %collective-permute-start.22 = (bf16[128,128]{1,0:T(8,128)(2,1)S(1)}, bf16[128,128]{1,0:T(8,128)(2,1)S(1)}, u32[]{:S(2)}, u32[]{:S(2)}) collective-permute-start(bf16[128,128]{1,0:T(8,128)(2,1)S(1)} %get-tuple-element.110), channel_id=1, source_target_pairs={{12,0},{16,4},{20,8},{24,12},{28,16},{13,1},{17,5},{21,9},{25,13},... | collective-permute-start | bytes 98312 | tf_op jit(solution)/shard_map/ppermute | solution.py:37
  57.2 1.3 %collective-permute-start.23 = (bf16[128,128]{1,0:T(8,128)(2,1)S(1)}, bf16[128,128]{1,0:T(8,128)(2,1)S(1)}, u32[]{:S(2)}, u32[]{:S(2)}) collective-permute-start(bf16[128,128]{1,0:T(8,128)(2,1)S(1)} %get-tuple-element.111), channel_id=1, source_target_pairs={{16,0},{20,4},{24,8},{28,12},{17,1},{21,5},{25,9},{29,13},{18,2},{... | collective-permute-start | bytes 98312 | tf_op jit(solution)/shard_map/ppermute | solution.py:37
  58.8 1.2 collective-permute-done.20.refs_0_
  60.7 3.3 %collective-permute-start.18 = (bf16[128,256]{1,0:T(8,128)(2,1)S(1)}, bf16[128,256]{1,0:T(8,128)(2,1)S(1)}, u32[]{:S(2)}, u32[]{:S(2)}) collective-permute-start(bf16[128,256]{1,0:T(8,128)(2,1)S(1)} %shard_map.89.gq_ref.refs_0_), channel_id=1, source_target_pairs={{0,2},{1,3},{2,0},{3,1},{4,6},{5,7},{6,4},{7,5},{8,10},{9,11},{10,... | collective-permute-start | bytes 196616 | tf_op jit(solution)/shard_map/ppermute | solution.py:44
  65.6 3.2 %collective-permute-start.25 = (bf16[144,128]{1,0:T(8,128)(2,1)S(1)}, bf16[144,128]{1,0:T(8,128)(2,1)S(1)}, u32[]{:S(2)}, u32[]{:S(2)}) collective-permute-start(bf16[144,128]{1,0:T(8,128)(2,1)S(1)} %shard_map.90.refs_4_), channel_id=1, source_target_pairs={{0,2},{1,3},{2,0},{3,1},{4,6},{5,7},{6,4},{7,5},{8,10},{9,11},{10,... | collective-permute-start | bytes 110600 | tf_op jit(solution)/shard_map/ppermute | solution.py:44
  69.7 1.9 %collective-permute-done.25.refs_6_ = bf16[144,128]{1,0:T(8,128)(2,1)S(1)} collective-permute-done((bf16[144,128]{1,0:T(8,128)(2,1)S(1)}, bf16[144,128]{1,0:T(8,128)(2,1)S(1)}, u32[]{:S(2)}, u32[]{:S(2)}) %collective-permute-start.25) | collective-permute-done | bytes 36896 | tf_op jit(solution)/shard_map/ppermute | solution.py:44
  71.7 0.9 collective-permute-done.24.refs_5_
  73.4 1.9 %shard_map.91 = (bf16[640,512]{1,0:T(8,128)(2,1)S(1)}, f32[128,128]{1,0:T(8,128)S(1)}, bf16[4,128,384]{2,1,0:T(8,128)(2,1)S(1)}, f32[16,128]{1,0:T(8,128)S(1)}, ...) custom-call(s32[2]{0:T(128)S(1)} %pad_add_fusion.spot_ref, ...), custom_call_target="tpu_custom_call" | custom-call | flops 226492416 | bytes 1441792 | tf_op jit(solution)/shard_map/pallas_call | solution.py:495
  76.3 2.6 %collective-permute-start.33 = (bf16[128,128]{1,0:T(8,128)(2,1)S(1)}, bf16[128,128]{1,0:T(8,128)(2,1)S(1)}, u32[]{:S(2)}, u32[]{:S(2)}) collective-permute-start(bf16[128,128]{1,0:T(8,128)(2,1)S(1)} %get-tuple-element.121), channel_id=1, source_target_pairs={{4,0},{8,4},{12,8},{16,12},{20,16},{24,20},{28,24},{5,1},{9,5},{13... | collective-permute-start | bytes 98312 | tf_op jit(solution)/shard_map/ppermute | solution.py:37
  78.8 1.3 %collective-permute-start.34 = (bf16[128,128]{1,0:T(8,128)(2,1)S(1)}, bf16[128,128]{1,0:T(8,128)(2,1)S(1)}, u32[]{:S(2)}, u32[]{:S(2)}) collective-permute-start(bf16[128,128]{1,0:T(8,128)(2,1)S(1)} %get-tuple-element.122), channel_id=1, source_target_pairs={{8,0},{12,4},{16,8},{20,12},{24,16},{28,20},{9,1},{13,5},{17,9},{2... | collective-permute-start | bytes 98312 | tf_op jit(solution)/shard_map/ppermute | solution.py:37
  80.1 1.3 %collective-permute-start.35 = (bf16[128,128]{1,0:T(8,128)(2,1)S(1)}, bf16[128,128]{1,0:T(8,128)(2,1)S(1)}, u32[]{:S(2)}, u32[]{:S(2)}) collective-permute-start(bf16[128,128]{1,0:T(8,128)(2,1)S(1)} %get-tuple-element.123), channel_id=1, source_target_pairs={{12,0},{16,4},{20,8},{24,12},{28,16},{13,1},{17,5},{21,9},{25,13},... | collective-permute-start | bytes 98312 | tf_op jit(solution)/shard_map/ppermute | solution.py:37
  81.4 1.3 %collective-permute-start.36 = (bf16[128,128]{1,0:T(8,128)(2,1)S(1)}, bf16[128,128]{1,0:T(8,128)(2,1)S(1)}, u32[]{:S(2)}, u32[]{:S(2)}) collective-permute-start(bf16[128,128]{1,0:T(8,128)(2,1)S(1)} %get-tuple-element.124), channel_id=1, source_target_pairs={{16,0},{20,4},{24,8},{28,12},{17,1},{21,5},{25,9},{29,13},{18,2},{... | collective-permute-start | bytes 98312 | tf_op jit(solution)/shard_map/ppermute | solution.py:37
  83.6 0.9 collective-permute-done.34.refs_1_
  84.6 2.9 %collective-permute-start.31 = (bf16[128,256]{1,0:T(8,128)(2,1)S(1)}, bf16[128,256]{1,0:T(8,128)(2,1)S(1)}, u32[]{:S(2)}, u32[]{:S(2)}) collective-permute-start(bf16[128,256]{1,0:T(8,128)(2,1)S(1)} %shard_map.92.gq_ref.refs_0_), channel_id=1, source_target_pairs={{0,2},{1,3},{2,0},{3,1},{4,6},{5,7},{6,4},{7,5},{8,10},{9,11},{10,... | collective-permute-start | bytes 196616 | tf_op jit(solution)/shard_map/ppermute | solution.py:44
  89.3 3.8 %collective-permute-start.38 = (bf16[144,128]{1,0:T(8,128)(2,1)S(1)}, bf16[144,128]{1,0:T(8,128)(2,1)S(1)}, u32[]{:S(2)}, u32[]{:S(2)}) collective-permute-start(bf16[144,128]{1,0:T(8,128)(2,1)S(1)} %shard_map.93.refs_4_), channel_id=1, source_target_pairs={{0,2},{1,3},{2,0},{3,1},{4,6},{5,7},{6,4},{7,5},{8,10},{9,11},{10,... | collective-permute-start | bytes 110600 | tf_op jit(solution)/shard_map/ppermute | solution.py:44
  93.1 1.7 %collective-permute-done.38.refs_6_ = bf16[144,128]{1,0:T(8,128)(2,1)S(1)} collective-permute-done((bf16[144,128]{1,0:T(8,128)(2,1)S(1)}, bf16[144,128]{1,0:T(8,128)(2,1)S(1)}, u32[]{:S(2)}, u32[]{:S(2)}) %collective-permute-start.38) | collective-permute-done | bytes 36896 | tf_op jit(solution)/shard_map/ppermute | solution.py:44
  94.8 1.8 %collective-permute-done.37.refs_5_ = bf16[144,128]{1,0:T(8,128)(2,1)S(1)} collective-permute-done((bf16[144,128]{1,0:T(8,128)(2,1)S(1)}, bf16[144,128]{1,0:T(8,128)(2,1)S(1)}, u32[]{:S(2)}, u32[]{:S(2)}) %collective-permute-start.37) | collective-permute-done | bytes 36896 | tf_op jit(solution)/shard_map/ppermute | solution.py:44
  96.6 1.9 %shard_map.94 = (f32[3,128,512]{2,1,0:T(8,128)S(1)}, f32[32,8,128]{2,1,0:T(8,128)S(1)}) custom-call(s32[2]{0:T(128)S(1)} %pad_add_fusion.spot_ref, bf16[128,256]{1,0:T(8,128)(2,1)S(1)} %shard_map.92.gq_ref.refs_0_, bf16[128,256]{1,0:T(8,128)(2,1)S(1)} %collective-permute-done.30.refs_1_, bf16[128,256]{1,0:T(8,128)(2,1)S(1)} %collective-permute-done.31.refs_2_, ...), custom_call_target="tpu_custom_call" | custom-call | flops 603979776 | bytes 1572864 | tf_op jit(solution)/shard_map/pallas_call | solution.py:534
  98.5 12.5 %all_to_all.5.tot_ref = f32[32,8,128]{2,1,0:T(8,128)S(1)} all-to-all(f32[32,8,128]{2,1,0:T(8,128)S(1)} %get-tuple-element.135), channel_id=1, replica_groups=mesh['seq'=8,'head'=4] {'seq','head'}, dimensions={0} | all-to-all | bytes 262144 | tf_op jit(solution)/shard_map/all_to_all | solution.py:550
  112.4 2.2 %collective-permute-start.41 = (bf16[128,512]{1,0:T(8,128)(2,1)S(1)}, bf16[128,512]{1,0:T(8,128)(2,1)S(1)}, u32[]{:S(2)}, u32[]{:S(2)}) collective-permute-start(bf16[128,512]{1,0:T(8,128)(2,1)S(1)} %shard_map.95.refs_0_), channel_id=1, source_target_pairs={{0,2},{1,3},{2,0},{3,1},{4,6},{5,7},{6,4},{7,5},{8,10},{9,11},{10,... | collective-permute-start | bytes 393224 | tf_op jit(solution)/shard_map/ppermute | solution.py:44
  114.6 2.2 %collective-permute-done.42.refs_3_ = bf16[128,512]{1,0:T(8,128)(2,1)S(1)} collective-permute-done((bf16[128,512]{1,0:T(8,128)(2,1)S(1)}, bf16[128,512]{1,0:T(8,128)(2,1)S(1)}, u32[]{:S(2)}, u32[]{:S(2)}) %collective-permute-start.42) | collective-permute-done | bytes 131104 | tf_op jit(solution)/shard_map/ppermute | solution.py:44
  116.8 6.4 %collective-permute-done.41.refs_2_ = bf16[128,512]{1,0:T(8,128)(2,1)S(1)} collective-permute-done((bf16[128,512]{1,0:T(8,128)(2,1)S(1)}, bf16[128,512]{1,0:T(8,128)(2,1)S(1)}, u32[]{:S(2)}, u32[]{:S(2)}) %collective-permute-start.41) | collective-permute-done | bytes 131104 | tf_op jit(solution)/shard_map/ppermute | solution.py:44
  123.2 3.7 %collective-permute-done.40.refs_1_ = bf16[128,512]{1,0:T(8,128)(2,1)S(1)} collective-permute-done((bf16[128,512]{1,0:T(8,128)(2,1)S(1)}, bf16[128,512]{1,0:T(8,128)(2,1)S(1)}, u32[]{:S(2)}, u32[]{:S(2)}) %collective-permute-start.40) | collective-permute-done | bytes 131104 | tf_op jit(solution)/shard_map/ppermute | solution.py:44
  126.9 1.6 %shard_map.96 = f32[128,2048]{1,0:T(8,128)} custom-call(s32[2]{0:T(128)S(1)} %pad_add_fusion.spot_ref, bf16[128,512]{1,0:T(8,128)(2,1)S(1)} %shard_map.95.refs_0_, bf16[128,512]{1,0:T(8,128)(2,1)S(1)} %collective-permute-done.40.refs_1_, bf16[128,512]{1,0:T(8,128)(2,1)S(1)} %collective-permute-done.41.refs_2_, ...), custom_call_target="tpu_custom_call" | custom-call | bytes 1572864 | tf_op jit(solution)/shard_map/pallas_call | solution.py:562
  (73 shorter events, 14.2 us)
Async XLA Ops:
  0.0 19.2 %copy-start.2 = (bf16[2048,256]{1,0:T(8,128)(2,1)S(1)}, bf16[2048,256]{1,0:T(8,128)(2,1)}, u32[]{:S(2)}) copy-start(bf16[2048,256]{1,0:T(8,128)(2,1)} %qw_ref.3) | copy-start | bytes 3145732
  2.2 20.9 %collective-permute-start.6 = (bf16[48,2048]{1,0:T(8,128)(2,1)S(1)}, bf16[48,2048]{1,0:T(8,128)(2,1)S(1)}, u32[]{:S(2)}, u32[]{:S(2)}) collective-permute-start(bf16[48,2048]{1,0:T(8,128)(2,1)S(1)} %get-tuple-element.87), channel_id=1, source_target_pairs={{0,1},{1,2},{2,3},{3,0},{4,5},{5,6},{6,7},{7,4},{8,9},{9,10},{10,1... | collective-permute-start | bytes 589832 | tf_op jit(solution)/shard_map/ppermute | solution.py:44
  3.5 19.6 %collective-permute-start.5 = (bf16[48,2048]{1,0:T(8,128)(2,1)S(1)}, bf16[48,2048]{1,0:T(8,128)(2,1)S(1)}, u32[]{:S(2)}, u32[]{:S(2)}) collective-permute-start(bf16[48,2048]{1,0:T(8,128)(2,1)S(1)} %get-tuple-element.87), channel_id=1, source_target_pairs={{0,2},{1,3},{2,0},{3,1},{4,6},{5,7},{6,4},{7,5},{8,10},{9,11},{10,... | collective-permute-start | bytes 589832 | tf_op jit(solution)/shard_map/ppermute | solution.py:44
  4.6 18.5 %collective-permute-start.4 = (bf16[48,2048]{1,0:T(8,128)(2,1)S(1)}, bf16[48,2048]{1,0:T(8,128)(2,1)S(1)}, u32[]{:S(2)}, u32[]{:S(2)}) collective-permute-start(bf16[48,2048]{1,0:T(8,128)(2,1)S(1)} %get-tuple-element.87), channel_id=1, source_target_pairs={{0,3},{1,0},{2,1},{3,2},{4,7},{5,4},{6,5},{7,6},{8,11},{9,8},{10,9... | collective-permute-start | bytes 589832 | tf_op jit(solution)/shard_map/ppermute | solution.py:44
  6.0 7.6 %collective-permute-start.3 = (bf16[128,128]{1,0:T(8,128)(2,1)S(1)}, bf16[128,128]{1,0:T(8,128)(2,1)S(1)}, u32[]{:S(2)}, u32[]{:S(2)}) collective-permute-start(bf16[128,128]{1,0:T(8,128)(2,1)S(1)} %get-tuple-element.71.refs_4_), channel_id=1, source_target_pairs={{0,4},{4,8},{8,12},{12,16},{16,20},{20,24},{24,28},{1,5},{5,9},{9,... | collective-permute-start | bytes 98312 | tf_op jit(solution)/shard_map/ppermute | solution.py:37
  10.5 6.1 %collective-permute-start.2 = (bf16[128,128]{1,0:T(8,128)(2,1)S(1)}, bf16[128,128]{1,0:T(8,128)(2,1)S(1)}, u32[]{:S(2)}, u32[]{:S(2)}) collective-permute-start(bf16[128,128]{1,0:T(8,128)(2,1)S(1)} %get-tuple-element.71.refs_4_), channel_id=1, source_target_pairs={{0,8},{4,12},{8,16},{12,20},{16,24},{20,28},{1,9},{5,13},{9,17},{1... | collective-permute-start | bytes 98312 | tf_op jit(solution)/shard_map/ppermute | solution.py:37
  13.6 8.3 %collective-permute-start.1 = (bf16[128,128]{1,0:T(8,128)(2,1)S(1)}, bf16[128,128]{1,0:T(8,128)(2,1)S(1)}, u32[]{:S(2)}, u32[]{:S(2)}) collective-permute-start(bf16[128,128]{1,0:T(8,128)(2,1)S(1)} %get-tuple-element.71.refs_4_), channel_id=1, source_target_pairs={{0,12},{4,16},{8,20},{12,24},{16,28},{1,13},{5,17},{9,21},{13,25},... | collective-permute-start | bytes 98312 | tf_op jit(solution)/shard_map/ppermute | solution.py:37
  16.7 5.2 %collective-permute-start = (bf16[128,128]{1,0:T(8,128)(2,1)S(1)}, bf16[128,128]{1,0:T(8,128)(2,1)S(1)}, u32[]{:S(2)}, u32[]{:S(2)}) collective-permute-start(bf16[128,128]{1,0:T(8,128)(2,1)S(1)} %get-tuple-element.71.refs_4_), channel_id=1, source_target_pairs={{0,16},{4,20},{8,24},{12,28},{1,17},{5,21},{9,25},{13,29},{2,18},{... | collective-permute-start | bytes 98312 | tf_op jit(solution)/shard_map/ppermute | solution.py:37
  23.7 12.1 %collective-permute-start.11 = (bf16[1,4,48,256]{3,2,1,0:T(8,128)(2,1)S(1)}, bf16[1,4,48,256]{3,2,1,0:T(8,128)(2,1)S(1)}, u32[]{:S(2)}, u32[]{:S(2)}) collective-permute-start(bf16[1,4,48,256]{3,2,1,0:T(8,128)(2,1)S(1)} %bitcast.14), channel_id=1, source_target_pairs={{0,16},{4,20},{8,24},{12,28},{16,0},{20,4},{24,8},{28,12},{1,17},{... | collective-permute-start | bytes 294920 | tf_op jit(solution)/shard_map/ppermute | solution.py:522
  24.5 7.0 %collective-permute-start.7 = (bf16[128,128]{1,0:T(8,128)(2,1)S(1)}, bf16[128,128]{1,0:T(8,128)(2,1)S(1)}, u32[]{:S(2)}, u32[]{:S(2)}) collective-permute-start(bf16[128,128]{1,0:T(8,128)(2,1)S(1)} %get-tuple-element.90), channel_id=1, source_target_pairs={{4,0},{8,4},{12,8},{16,12},{20,16},{24,20},{28,24},{5,1},{9,5},{13... | collective-permute-start | bytes 98312 | tf_op jit(solution)/shard_map/ppermute | solution.py:37
  27.2 5.0 %collective-permute-start.8 = (bf16[128,128]{1,0:T(8,128)(2,1)S(1)}, bf16[128,128]{1,0:T(8,128)(2,1)S(1)}, u32[]{:S(2)}, u32[]{:S(2)}) collective-permute-start(bf16[128,128]{1,0:T(8,128)(2,1)S(1)} %get-tuple-element.91), channel_id=1, source_target_pairs={{8,0},{12,4},{16,8},{20,12},{24,16},{28,20},{9,1},{13,5},{17,9},{2... | collective-permute-start | bytes 98312 | tf_op jit(solution)/shard_map/ppermute | solution.py:37
  28.5 6.6 %collective-permute-start.9 = (bf16[128,128]{1,0:T(8,128)(2,1)S(1)}, bf16[128,128]{1,0:T(8,128)(2,1)S(1)}, u32[]{:S(2)}, u32[]{:S(2)}) collective-permute-start(bf16[128,128]{1,0:T(8,128)(2,1)S(1)} %get-tuple-element.92), channel_id=1, source_target_pairs={{12,0},{16,4},{20,8},{24,12},{28,16},{13,1},{17,5},{21,9},{25,13},... | collective-permute-start | bytes 98312 | tf_op jit(solution)/shard_map/ppermute | solution.py:37
  29.8 6.0 %collective-permute-start.10 = (bf16[128,128]{1,0:T(8,128)(2,1)S(1)}, bf16[128,128]{1,0:T(8,128)(2,1)S(1)}, u32[]{:S(2)}, u32[]{:S(2)}) collective-permute-start(bf16[128,128]{1,0:T(8,128)(2,1)S(1)} %get-tuple-element.93), channel_id=1, source_target_pairs={{16,0},{20,4},{24,8},{28,12},{17,1},{21,5},{25,9},{29,13},{18,2},{... | collective-permute-start | bytes 98312 | tf_op jit(solution)/shard_map/ppermute | solution.py:37
  36.0 6.5 %collective-permute-start.15 = (bf16[2,4,48,256]{3,2,1,0:T(8,128)(2,1)S(1)}, bf16[2,4,48,256]{3,2,1,0:T(8,128)(2,1)S(1)}, u32[]{:S(2)}, u32[]{:S(2)}) collective-permute-start(bf16[2,4,48,256]{3,2,1,0:T(8,128)(2,1)S(1)} %constant_dynamic-update-slice_fusion), channel_id=1, source_target_pairs={{0,8},{4,12},{8,0},{12,4},{16,24},{20,28},{24,16},{28,20},{1,9},{5... | collective-permute-start | bytes 589832 | tf_op jit(solution)/shard_map/ppermute | solution.py:58
  37.8 4.7 %collective-permute-start.12 = (bf16[144,384]{1,0:T(8,128)(2,1)S(1)}, bf16[144,384]{1,0:T(8,128)(2,1)S(1)}, u32[]{:S(2)}, u32[]{:S(2)}) collective-permute-start(bf16[144,384]{1,0:T(8,128)(2,1)S(1)} %shard_map.87.refs_0_), channel_id=1, source_target_pairs={{0,3},{1,0},{2,1},{3,2},{4,7},{5,4},{6,5},{7,6},{8,11},{9,8},{10,9... | collective-permute-start | bytes 331784 | tf_op jit(solution)/shard_map/ppermute | solution.py:44
  38.9 6.5 %collective-permute-start.14 = (bf16[144,384]{1,0:T(8,128)(2,1)S(1)}, bf16[144,384]{1,0:T(8,128)(2,1)S(1)}, u32[]{:S(2)}, u32[]{:S(2)}) collective-permute-start(bf16[144,384]{1,0:T(8,128)(2,1)S(1)} %shard_map.87.refs_0_), channel_id=1, source_target_pairs={{0,1},{1,2},{2,3},{3,0},{4,5},{5,6},{6,7},{7,4},{8,9},{9,10},{10,1... | collective-permute-start | bytes 331784 | tf_op jit(solution)/shard_map/ppermute | solution.py:44
  39.3 9.0 %collective-permute-start.13 = (bf16[144,384]{1,0:T(8,128)(2,1)S(1)}, bf16[144,384]{1,0:T(8,128)(2,1)S(1)}, u32[]{:S(2)}, u32[]{:S(2)}) collective-permute-start(bf16[144,384]{1,0:T(8,128)(2,1)S(1)} %shard_map.87.refs_0_), channel_id=1, source_target_pairs={{0,2},{1,3},{2,0},{3,1},{4,6},{5,7},{6,4},{7,5},{8,10},{9,11},{10,... | collective-permute-start | bytes 331784 | tf_op jit(solution)/shard_map/ppermute | solution.py:44
  42.5 5.8 %collective-permute-start.27 = (bf16[1,4,48,512]{3,2,1,0:T(8,128)(2,1)S(1)}, bf16[1,4,48,512]{3,2,1,0:T(8,128)(2,1)S(1)}, u32[]{:S(2)}, u32[]{:S(2)}) collective-permute-start(bf16[1,4,48,512]{3,2,1,0:T(8,128)(2,1)S(1)} %dynamic-slice_bitcast_fusion), channel_id=1, source_target_pairs={{0,16},{4,20},{8,24},{12,28},{16,0},{20,4},{24,8},{28,12},{1,17},{... | collective-permute-start | bytes 589832 | tf_op jit(solution)/shard_map/ppermute | solution.py:58
  42.5 6.8 %collective-permute-start.16 = (bf16[4,4,48,256]{3,2,1,0:T(8,128)(2,1)S(1)}, bf16[4,4,48,256]{3,2,1,0:T(8,128)(2,1)S(1)}, u32[]{:S(2)}, u32[]{:S(2)}) collective-permute-start(bf16[4,4,48,256]{3,2,1,0:T(8,128)(2,1)S(1)} %constant_dynamic-update-slice_fusion.2.refs_10_), channel_id=1, source_target_pairs={{0,4},{4,0},{8,12},{12,8},{16,20},{20,16},{24,28},{28,24},{1,5},{5... | collective-permute-start | bytes 1179656 | tf_op jit(solution)/shard_map/ppermute | solution.py:57
  48.4 17.2 %collective-permute-start.28 = (bf16[2,4,48,512]{3,2,1,0:T(8,128)(2,1)S(1)}, bf16[2,4,48,512]{3,2,1,0:T(8,128)(2,1)S(1)}, u32[]{:S(2)}, u32[]{:S(2)}) collective-permute-start(bf16[2,4,48,512]{3,2,1,0:T(8,128)(2,1)S(1)} %constant_dynamic-update-slice_fusion.4), channel_id=1, source_target_pairs={{0,8},{4,12},{8,0},{12,4},{16,24},{20,28},{24,16},{28,20},{1,9},{5... | collective-permute-start | bytes 1179656 | tf_op jit(solution)/shard_map/ppermute | solution.py:58
  51.3 8.7 %collective-permute-start.20 = (bf16[128,128]{1,0:T(8,128)(2,1)S(1)}, bf16[128,128]{1,0:T(8,128)(2,1)S(1)}, u32[]{:S(2)}, u32[]{:S(2)}) collective-permute-start(bf16[128,128]{1,0:T(8,128)(2,1)S(1)} %get-tuple-element.108), channel_id=1, source_target_pairs={{4,0},{8,4},{12,8},{16,12},{20,16},{24,20},{28,24},{5,1},{9,5},{13... | collective-permute-start | bytes 98312 | tf_op jit(solution)/shard_map/ppermute | solution.py:37
  54.6 6.1 %collective-permute-start.21 = (bf16[128,128]{1,0:T(8,128)(2,1)S(1)}, bf16[128,128]{1,0:T(8,128)(2,1)S(1)}, u32[]{:S(2)}, u32[]{:S(2)}) collective-permute-start(bf16[128,128]{1,0:T(8,128)(2,1)S(1)} %get-tuple-element.109), channel_id=1, source_target_pairs={{8,0},{12,4},{16,8},{20,12},{24,16},{28,20},{9,1},{13,5},{17,9},{2... | collective-permute-start | bytes 98312 | tf_op jit(solution)/shard_map/ppermute | solution.py:37
  55.9 8.1 %collective-permute-start.22 = (bf16[128,128]{1,0:T(8,128)(2,1)S(1)}, bf16[128,128]{1,0:T(8,128)(2,1)S(1)}, u32[]{:S(2)}, u32[]{:S(2)}) collective-permute-start(bf16[128,128]{1,0:T(8,128)(2,1)S(1)} %get-tuple-element.110), channel_id=1, source_target_pairs={{12,0},{16,4},{20,8},{24,12},{28,16},{13,1},{17,5},{21,9},{25,13},... | collective-permute-start | bytes 98312 | tf_op jit(solution)/shard_map/ppermute | solution.py:37
  57.2 7.5 %collective-permute-start.23 = (bf16[128,128]{1,0:T(8,128)(2,1)S(1)}, bf16[128,128]{1,0:T(8,128)(2,1)S(1)}, u32[]{:S(2)}, u32[]{:S(2)}) collective-permute-start(bf16[128,128]{1,0:T(8,128)(2,1)S(1)} %get-tuple-element.111), channel_id=1, source_target_pairs={{16,0},{20,4},{24,8},{28,12},{17,1},{21,5},{25,9},{29,13},{18,2},{... | collective-permute-start | bytes 98312 | tf_op jit(solution)/shard_map/ppermute | solution.py:37
  60.0 8.9 %collective-permute-start.19 = (bf16[128,256]{1,0:T(8,128)(2,1)S(1)}, bf16[128,256]{1,0:T(8,128)(2,1)S(1)}, u32[]{:S(2)}, u32[]{:S(2)}) collective-permute-start(bf16[128,256]{1,0:T(8,128)(2,1)S(1)} %shard_map.89.gq_ref.refs_0_), channel_id=1, source_target_pairs={{0,1},{1,2},{2,3},{3,0},{4,5},{5,6},{6,7},{7,4},{8,9},{9,10},{10,1... | collective-permute-start | bytes 196616 | tf_op jit(solution)/shard_map/ppermute | solution.py:44
  60.7 8.2 %collective-permute-start.18 = (bf16[128,256]{1,0:T(8,128)(2,1)S(1)}, bf16[128,256]{1,0:T(8,128)(2,1)S(1)}, u32[]{:S(2)}, u32[]{:S(2)}) collective-permute-start(bf16[128,256]{1,0:T(8,128)(2,1)S(1)} %shard_map.89.gq_ref.refs_0_), channel_id=1, source_target_pairs={{0,2},{1,3},{2,0},{3,1},{4,6},{5,7},{6,4},{7,5},{8,10},{9,11},{10,... | collective-permute-start | bytes 196616 | tf_op jit(solution)/shard_map/ppermute | solution.py:44
  64.0 5.2 %collective-permute-start.17 = (bf16[128,256]{1,0:T(8,128)(2,1)S(1)}, bf16[128,256]{1,0:T(8,128)(2,1)S(1)}, u32[]{:S(2)}, u32[]{:S(2)}) collective-permute-start(bf16[128,256]{1,0:T(8,128)(2,1)S(1)} %shard_map.89.gq_ref.refs_0_), channel_id=1, source_target_pairs={{0,3},{1,0},{2,1},{3,2},{4,7},{5,4},{6,5},{7,6},{8,11},{9,8},{10,9... | collective-permute-start | bytes 196616 | tf_op jit(solution)/shard_map/ppermute | solution.py:44
  64.8 4.9 %collective-permute-start.26 = (bf16[144,128]{1,0:T(8,128)(2,1)S(1)}, bf16[144,128]{1,0:T(8,128)(2,1)S(1)}, u32[]{:S(2)}, u32[]{:S(2)}) collective-permute-start(bf16[144,128]{1,0:T(8,128)(2,1)S(1)} %shard_map.90.refs_4_), channel_id=1, source_target_pairs={{0,1},{1,2},{2,3},{3,0},{4,5},{5,6},{6,7},{7,4},{8,9},{9,10},{10,1... | collective-permute-start | bytes 110600 | tf_op jit(solution)/shard_map/ppermute | solution.py:44
  65.6 6.1 %collective-permute-start.25 = (bf16[144,128]{1,0:T(8,128)(2,1)S(1)}, bf16[144,128]{1,0:T(8,128)(2,1)S(1)}, u32[]{:S(2)}, u32[]{:S(2)}) collective-permute-start(bf16[144,128]{1,0:T(8,128)(2,1)S(1)} %shard_map.90.refs_4_), channel_id=1, source_target_pairs={{0,2},{1,3},{2,0},{3,1},{4,6},{5,7},{6,4},{7,5},{8,10},{9,11},{10,... | collective-permute-start | bytes 110600 | tf_op jit(solution)/shard_map/ppermute | solution.py:44
  68.8 3.8 %collective-permute-start.24 = (bf16[144,128]{1,0:T(8,128)(2,1)S(1)}, bf16[144,128]{1,0:T(8,128)(2,1)S(1)}, u32[]{:S(2)}, u32[]{:S(2)}) collective-permute-start(bf16[144,128]{1,0:T(8,128)(2,1)S(1)} %shard_map.90.refs_4_), channel_id=1, source_target_pairs={{0,3},{1,0},{2,1},{3,2},{4,7},{5,4},{6,5},{7,6},{8,11},{9,8},{10,9... | collective-permute-start | bytes 110600 | tf_op jit(solution)/shard_map/ppermute | solution.py:44
  72.7 2.6 %collective-permute-start.29 = (bf16[4,4,48,512]{3,2,1,0:T(8,128)(2,1)S(1)}, bf16[4,4,48,512]{3,2,1,0:T(8,128)(2,1)S(1)}, u32[]{:S(2)}, u32[]{:S(2)}) collective-permute-start(bf16[4,4,48,512]{3,2,1,0:T(8,128)(2,1)S(1)} %constant_dynamic-update-slice_fusion.6.refs_12_), channel_id=1, source_target_pairs={{0,4},{4,0},{8,12},{12,8},{16,20},{20,16},{24,28},{28,24},{1,5},{5... | collective-permute-start | bytes 2359304 | tf_op jit(solution)/shard_map/ppermute | solution.py:57
  75.6 12.8 %collective-permute-start.30 = (bf16[128,256]{1,0:T(8,128)(2,1)S(1)}, bf16[128,256]{1,0:T(8,128)(2,1)S(1)}, u32[]{:S(2)}, u32[]{:S(2)}) collective-permute-start(bf16[128,256]{1,0:T(8,128)(2,1)S(1)} %shard_map.92.gq_ref.refs_0_), channel_id=1, source_target_pairs={{0,3},{1,0},{2,1},{3,2},{4,7},{5,4},{6,5},{7,6},{8,11},{9,8},{10,9... | collective-permute-start | bytes 196616 | tf_op jit(solution)/shard_map/ppermute | solution.py:44
  76.3 6.5 %collective-permute-start.33 = (bf16[128,128]{1,0:T(8,128)(2,1)S(1)}, bf16[128,128]{1,0:T(8,128)(2,1)S(1)}, u32[]{:S(2)}, u32[]{:S(2)}) collective-permute-start(bf16[128,128]{1,0:T(8,128)(2,1)S(1)} %get-tuple-element.121), channel_id=1, source_target_pairs={{4,0},{8,4},{12,8},{16,12},{20,16},{24,20},{28,24},{5,1},{9,5},{13... | collective-permute-start | bytes 98312 | tf_op jit(solution)/shard_map/ppermute | solution.py:37
  78.8 5.7 %collective-permute-start.34 = (bf16[128,128]{1,0:T(8,128)(2,1)S(1)}, bf16[128,128]{1,0:T(8,128)(2,1)S(1)}, u32[]{:S(2)}, u32[]{:S(2)}) collective-permute-start(bf16[128,128]{1,0:T(8,128)(2,1)S(1)} %get-tuple-element.122), channel_id=1, source_target_pairs={{8,0},{12,4},{16,8},{20,12},{24,16},{28,20},{9,1},{13,5},{17,9},{2... | collective-permute-start | bytes 98312 | tf_op jit(solution)/shard_map/ppermute | solution.py:37
  80.1 7.6 %collective-permute-start.35 = (bf16[128,128]{1,0:T(8,128)(2,1)S(1)}, bf16[128,128]{1,0:T(8,128)(2,1)S(1)}, u32[]{:S(2)}, u32[]{:S(2)}) collective-permute-start(bf16[128,128]{1,0:T(8,128)(2,1)S(1)} %get-tuple-element.123), channel_id=1, source_target_pairs={{12,0},{16,4},{20,8},{24,12},{28,16},{13,1},{17,5},{21,9},{25,13},... | collective-permute-start | bytes 98312 | tf_op jit(solution)/shard_map/ppermute | solution.py:37
  81.4 7.0 %collective-permute-start.36 = (bf16[128,128]{1,0:T(8,128)(2,1)S(1)}, bf16[128,128]{1,0:T(8,128)(2,1)S(1)}, u32[]{:S(2)}, u32[]{:S(2)}) collective-permute-start(bf16[128,128]{1,0:T(8,128)(2,1)S(1)} %get-tuple-element.124), channel_id=1, source_target_pairs={{16,0},{20,4},{24,8},{28,12},{17,1},{21,5},{25,9},{29,13},{18,2},{... | collective-permute-start | bytes 98312 | tf_op jit(solution)/shard_map/ppermute | solution.py:37
  82.7 10.3 %collective-permute-start.32 = (bf16[128,256]{1,0:T(8,128)(2,1)S(1)}, bf16[128,256]{1,0:T(8,128)(2,1)S(1)}, u32[]{:S(2)}, u32[]{:S(2)}) collective-permute-start(bf16[128,256]{1,0:T(8,128)(2,1)S(1)} %shard_map.92.gq_ref.refs_0_), channel_id=1, source_target_pairs={{0,1},{1,2},{2,3},{3,0},{4,5},{5,6},{6,7},{7,4},{8,9},{9,10},{10,1... | collective-permute-start | bytes 196616 | tf_op jit(solution)/shard_map/ppermute | solution.py:44
  84.6 8.5 %collective-permute-start.31 = (bf16[128,256]{1,0:T(8,128)(2,1)S(1)}, bf16[128,256]{1,0:T(8,128)(2,1)S(1)}, u32[]{:S(2)}, u32[]{:S(2)}) collective-permute-start(bf16[128,256]{1,0:T(8,128)(2,1)S(1)} %shard_map.92.gq_ref.refs_0_), channel_id=1, source_target_pairs={{0,2},{1,3},{2,0},{3,1},{4,6},{5,7},{6,4},{7,5},{8,10},{9,11},{10,... | collective-permute-start | bytes 196616 | tf_op jit(solution)/shard_map/ppermute | solution.py:44
  88.4 8.2 %copy-start = (bf16[128,2048]{1,0:T(8,128)(2,1)S(1)}, bf16[128,2048]{1,0:T(8,128)(2,1)}, u32[]{:S(2)}) copy-start(bf16[128,2048]{1,0:T(8,128)(2,1)} %refs_14_.1) | copy-start | bytes 1572868
  88.4 8.2 %copy-start.1 = (bf16[128,2048]{1,0:T(8,128)(2,1)S(1)}, bf16[128,2048]{1,0:T(8,128)(2,1)}, u32[]{:S(2)}) copy-start(bf16[128,2048]{1,0:T(8,128)(2,1)} %up_ref.3) | copy-start | bytes 1572868
  88.4 8.2 %copy-start.3 = (f32[2048]{0:T(1024)S(1)}, f32[2048]{0:T(1024)}, u32[]{:S(2)}) copy-start(f32[2048]{0:T(1024)} %param.10) | copy-start | bytes 24580
  88.6 4.5 %collective-permute-start.39 = (bf16[144,128]{1,0:T(8,128)(2,1)S(1)}, bf16[144,128]{1,0:T(8,128)(2,1)S(1)}, u32[]{:S(2)}, u32[]{:S(2)}) collective-permute-start(bf16[144,128]{1,0:T(8,128)(2,1)S(1)} %shard_map.93.refs_4_), channel_id=1, source_target_pairs={{0,1},{1,2},{2,3},{3,0},{4,5},{5,6},{6,7},{7,4},{8,9},{9,10},{10,1... | collective-permute-start | bytes 110600 | tf_op jit(solution)/shard_map/ppermute | solution.py:44
  89.3 5.5 %collective-permute-start.38 = (bf16[144,128]{1,0:T(8,128)(2,1)S(1)}, bf16[144,128]{1,0:T(8,128)(2,1)S(1)}, u32[]{:S(2)}, u32[]{:S(2)}) collective-permute-start(bf16[144,128]{1,0:T(8,128)(2,1)S(1)} %shard_map.93.refs_4_), channel_id=1, source_target_pairs={{0,2},{1,3},{2,0},{3,1},{4,6},{5,7},{6,4},{7,5},{8,10},{9,11},{10,... | collective-permute-start | bytes 110600 | tf_op jit(solution)/shard_map/ppermute | solution.py:44
  93.1 3.6 %collective-permute-start.37 = (bf16[144,128]{1,0:T(8,128)(2,1)S(1)}, bf16[144,128]{1,0:T(8,128)(2,1)S(1)}, u32[]{:S(2)}, u32[]{:S(2)}) collective-permute-start(bf16[144,128]{1,0:T(8,128)(2,1)S(1)} %shard_map.93.refs_4_), channel_id=1, source_target_pairs={{0,3},{1,0},{2,1},{3,2},{4,7},{5,4},{6,5},{7,6},{8,11},{9,8},{10,9... | collective-permute-start | bytes 110600 | tf_op jit(solution)/shard_map/ppermute | solution.py:44
  111.9 4.9 %collective-permute-start.42 = (bf16[128,512]{1,0:T(8,128)(2,1)S(1)}, bf16[128,512]{1,0:T(8,128)(2,1)S(1)}, u32[]{:S(2)}, u32[]{:S(2)}) collective-permute-start(bf16[128,512]{1,0:T(8,128)(2,1)S(1)} %shard_map.95.refs_0_), channel_id=1, source_target_pairs={{0,1},{1,2},{2,3},{3,0},{4,5},{5,6},{6,7},{7,4},{8,9},{9,10},{10,1... | collective-permute-start | bytes 393224 | tf_op jit(solution)/shard_map/ppermute | solution.py:44
  112.4 10.8 %collective-permute-start.41 = (bf16[128,512]{1,0:T(8,128)(2,1)S(1)}, bf16[128,512]{1,0:T(8,128)(2,1)S(1)}, u32[]{:S(2)}, u32[]{:S(2)}) collective-permute-start(bf16[128,512]{1,0:T(8,128)(2,1)S(1)} %shard_map.95.refs_0_), channel_id=1, source_target_pairs={{0,2},{1,3},{2,0},{3,1},{4,6},{5,7},{6,4},{7,5},{8,10},{9,11},{10,... | collective-permute-start | bytes 393224 | tf_op jit(solution)/shard_map/ppermute | solution.py:44
  114.6 12.3 %collective-permute-start.40 = (bf16[128,512]{1,0:T(8,128)(2,1)S(1)}, bf16[128,512]{1,0:T(8,128)(2,1)S(1)}, u32[]{:S(2)}, u32[]{:S(2)}) collective-permute-start(bf16[128,512]{1,0:T(8,128)(2,1)S(1)} %shard_map.95.refs_0_), channel_id=1, source_target_pairs={{0,3},{1,0},{2,1},{3,2},{4,7},{5,4},{6,5},{7,6},{8,11},{9,8},{10,9... | collective-permute-start | bytes 393224 | tf_op jit(solution)/shard_map/ppermute | solution.py:44
